TPU v7x, 128 devices: a whole 4x4x4 slice. The times are simulated.
128 devices in a mesh: blk: 16 (over z, y_lo, core), dp: 8 (over y_hi, x).
Axes of the slice: x: 4, y: 4 (y_hi: 2, y_lo: 2; y = y_hi * 2 + y_lo), z: 4, core: 2. Of those that a mesh axis runs over, the one named last changes fastest.
Arguments:
- pooled_image_rows: bfloat16 [8, 6144, 1152], P('dp', 'blk'), may hold values from -6 to 6
- text_embed_rows: bfloat16 [8, 6144, 1152], P('dp', 'blk'), may hold values from -6 to 6
- projection_matrix: bfloat16 [1152, 1152], replicated, may hold values from -0.1875 to 0.1875
- lowrank_down_weight: bfloat16 [1152, 64], replicated, may hold values from -0.1875 to 0.1875
- lowrank_up_weight: bfloat16 [64, 1152], replicated, may hold values from -0.75 to 0.75
- similarity_scale: float32 [1], replicated, may hold values from 2 to 5
- similarity_bias: float32 [1], replicated, may hold values from -6 to -2
Outputs:
- text_grad: float32 [8, 6144, 1152], P('dp', 'blk')
- grad_down: float32 [1152, 64], replicated
- grad_up: float32 [64, 1152], replicated
All inputs are finite; a program needn't handle non-finite values.
Results may differ from a plain program's by a relative error of at most 0.0015.
Values may be sent and summed in bfloat16 or wider, within the bound.
No kernel may reach another device: no remote copies, remote signals or barrier semaphores. Data moves between devices by JAX's collectives and lax.ppermute only.
A program may use at most 128 MiB of HBM per device.

v0:
```python
import math

import jax
import jax.numpy as jnp
from jax import lax
from jax.sharding import PartitionSpec as P


def from_behind(block, axis, distance):
    devices = range(lax.axis_size(axis))
    route = [((i - distance) % len(devices), i) for i in devices]
    return lax.ppermute(block, axis, route)


def shards(
    pooled_image_rows,
    text_embed_rows,
    projection_matrix,
    lowrank_down_weight,
    lowrank_up_weight,
    similarity_scale,
    similarity_bias,
):
    feature_rows = pooled_image_rows[0]
    texts = text_embed_rows[0]
    rows_here = feature_rows.shape[0]
    width = texts.shape[1]
    factor = similarity_scale[0] / math.sqrt(width)
    bias = similarity_bias[0]
    hidden_rows = jnp.dot(
        feature_rows, lowrank_down_weight, preferred_element_type=jnp.float32
    ).astype(jnp.bfloat16)
    embed_vectors = (
        jnp.dot(feature_rows, projection_matrix, preferred_element_type=jnp.float32)
        + jnp.dot(hidden_rows, lowrank_up_weight, preferred_element_type=jnp.float32)
    ).astype(jnp.bfloat16)

    def pair_logits(images, group):
        sims = lax.dot_general(
            images, group, (((1,), (1,)), ((), ())), preferred_element_type=jnp.float32
        )
        return factor * sims + bias

    def logit_block(group):
        return pair_logits(embed_vectors, group)

    def column_terms(weights, images):
        return lax.dot_general(
            weights, images, (((0,), (0,)), ((), ())), preferred_element_type=jnp.float32
        )

    def text_terms(weights):
        return column_terms(weights, embed_vectors)

    logits = logit_block(texts)
    same = jnp.eye(rows_here, dtype=bool)
    coef = jnp.where(same, -jax.nn.sigmoid(-logits), jax.nn.sigmoid(logits))
    weights = (coef * factor).astype(jnp.bfloat16)
    image_acc = jnp.dot(weights, texts, preferred_element_type=jnp.float32)
    carried = text_terms(weights)

    def turn(step, state):
        group, travel, image_sum = state
        group = from_behind(group, "blk", 1)
        travel = from_behind(travel, "blk", 1)
        block_weights = (jax.nn.sigmoid(logit_block(group)) * factor).astype(jnp.bfloat16)
        image_sum = image_sum + jnp.dot(block_weights, group, preferred_element_type=jnp.float32)
        return (group, travel + text_terms(block_weights), image_sum)

    texts_end, carried, image_acc = lax.fori_loop(
        1, lax.axis_size("blk"), turn, (texts, carried, image_acc)
    )
    text_grad = from_behind(carried, "blk", 1)
    image_gradient = image_acc.astype(jnp.bfloat16)
    inner_product = jnp.dot(
        image_gradient, lowrank_up_weight.T, preferred_element_type=jnp.float32
    ).astype(jnp.bfloat16)
    part_up = lax.dot_general(
        hidden_rows, image_gradient, (((0,), (0,)), ((), ())), preferred_element_type=jnp.float32
    )
    part_down = lax.dot_general(
        feature_rows, inner_product, (((0,), (0,)), ((), ())), preferred_element_type=jnp.float32
    )
    total_down, total_up = lax.psum((part_down, part_up), ("blk", "dp"))
    pair_count = rows_here * lax.axis_size("blk")
    return (text_grad[None], total_down / pair_count, total_up / pair_count)


def solution(mesh):
    placed = (P("dp", "blk", None), P("dp", "blk", None), P(), P(), P(), P(), P())
    return jax.shard_map(
        shards,
        mesh=mesh,
        in_specs=placed,
        out_specs=(P("dp", "blk", None), P(), P()),
        check_vma=False,
    )
```

profile of v0, /device:TPU:1, one launch (start us, length us, event | category | flops | bytes accessed | tf_op | source)
XLA Modules:
  0.0 800.9 jit_solution(3493887538853080204)
XLA Ops:
  16.7 589.8 %while.14 = (s32[]{:T(128)}, bf16[384,1152]{1,0:T(8,128)(2,1)S(1)}, f32[384,1152]{1,0:T(8,128)}, f32[384,1152]{1,0:T(8,128)}, f32[]{:T(128)}, /*index=5*/bf16[384,1152]{1,0:T(8,128)(2,1)}, f32[]{:T(128)}, s32[]{:T(128)}) while((s32[]{:T(128)}, bf16[384,1152]{1,0:T(8,128)(2,1)S(1)}, f32[384,1152]{1,0:T(8,128)}, f32[384,1152]{1,0:T(8,128)}, ...), condition=%wide.region_1.2_spmd, body=%wide.region_0.1_spmd.sunk | while | flops 1021132800 | bytes 48660792 | solution.py:70
  20.4 28.3 %collective-permute-done = bf16[384,1152]{1,0:T(8,128)(2,1)S(1)} collective-permute-done((bf16[384,1152]{1,0:T(8,128)(2,1)}, bf16[384,1152]{1,0:T(8,128)(2,1)S(1)}, u32[]{:S(2)}, u32[]{:S(2)}) %collective-permute-start) | collective-permute-done | bytes 884768 | tf_op jit(solution)/shard_map/while/body/eval_jaxpr/ppermute | solution.py:12
  59.3 28.4 %collective-permute-done = bf16[384,1152]{1,0:T(8,128)(2,1)S(1)} collective-permute-done((bf16[384,1152]{1,0:T(8,128)(2,1)}, bf16[384,1152]{1,0:T(8,128)(2,1)S(1)}, u32[]{:S(2)}, u32[]{:S(2)}) %collective-permute-start) | collective-permute-done | bytes 884768 | tf_op jit(solution)/shard_map/while/body/eval_jaxpr/ppermute | solution.py:12
  98.3 28.4 %collective-permute-done = bf16[384,1152]{1,0:T(8,128)(2,1)S(1)} collective-permute-done((bf16[384,1152]{1,0:T(8,128)(2,1)}, bf16[384,1152]{1,0:T(8,128)(2,1)S(1)}, u32[]{:S(2)}, u32[]{:S(2)}) %collective-permute-start) | collective-permute-done | bytes 884768 | tf_op jit(solution)/shard_map/while/body/eval_jaxpr/ppermute | solution.py:12
  137.8 27.9 %collective-permute-done = bf16[384,1152]{1,0:T(8,128)(2,1)S(1)} collective-permute-done((bf16[384,1152]{1,0:T(8,128)(2,1)}, bf16[384,1152]{1,0:T(8,128)(2,1)S(1)}, u32[]{:S(2)}, u32[]{:S(2)}) %collective-permute-start) | collective-permute-done | bytes 884768 | tf_op jit(solution)/shard_map/while/body/eval_jaxpr/ppermute | solution.py:12
  177.7 27.0 %collective-permute-done = bf16[384,1152]{1,0:T(8,128)(2,1)S(1)} collective-permute-done((bf16[384,1152]{1,0:T(8,128)(2,1)}, bf16[384,1152]{1,0:T(8,128)(2,1)S(1)}, u32[]{:S(2)}, u32[]{:S(2)}) %collective-permute-start) | collective-permute-done | bytes 884768 | tf_op jit(solution)/shard_map/while/body/eval_jaxpr/ppermute | solution.py:12
  217.6 26.1 %collective-permute-done = bf16[384,1152]{1,0:T(8,128)(2,1)S(1)} collective-permute-done((bf16[384,1152]{1,0:T(8,128)(2,1)}, bf16[384,1152]{1,0:T(8,128)(2,1)S(1)}, u32[]{:S(2)}, u32[]{:S(2)}) %collective-permute-start) | collective-permute-done | bytes 884768 | tf_op jit(solution)/shard_map/while/body/eval_jaxpr/ppermute | solution.py:12
  257.5 25.2 %collective-permute-done = bf16[384,1152]{1,0:T(8,128)(2,1)S(1)} collective-permute-done((bf16[384,1152]{1,0:T(8,128)(2,1)}, bf16[384,1152]{1,0:T(8,128)(2,1)S(1)}, u32[]{:S(2)}, u32[]{:S(2)}) %collective-permute-start) | collective-permute-done | bytes 884768 | tf_op jit(solution)/shard_map/while/body/eval_jaxpr/ppermute | solution.py:12
  297.5 24.3 %collective-permute-done = bf16[384,1152]{1,0:T(8,128)(2,1)S(1)} collective-permute-done((bf16[384,1152]{1,0:T(8,128)(2,1)}, bf16[384,1152]{1,0:T(8,128)(2,1)S(1)}, u32[]{:S(2)}, u32[]{:S(2)}) %collective-permute-start) | collective-permute-done | bytes 884768 | tf_op jit(solution)/shard_map/while/body/eval_jaxpr/ppermute | solution.py:12
  331.5 5.8 collective-permute-start
  337.4 23.4 %collective-permute-done = bf16[384,1152]{1,0:T(8,128)(2,1)S(1)} collective-permute-done((bf16[384,1152]{1,0:T(8,128)(2,1)}, bf16[384,1152]{1,0:T(8,128)(2,1)S(1)}, u32[]{:S(2)}, u32[]{:S(2)}) %collective-permute-start) | collective-permute-done | bytes 884768 | tf_op jit(solution)/shard_map/while/body/eval_jaxpr/ppermute | solution.py:12
  370.6 6.7 collective-permute-start
  377.3 22.5 %collective-permute-done = bf16[384,1152]{1,0:T(8,128)(2,1)S(1)} collective-permute-done((bf16[384,1152]{1,0:T(8,128)(2,1)}, bf16[384,1152]{1,0:T(8,128)(2,1)S(1)}, u32[]{:S(2)}, u32[]{:S(2)}) %collective-permute-start) | collective-permute-done | bytes 884768 | tf_op jit(solution)/shard_map/while/body/eval_jaxpr/ppermute | solution.py:12
  409.6 7.6 collective-permute-start
  417.2 21.6 %collective-permute-done = bf16[384,1152]{1,0:T(8,128)(2,1)S(1)} collective-permute-done((bf16[384,1152]{1,0:T(8,128)(2,1)}, bf16[384,1152]{1,0:T(8,128)(2,1)S(1)}, u32[]{:S(2)}, u32[]{:S(2)}) %collective-permute-start) | collective-permute-done | bytes 884768 | tf_op jit(solution)/shard_map/while/body/eval_jaxpr/ppermute | solution.py:12
  448.6 8.5 %collective-permute-start = (bf16[384,1152]{1,0:T(8,128)(2,1)}, bf16[384,1152]{1,0:T(8,128)(2,1)S(1)}, u32[]{:S(2)}, u32[]{:S(2)}) collective-permute-start(bf16[384,1152]{1,0:T(8,128)(2,1)} %copy-done.5), channel_id=1, source_target_pairs={{120,0},{0,8},{8,16},{16,24},{24,32},{32,40},{40,48},{48,56},{56,6... | collective-permute-start | bytes 2654216 | tf_op jit(solution)/shard_map/while/body/eval_jaxpr/ppermute | solution.py:12
  457.1 20.7 %collective-permute-done = bf16[384,1152]{1,0:T(8,128)(2,1)S(1)} collective-permute-done((bf16[384,1152]{1,0:T(8,128)(2,1)}, bf16[384,1152]{1,0:T(8,128)(2,1)S(1)}, u32[]{:S(2)}, u32[]{:S(2)}) %collective-permute-start) | collective-permute-done | bytes 884768 | tf_op jit(solution)/shard_map/while/body/eval_jaxpr/ppermute | solution.py:12
  487.6 9.4 %collective-permute-start = (bf16[384,1152]{1,0:T(8,128)(2,1)}, bf16[384,1152]{1,0:T(8,128)(2,1)S(1)}, u32[]{:S(2)}, u32[]{:S(2)}) collective-permute-start(bf16[384,1152]{1,0:T(8,128)(2,1)} %copy-done.5), channel_id=1, source_target_pairs={{120,0},{0,8},{8,16},{16,24},{24,32},{32,40},{40,48},{48,56},{56,6... | collective-permute-start | bytes 2654216 | tf_op jit(solution)/shard_map/while/body/eval_jaxpr/ppermute | solution.py:12
  497.0 20.0 %collective-permute-done = bf16[384,1152]{1,0:T(8,128)(2,1)S(1)} collective-permute-done((bf16[384,1152]{1,0:T(8,128)(2,1)}, bf16[384,1152]{1,0:T(8,128)(2,1)S(1)}, u32[]{:S(2)}, u32[]{:S(2)}) %collective-permute-start) | collective-permute-done | bytes 884768 | tf_op jit(solution)/shard_map/while/body/eval_jaxpr/ppermute | solution.py:12
  526.6 10.3 %collective-permute-start = (bf16[384,1152]{1,0:T(8,128)(2,1)}, bf16[384,1152]{1,0:T(8,128)(2,1)S(1)}, u32[]{:S(2)}, u32[]{:S(2)}) collective-permute-start(bf16[384,1152]{1,0:T(8,128)(2,1)} %copy-done.5), channel_id=1, source_target_pairs={{120,0},{0,8},{8,16},{16,24},{24,32},{32,40},{40,48},{48,56},{56,6... | collective-permute-start | bytes 2654216 | tf_op jit(solution)/shard_map/while/body/eval_jaxpr/ppermute | solution.py:12
  536.9 21.2 %collective-permute-done = bf16[384,1152]{1,0:T(8,128)(2,1)S(1)} collective-permute-done((bf16[384,1152]{1,0:T(8,128)(2,1)}, bf16[384,1152]{1,0:T(8,128)(2,1)S(1)}, u32[]{:S(2)}, u32[]{:S(2)}) %collective-permute-start) | collective-permute-done | bytes 884768 | tf_op jit(solution)/shard_map/while/body/eval_jaxpr/ppermute | solution.py:12
  566.3 10.5 %collective-permute-start = (bf16[384,1152]{1,0:T(8,128)(2,1)}, bf16[384,1152]{1,0:T(8,128)(2,1)S(1)}, u32[]{:S(2)}, u32[]{:S(2)}) collective-permute-start(bf16[384,1152]{1,0:T(8,128)(2,1)} %copy-done.5), channel_id=1, source_target_pairs={{120,0},{0,8},{8,16},{16,24},{24,32},{32,40},{40,48},{48,56},{56,6... | collective-permute-start | bytes 2654216 | tf_op jit(solution)/shard_map/while/body/eval_jaxpr/ppermute | solution.py:12
  576.8 22.4 %collective-permute-done = bf16[384,1152]{1,0:T(8,128)(2,1)S(1)} collective-permute-done((bf16[384,1152]{1,0:T(8,128)(2,1)}, bf16[384,1152]{1,0:T(8,128)(2,1)S(1)}, u32[]{:S(2)}, u32[]{:S(2)}) %collective-permute-start) | collective-permute-done | bytes 884768 | tf_op jit(solution)/shard_map/while/body/eval_jaxpr/ppermute | solution.py:12
  612.2 175.6 %all-reduce.3.cloned.1.call-done = (f32[1152,64]{0,1:T(8,128)}, f32[64,1152]{1,0:T(8,128)}) async-done(((f32[1152,64]{0,1:T(8,128)}, f32[64,1152]{1,0:T(8,128)}), (f32[1152,64]{0,1:T(8,128)}, f32[64,1152]{1,0:T(8,128)})) %all-reduce.3.cloned.1.call-update) | async-done | bytes 589840 | tf_op jit(solution)/shard_map/psum | solution.py:84
  (278 shorter events, 182.5 us)
Async XLA Ops:
  7.2 780.6 %all-reduce.3.cloned.1.call-start = ((), (), s32[]{:S(2)}) async-start(), calls=%async_computation | async-start | bytes 1179648 | tf_op jit(solution)/shard_map/psum | solution.py:84
  16.7 35.2 %collective-permute-start.1 = (f32[384,1152]{1,0:T(8,128)}, f32[384,1152]{1,0:T(8,128)}, u32[]{:S(2)}, u32[]{:S(2)}) collective-permute-start(f32[384,1152]{1,0:T(8,128)} %get-tuple-element.112), channel_id=1, source_target_pairs={{120,0},{0,8},{8,16},{16,24},{24,32},{32,40},{40,48},{48,56},{56,6... | collective-permute-start | bytes 5308424 | tf_op jit(solution)/shard_map/while/body/eval_jaxpr/ppermute | solution.py:12
  19.4 29.3 %collective-permute-start = (bf16[384,1152]{1,0:T(8,128)(2,1)}, bf16[384,1152]{1,0:T(8,128)(2,1)S(1)}, u32[]{:S(2)}, u32[]{:S(2)}) collective-permute-start(bf16[384,1152]{1,0:T(8,128)(2,1)} %copy-done.5), channel_id=1, source_target_pairs={{120,0},{0,8},{8,16},{16,24},{24,32},{32,40},{40,48},{48,56},{56,6... | collective-permute-start | bytes 2654216 | tf_op jit(solution)/shard_map/while/body/eval_jaxpr/ppermute | solution.py:12
  56.0 35.0 %collective-permute-start.1 = (f32[384,1152]{1,0:T(8,128)}, f32[384,1152]{1,0:T(8,128)}, u32[]{:S(2)}, u32[]{:S(2)}) collective-permute-start(f32[384,1152]{1,0:T(8,128)} %get-tuple-element.112), channel_id=1, source_target_pairs={{120,0},{0,8},{8,16},{16,24},{24,32},{32,40},{40,48},{48,56},{56,6... | collective-permute-start | bytes 5308424 | tf_op jit(solution)/shard_map/while/body/eval_jaxpr/ppermute | solution.py:12
  95.0 35.0 %collective-permute-start.1 = (f32[384,1152]{1,0:T(8,128)}, f32[384,1152]{1,0:T(8,128)}, u32[]{:S(2)}, u32[]{:S(2)}) collective-permute-start(f32[384,1152]{1,0:T(8,128)} %get-tuple-element.112), channel_id=1, source_target_pairs={{120,0},{0,8},{8,16},{16,24},{24,32},{32,40},{40,48},{48,56},{56,6... | collective-permute-start | bytes 5308424 | tf_op jit(solution)/shard_map/while/body/eval_jaxpr/ppermute | solution.py:12
  134.0 35.0 %collective-permute-start.1 = (f32[384,1152]{1,0:T(8,128)}, f32[384,1152]{1,0:T(8,128)}, u32[]{:S(2)}, u32[]{:S(2)}) collective-permute-start(f32[384,1152]{1,0:T(8,128)} %get-tuple-element.112), channel_id=1, source_target_pairs={{120,0},{0,8},{8,16},{16,24},{24,32},{32,40},{40,48},{48,56},{56,6... | collective-permute-start | bytes 5308424 | tf_op jit(solution)/shard_map/while/body/eval_jaxpr/ppermute | solution.py:12
  173.0 35.0 %collective-permute-start.1 = (f32[384,1152]{1,0:T(8,128)}, f32[384,1152]{1,0:T(8,128)}, u32[]{:S(2)}, u32[]{:S(2)}) collective-permute-start(f32[384,1152]{1,0:T(8,128)} %get-tuple-element.112), channel_id=1, source_target_pairs={{120,0},{0,8},{8,16},{16,24},{24,32},{32,40},{40,48},{48,56},{56,6... | collective-permute-start | bytes 5308424 | tf_op jit(solution)/shard_map/while/body/eval_jaxpr/ppermute | solution.py:12
  175.5 29.3 %collective-permute-start = (bf16[384,1152]{1,0:T(8,128)(2,1)}, bf16[384,1152]{1,0:T(8,128)(2,1)S(1)}, u32[]{:S(2)}, u32[]{:S(2)}) collective-permute-start(bf16[384,1152]{1,0:T(8,128)(2,1)} %copy-done.5), channel_id=1, source_target_pairs={{120,0},{0,8},{8,16},{16,24},{24,32},{32,40},{40,48},{48,56},{56,6... | collective-permute-start | bytes 2654216 | tf_op jit(solution)/shard_map/while/body/eval_jaxpr/ppermute | solution.py:12
  212.0 35.0 %collective-permute-start.1 = (f32[384,1152]{1,0:T(8,128)}, f32[384,1152]{1,0:T(8,128)}, u32[]{:S(2)}, u32[]{:S(2)}) collective-permute-start(f32[384,1152]{1,0:T(8,128)} %get-tuple-element.112), channel_id=1, source_target_pairs={{120,0},{0,8},{8,16},{16,24},{24,32},{32,40},{40,48},{48,56},{56,6... | collective-permute-start | bytes 5308424 | tf_op jit(solution)/shard_map/while/body/eval_jaxpr/ppermute | solution.py:12
  214.5 29.3 %collective-permute-start = (bf16[384,1152]{1,0:T(8,128)(2,1)}, bf16[384,1152]{1,0:T(8,128)(2,1)S(1)}, u32[]{:S(2)}, u32[]{:S(2)}) collective-permute-start(bf16[384,1152]{1,0:T(8,128)(2,1)} %copy-done.5), channel_id=1, source_target_pairs={{120,0},{0,8},{8,16},{16,24},{24,32},{32,40},{40,48},{48,56},{56,6... | collective-permute-start | bytes 2654216 | tf_op jit(solution)/shard_map/while/body/eval_jaxpr/ppermute | solution.py:12
  251.1 35.0 %collective-permute-start.1 = (f32[384,1152]{1,0:T(8,128)}, f32[384,1152]{1,0:T(8,128)}, u32[]{:S(2)}, u32[]{:S(2)}) collective-permute-start(f32[384,1152]{1,0:T(8,128)} %get-tuple-element.112), channel_id=1, source_target_pairs={{120,0},{0,8},{8,16},{16,24},{24,32},{32,40},{40,48},{48,56},{56,6... | collective-permute-start | bytes 5308424 | tf_op jit(solution)/shard_map/while/body/eval_jaxpr/ppermute | solution.py:12
  253.5 29.3 %collective-permute-start = (bf16[384,1152]{1,0:T(8,128)(2,1)}, bf16[384,1152]{1,0:T(8,128)(2,1)S(1)}, u32[]{:S(2)}, u32[]{:S(2)}) collective-permute-start(bf16[384,1152]{1,0:T(8,128)(2,1)} %copy-done.5), channel_id=1, source_target_pairs={{120,0},{0,8},{8,16},{16,24},{24,32},{32,40},{40,48},{48,56},{56,6... | collective-permute-start | bytes 2654216 | tf_op jit(solution)/shard_map/while/body/eval_jaxpr/ppermute | solution.py:12
  290.1 35.0 %collective-permute-start.1 = (f32[384,1152]{1,0:T(8,128)}, f32[384,1152]{1,0:T(8,128)}, u32[]{:S(2)}, u32[]{:S(2)}) collective-permute-start(f32[384,1152]{1,0:T(8,128)} %get-tuple-element.112), channel_id=1, source_target_pairs={{120,0},{0,8},{8,16},{16,24},{24,32},{32,40},{40,48},{48,56},{56,6... | collective-permute-start | bytes 5308424 | tf_op jit(solution)/shard_map/while/body/eval_jaxpr/ppermute | solution.py:12
  329.1 35.0 %collective-permute-start.1 = (f32[384,1152]{1,0:T(8,128)}, f32[384,1152]{1,0:T(8,128)}, u32[]{:S(2)}, u32[]{:S(2)}) collective-permute-start(f32[384,1152]{1,0:T(8,128)} %get-tuple-element.112), channel_id=1, source_target_pairs={{120,0},{0,8},{8,16},{16,24},{24,32},{32,40},{40,48},{48,56},{56,6... | collective-permute-start | bytes 5308424 | tf_op jit(solution)/shard_map/while/body/eval_jaxpr/ppermute | solution.py:12
  368.1 35.0 %collective-permute-start.1 = (f32[384,1152]{1,0:T(8,128)}, f32[384,1152]{1,0:T(8,128)}, u32[]{:S(2)}, u32[]{:S(2)}) collective-permute-start(f32[384,1152]{1,0:T(8,128)} %get-tuple-element.112), channel_id=1, source_target_pairs={{120,0},{0,8},{8,16},{16,24},{24,32},{32,40},{40,48},{48,56},{56,6... | collective-permute-start | bytes 5308424 | tf_op jit(solution)/shard_map/while/body/eval_jaxpr/ppermute | solution.py:12
  407.1 35.0 %collective-permute-start.1 = (f32[384,1152]{1,0:T(8,128)}, f32[384,1152]{1,0:T(8,128)}, u32[]{:S(2)}, u32[]{:S(2)}) collective-permute-start(f32[384,1152]{1,0:T(8,128)} %get-tuple-element.112), channel_id=1, source_target_pairs={{120,0},{0,8},{8,16},{16,24},{24,32},{32,40},{40,48},{48,56},{56,6... | collective-permute-start | bytes 5308424 | tf_op jit(solution)/shard_map/while/body/eval_jaxpr/ppermute | solution.py:12
  446.1 35.0 %collective-permute-start.1 = (f32[384,1152]{1,0:T(8,128)}, f32[384,1152]{1,0:T(8,128)}, u32[]{:S(2)}, u32[]{:S(2)}) collective-permute-start(f32[384,1152]{1,0:T(8,128)} %get-tuple-element.112), channel_id=1, source_target_pairs={{120,0},{0,8},{8,16},{16,24},{24,32},{32,40},{40,48},{48,56},{56,6... | collective-permute-start | bytes 5308424 | tf_op jit(solution)/shard_map/while/body/eval_jaxpr/ppermute | solution.py:12
  485.2 35.1 %collective-permute-start.1 = (f32[384,1152]{1,0:T(8,128)}, f32[384,1152]{1,0:T(8,128)}, u32[]{:S(2)}, u32[]{:S(2)}) collective-permute-start(f32[384,1152]{1,0:T(8,128)} %get-tuple-element.112), channel_id=1, source_target_pairs={{120,0},{0,8},{8,16},{16,24},{24,32},{32,40},{40,48},{48,56},{56,6... | collective-permute-start | bytes 5308424 | tf_op jit(solution)/shard_map/while/body/eval_jaxpr/ppermute | solution.py:12
  487.6 29.4 %collective-permute-start = (bf16[384,1152]{1,0:T(8,128)(2,1)}, bf16[384,1152]{1,0:T(8,128)(2,1)S(1)}, u32[]{:S(2)}, u32[]{:S(2)}) collective-permute-start(bf16[384,1152]{1,0:T(8,128)(2,1)} %copy-done.5), channel_id=1, source_target_pairs={{120,0},{0,8},{8,16},{16,24},{24,32},{32,40},{40,48},{48,56},{56,6... | collective-permute-start | bytes 2654216 | tf_op jit(solution)/shard_map/while/body/eval_jaxpr/ppermute | solution.py:12
  524.3 37.1 %collective-permute-start.1 = (f32[384,1152]{1,0:T(8,128)}, f32[384,1152]{1,0:T(8,128)}, u32[]{:S(2)}, u32[]{:S(2)}) collective-permute-start(f32[384,1152]{1,0:T(8,128)} %get-tuple-element.112), channel_id=1, source_target_pairs={{120,0},{0,8},{8,16},{16,24},{24,32},{32,40},{40,48},{48,56},{56,6... | collective-permute-start | bytes 5308424 | tf_op jit(solution)/shard_map/while/body/eval_jaxpr/ppermute | solution.py:12
  526.6 31.5 %collective-permute-start = (bf16[384,1152]{1,0:T(8,128)(2,1)}, bf16[384,1152]{1,0:T(8,128)(2,1)S(1)}, u32[]{:S(2)}, u32[]{:S(2)}) collective-permute-start(bf16[384,1152]{1,0:T(8,128)(2,1)} %copy-done.5), channel_id=1, source_target_pairs={{120,0},{0,8},{8,16},{16,24},{24,32},{32,40},{40,48},{48,56},{56,6... | collective-permute-start | bytes 2654216 | tf_op jit(solution)/shard_map/while/body/eval_jaxpr/ppermute | solution.py:12
  565.4 37.1 %collective-permute-start.1 = (f32[384,1152]{1,0:T(8,128)}, f32[384,1152]{1,0:T(8,128)}, u32[]{:S(2)}, u32[]{:S(2)}) collective-permute-start(f32[384,1152]{1,0:T(8,128)} %get-tuple-element.112), channel_id=1, source_target_pairs={{120,0},{0,8},{8,16},{16,24},{24,32},{32,40},{40,48},{48,56},{56,6... | collective-permute-start | bytes 5308424 | tf_op jit(solution)/shard_map/while/body/eval_jaxpr/ppermute | solution.py:12
  566.3 32.9 %collective-permute-start = (bf16[384,1152]{1,0:T(8,128)(2,1)}, bf16[384,1152]{1,0:T(8,128)(2,1)S(1)}, u32[]{:S(2)}, u32[]{:S(2)}) collective-permute-start(bf16[384,1152]{1,0:T(8,128)(2,1)} %copy-done.5), channel_id=1, source_target_pairs={{120,0},{0,8},{8,16},{16,24},{24,32},{32,40},{40,48},{48,56},{56,6... | collective-permute-start | bytes 2654216 | tf_op jit(solution)/shard_map/while/body/eval_jaxpr/ppermute | solution.py:12
  606.5 184.7 %collective-permute-start.2 = (f32[384,1152]{1,0:T(8,128)}, f32[384,1152]{1,0:T(8,128)}, u32[]{:S(2)}, u32[]{:S(2)}) collective-permute-start(f32[384,1152]{1,0:T(8,128)} %get-tuple-element.41), channel_id=1, source_target_pairs={{120,0},{0,8},{8,16},{16,24},{24,32},{32,40},{40,48},{48,56},{56,6... | collective-permute-start | bytes 5308424 | tf_op jit(solution)/shard_map/ppermute | solution.py:12
  (90 other events, 811.7 us)
Sparse Core Ops, SparseCore 0:
  612.3 175.4 all-reduce.2
where the time goes:
time: 802 us; the launch traced here: 801 us
  waiting for transfers between devices  543 us (68%)
  starting transfers between devices  112 us (14%)
  matrix products  107 us (13%)
  local copies, waits for them, and re-layouts  19.3 us (2%)
  between operations  15.4 us (2%)
    ppermute x31, waiting for transfers between devices, from_behind(): return lax.ppermute(block, axis, route)  368 us
    psum x1, waiting for transfers between devices, shards(): total_down, total_up = lax.psum((part_down, part_up), ('blk', 'dp'))  176 us
    ppermute x31, starting transfers between devices, from_behind(): return lax.ppermute(block, axis, route)  112 us
    dot_general x16, matrix products, column_terms(): lax.dot_general(weights, images, (((0,), (0,)), ((), ())), preferred_elem...  62.1 us
    dot_general x16, matrix products, pair_logits(): lax.dot_general(images, group, (((1,), (1,)), ((), ())), preferred_elemen...  23.3 us
  transfers between devices with their start and end apart: 32, of which 16 were waited for; matrix products, arithmetic and copies ran while one was open for 7% of the time, Pallas kernels for 0%

commit v1 on v0

v1 whole, which is shorter than its diff:
```python
import math

import jax
import jax.numpy as jnp
from jax import lax
from jax.sharding import Mesh, PartitionSpec as P

F32, BF16, F16 = jnp.float32, jnp.bfloat16, jnp.float16
AXES = ("z", "y", "c", "h", "x")
HEIGHT = 1024.0


def from_ahead(block, axis, distance):
    n = lax.axis_size(axis)
    return lax.ppermute(block, axis, [((i + distance) % n, i) for i in range(n)])


def mm(a, b):
    return jnp.dot(a, b, preferred_element_type=F32)


def mm_nt(a, b):
    return lax.dot_general(a, b, (((1,), (1,)), ((), ())), preferred_element_type=F32)


def mm_tn(a, b):
    return lax.dot_general(a, b, (((0,), (0,)), ((), ())), preferred_element_type=F32)


def halves(a):
    high = a.astype(BF16)
    return high, (a - high.astype(F32)).astype(BF16)


def scatter_sum(block, axis):
    n, here, part = 4, lax.axis_index(axis), block.shape[0] // 4
    piece = lambda d: lax.dynamic_slice_in_dim(block, ((here - d) % n) * part, part, 0)
    others = [from_ahead(piece(d), axis, d) for d in (1, 3, 2)]
    return piece(0) + others[0] + others[1] + others[2]


def gathered(block, axis):
    n, here, part = 4, lax.axis_index(axis), block.shape[0]
    whole = jnp.zeros((n * part,) + block.shape[1:], block.dtype)
    others = [(0, block)] + [(d, from_ahead(block, axis, d)) for d in (1, 3, 2)]
    for d, other in others:
        whole = lax.dynamic_update_slice_in_dim(whole, other, ((here + d) % n) * part, 0)
    return whole


def everyones(block, axis):
    return block + from_ahead(block, axis, 1) + from_ahead(block, axis, 3) + from_ahead(block, axis, 2)


def shards(images, texts, proj, down, up, scale, offset):
    own, texts = images[0], texts[0]
    rows, width = texts.shape
    half = rows // 2
    factor = scale[0] / math.sqrt(width)
    bias = offset[0]
    core = lax.axis_index("c")

    ahead = from_ahead(own, "z", 1)
    behind = from_ahead(own, "z", -1)
    across = from_ahead(texts, "y", 1)
    twin = from_ahead(texts, "c", 1)
    across_twin = from_ahead(across, "c", 1)
    far = jnp.concatenate([from_ahead(ahead[:half], "z", 1), from_ahead(behind[half:], "z", -1)])

    near_pair = jnp.concatenate([texts, twin])
    far_pair = jnp.concatenate([across, across_twin])
    group = jnp.concatenate([near_pair, far_pair])
    text_up = jnp.concatenate(halves(mm_nt(group, up)), axis=1)

    def embedded(block):
        hidden = mm(block, down).astype(BF16)
        return hidden, (mm(block, proj) + mm(hidden, up)).astype(BF16)

    def weights_of(columns, embeds, same=False):
        logits = factor * mm_nt(columns, embeds) + bias
        coef = jax.nn.sigmoid(logits)
        if same:
            row = lax.broadcasted_iota(jnp.int32, logits.shape, 0)
            col = lax.broadcasted_iota(jnp.int32, logits.shape, 1)
            coef = jnp.where(row == col, -jax.nn.sigmoid(-logits), coef)
        return (coef * factor).astype(BF16)

    def share(block, hidden, weights):
        inner = mm_tn(weights, text_up)
        rank = inner.shape[1] // 2
        inner = jnp.concatenate(halves(inner[:, :rank] + inner[:, rank:]), axis=1)
        grad = mm_tn(inner, block)
        return grad[:rank] + grad[rank:], mm(weights, hidden)

    hidden, embeds = embedded(own)
    near = weights_of(near_pair, embeds, True)
    weights = jnp.concatenate([near, weights_of(far_pair, embeds)])
    part_down, hidden_sum = share(own, hidden, weights)
    text_sum = mm(weights, embeds)

    sides = jnp.concatenate([ahead, behind])
    hidden, embeds = embedded(sides)
    weights = weights_of(group, embeds)
    d, h = share(sides, hidden, weights)
    part_down, hidden_sum = part_down + d, hidden_sum + h
    text_sum = text_sum + mm(weights, embeds)

    hidden, embeds = embedded(far)
    weights = weights_of(group, embeds)
    d, h = share(far, hidden, weights)
    part_down, hidden_sum = part_down + d, hidden_sum + h
    rank = hidden_sum.shape[1]
    part_up = mm_tn(jnp.concatenate(halves(hidden_sum), axis=1), group)
    part_up = part_up[:rank] + part_up[rank:]

    first = core == 0
    kept = jnp.where(first, part_down, part_up)
    kept = kept + from_ahead(jnp.where(first, part_up, part_down), "c", 1)
    kept = scatter_sum(kept, "z")
    kept = everyones(kept, "x")
    kept = everyones(kept, ("y", "h"))
    kept = gathered(kept, "z") / (rows * 16)
    other = from_ahead(kept, "c", 1)
    grad_down = jnp.where(first, kept, other).T
    grad_up = jnp.where(first, other, kept)

    text_sum = text_sum + mm(weights, embeds)
    away = text_sum[2 * rows : 3 * rows] + from_ahead(text_sum[3 * rows :], "c", 1)
    height = jnp.maximum(jnp.max(jnp.abs(away), axis=1, keepdims=True), 1e-30)
    packed = (away * (HEIGHT / height)).astype(F16)
    packed = from_ahead(packed, "y", 1)
    height = from_ahead(jnp.broadcast_to(height, (rows, 128)), "y", 1)[:, :1]
    text_grad = text_sum[:rows] + from_ahead(text_sum[rows : 2 * rows], "c", 1)
    text_grad = text_grad + packed.astype(F32) * (height / HEIGHT)
    return text_grad[None], grad_down, grad_up


def solution(mesh):
    grid = Mesh(mesh.devices.reshape(4, 2, 2, 2, 4), AXES)
    blk, dp = ("z", "y", "c"), ("h", "x")
    placed = (P(dp, blk, None), P(dp, blk, None), P(), P(), P(), P(), P())
    return jax.shard_map(
        shards,
        mesh=grid,
        in_specs=placed,
        out_specs=(P(dp, blk, None), P(), P()),
        check_vma=False,
    )
```

time: 802 us -> 144 us (0.18)
  waiting for transfers between devices: 543 us -> 45.8 us
  starting transfers between devices: 112 us -> 33 us
  matrix products: 107 us -> 41.6 us
  between operations: 15.4 us -> 2.5 us
    ppermute x31 -> x25, waiting for transfers between devices: 368 us -> 45.8 us  [from_ahead(): lax.ppermute(block, axis, [((i + distance) % n, i) for i in range(n)])]
    psum x1 -> x0, waiting for transfers between devices: 176 us -> none  [shards(): total_down, total_up = lax.psum((part_down, part_up), ('blk', 'dp'))]
    ppermute x31 -> x25, starting transfers between devices: 112 us -> 33 us  [from_ahead(): lax.ppermute(block, axis, [((i + distance) % n, i) for i in range(n)])]
    dot_general x53 -> x27, matrix products: 107 us -> 41.6 us  [the longest x15 20.5 us: mm(): return jnp.dot(a, b, preferred_element_type=F32)]
    while x165 -> x0, local copies, waits for them, and re-layouts: 15.1 us -> none
  transfers between devices with their start and end apart: 32 -> 25, of which waited for: 16 -> 7; matrix products, arithmetic and copies ran while one was open for 7% -> 20% of each run, Pallas kernels for 0% -> 0%
where the time goes in v1:
time: 144 us
  waiting for transfers between devices  45.8 us (32%)
  matrix products  41.6 us (29%)
  starting transfers between devices  33 us (23%)
  local copies, waits for them, and re-layouts  12.2 us (8%)
  other arithmetic  8.49 us (6%)
  between operations  2.5 us (2%)
    ppermute x25, waiting for transfers between devices, from_ahead(): lax.ppermute(block, axis, [((i + distance) % n, i) for i in range(n)])  45.8 us
    ppermute x25, starting transfers between devices, from_ahead(): lax.ppermute(block, axis, [((i + distance) % n, i) for i in range(n)])  33 us
    dot_general x15, matrix products, mm(): return jnp.dot(a, b, preferred_element_type=F32)  20.5 us
    dot_general x5, matrix products, mm_nt(): lax.dot_general(a, b, (((1,), (1,)), ((), ())), preferred_element_type=F32)  16.7 us
    unnamed x23, local copies, waits for them, and re-layouts  7.3 us
    dot_general x7, matrix products, mm_tn(): lax.dot_general(a, b, (((0,), (0,)), ((), ())), preferred_element_type=F32)  4.44 us
    broadcast_in_dim x1, other arithmetic, shards(): return (text_grad[None], grad_down, grad_up)  3.25 us
  transfers between devices with their start and end apart: 25, of which 7 were waited for; matrix products, arithmetic and copies ran while one was open for 20% of the time, Pallas kernels for 0%

profile of v1, /device:TPU:1, one launch (start us, length us, event | category | flops | bytes accessed | tf_op | source)
XLA Modules:
  0.0 143.6 jit_solution(10593717885552509197)
XLA Ops:
  0.6 2.2 %collective-permute-start.1 = (bf16[384,1152]{1,0:T(8,128)(2,1)}, bf16[384,1152]{1,0:T(8,128)(2,1)}, u32[]{:S(2)}, u32[]{:S(2)}) collective-permute-start(bf16[384,1152]{1,0:T(8,128)(2,1)} %bitcast.55), channel_id=1, source_target_pairs={{16,0},{0,16},{17,1},{1,17},{18,2},{2,18},{19,3},{3,19},{20,4},{4,... | collective-permute-start | bytes 2654216 | tf_op jit(solution)/shard_map/ppermute | solution.py:15
  3.8 3.8 %collective-permute-start.3 = (bf16[384,1152]{1,0:T(8,128)(2,1)}, bf16[384,1152]{1,0:T(8,128)(2,1)}, u32[]{:S(2)}, u32[]{:S(2)}) collective-permute-start(bf16[384,1152]{1,0:T(8,128)(2,1)} %bitcast.53), channel_id=1, source_target_pairs={{32,0},{64,32},{96,64},{0,96},{33,1},{65,33},{97,65},{1,97},{34,2}... | collective-permute-start | bytes 2654216 | tf_op jit(solution)/shard_map/ppermute | solution.py:15
  9.2 2.6 %fusion.84 = f32[384,1152]{1,0:T(8,128)S(1)} fusion(bf16[1152,1152]{1,0:T(8,128)(2,1)S(1)} %copy-done, bf16[1,384,1152]{2,1,0:T(8,128)(2,1)} %param.7), kind=kOutput, calls=%fused_computation.122 | convolution fusion | flops 1019215872 | bytes 5308416 | tf_op jit(solution)/shard_map/dot_general | solution.py:19
  13.7 13.3 %collective-permute-done.3 = bf16[384,1152]{1,0:T(8,128)(2,1)} collective-permute-done((bf16[384,1152]{1,0:T(8,128)(2,1)}, bf16[384,1152]{1,0:T(8,128)(2,1)}, u32[]{:S(2)}, u32[]{:S(2)}) %collective-permute-start.3) | collective-permute-done | bytes 884768 | tf_op jit(solution)/shard_map/ppermute | solution.py:15
  28.0 3.5 %collective-permute-start.5 = (bf16[192,1152]{1,0:T(8,128)(2,1)S(1)}, bf16[192,1152]{1,0:T(8,128)(2,1)S(1)}, u32[]{:S(2)}, u32[]{:S(2)}) collective-permute-start(bf16[192,1152]{1,0:T(8,128)(2,1)S(1)} %slice.84), channel_id=1, source_target_pairs={{32,0},{64,32},{96,64},{0,96},{33,1},{65,33},{97,65},{1,97},{34,2}... | collective-permute-start | bytes 1327112 | tf_op jit(solution)/shard_map/ppermute | solution.py:15
  37.8 2.7 %fusion = bf16[768,1152]{1,0:T(8,128)(2,1)S(1)} fusion(f32[768,1152]{1,0:T(8,128)S(1)} %fusion.92, bf16[768,1152]{1,0:T(8,128)(2,1)S(1)} %constant_dynamic-update-slice_fusion, bf16[1152,1152]{1,0:T(8,128)(2,1)S(1)} %copy-done), kind=kOutput, calls=%fused_computation.5 | convolution fusion | flops 2040201216 | bytes 9732096 | tf_op jit(solution)/shard_map/dot_general | solution.py:19
  40.6 2.5 %multiply_convert_fusion.3 = bf16[768,384]{1,0:T(8,128)(2,1)S(1)} fusion(bf16[384,1152]{1,0:T(8,128)(2,1)S(1)} %fusion.9, bf16[384,1152]{1,0:T(8,128)(2,1)} %collective-permute-done, bf16[384,1152]{1,0:T(8,128)(2,1)S(1)} %bitcast.57, f32[]{:T(128)} %bitcast.49, f32[]{:T(128)} %bitcast), kind=kOutput, calls=%fused_computation.43 | convolution fusion | flops 686555136 | bytes 3244040 | tf_op jit(solution)/shard_map/dot_general | solution.py:23
  46.8 2.4 %multiply_convert_fusion.2 = bf16[768,384]{1,0:T(8,128)(2,1)S(1)} fusion(bf16[384,1152]{1,0:T(8,128)(2,1)S(1)} %fusion.9, bf16[384,1152]{1,0:T(8,128)(2,1)S(1)} %collective-permute-done.2, bf16[384,1152]{1,0:T(8,128)(2,1)} %collective-permute-done.1, f32[]{:T(128)} %bitcast.52, f32[]{:T(128)} %bitcast), kind=kOutput, calls=%fused_computation.42 | convolution fusion | flops 685080576 | bytes 3244040 | tf_op jit(solution)/shard_map/dot_general | solution.py:23
  49.8 2.6 %fusion.91 = (bf16[1536,64]{0,1:T(8,128)(2,1)S(1)}, bf16[1536,64]{0,1:T(8,128)(2,1)S(1)}) fusion(bf16[64,1152]{1,0:T(8,128)(2,1)S(1)} %copy-done.6, bf16[384,1152]{1,0:T(8,128)(2,1)S(1)} %collective-permute-done.2, bf16[384,1152]{1,0:T(8,128)(2,1)} %collective-permute-done.1, bf16[384,1152]{1,0:T(8,128)(2,1)} %collective-permute-done, ...), kind=kOutput, calls=%fused_computation.125 | convolution fusion | flops 241041408 | bytes 4079616 | tf_op jit(solution)/shard_map/dot_general | solution.py:23
  52.8 5.3 %multiply_convert_fusion = bf16[1536,768]{1,0:T(8,128)(2,1)S(1)} fusion(bf16[768,1152]{1,0:T(8,128)(2,1)S(1)} %fusion, f32[]{:T(128)} %bitcast.50, f32[]{:T(128)} %bitcast, bf16[384,1152]{1,0:T(8,128)(2,1)S(1)} %collective-permute-done.2, bf16[384,1152]{1,0:T(8,128)(2,1)} %collective-permute-done.1, bf16[384,1152]{1,0:T(8,128)(2,1)} %collective-permute-done, ...), kind=kOutput, calls=%fused_computation.2 | convolution fusion | flops 2740322304 | bytes 7667720 | tf_op jit(solution)/shard_map/dot_general | solution.py:23
  58.5 3.3 %fusion.93 = f32[1536,1152]{0,1:T(8,128)S(1)} fusion(bf16[1536,768]{1,0:T(8,128)(2,1)S(1)} %multiply_convert_fusion, bf16[768,1152]{1,0:T(8,128)(2,1)S(1)} %fusion), kind=kOutput, calls=%fused_computation.127 | convolution fusion | flops 2717908992 | bytes 11206656 | tf_op jit(solution)/shard_map/dot_general | solution.py:19
  62.7 3.9 %fusion.8 = bf16[1536,384]{1,0:T(8,128)(2,1)S(1)} fusion(bf16[384,1152]{1,0:T(8,128)(2,1)S(1)} %fusion.7, f32[]{:T(128)} %bitcast.51, f32[]{:T(128)} %bitcast, bf16[384,1152]{1,0:T(8,128)(2,1)S(1)} %collective-permute-done.2, bf16[384,1152]{1,0:T(8,128)(2,1)} %collective-permute-done.1, bf16[384,1152]{1,0:T(8,128)(2,1)} %collective-permute-done, ...), kind=kOutput, calls=%fused_computation.16 | convolution fusion | flops 1377239040 | bytes 5603336 | tf_op jit(solution)/shard_map/dot_general | solution.py:23
  69.0 2.1 %fusion.45 = f32[128,1152]{1,0:T(8,128)S(1)} fusion(bf16[1536,64]{0,1:T(8,128)(2,1)S(1)} %get-tuple-element.13, bf16[1536,64]{0,1:T(8,128)(2,1)S(1)} %get-tuple-element.14, bf16[384,1152]{1,0:T(8,128)(2,1)S(1)} %collective-permute-done.2, bf16[384,1152]{1,0:T(8,128)(2,1)} %collective-permute-done.1, bf16[384,1152]{1,0:T(8,128)(2,1)} %collective-permute-done, ...), kind=kOutput, calls=%fused_computation.49 | convolution fusion | flops 467927040 | bytes 4521984 | tf_op jit(solution)/shard_map/dot_general | solution.py:27
  77.1 2.3 %convolution_add_fusion = f32[1536,1152]{0,1:T(8,128)S(1)} fusion(f32[1536,1152]{0,1:T(8,128)S(1)} %convolution_add_fusion.1, bf16[1536,384]{1,0:T(8,128)(2,1)S(1)} %fusion.8, bf16[384,1152]{1,0:T(8,128)(2,1)S(1)} %fusion.7), kind=kOutput, calls=%fused_computation | convolution fusion | flops 1360723968 | bytes 16220160 | tf_op jit(solution)/shard_map/dot_general | solution.py:19
  79.4 2.9 %copy-done.2 = f32[1536,1152]{0,1:T(8,128)} copy-done((f32[1536,1152]{0,1:T(8,128)}, f32[1536,1152]{0,1:T(8,128)S(1)}, u32[]{:S(2)}) %copy-start.2) | copy-done | bytes 7077912
  84.2 2.8 %collective-permute-start.15 = (f32[16,1152]{1,0:T(8,128)S(1)}, f32[16,1152]{1,0:T(8,128)S(1)}, u32[]{:S(2)}, u32[]{:S(2)}) collective-permute-start(f32[16,1152]{1,0:T(8,128)S(1)} %add_add_fusion.2), channel_id=1, source_target_pairs={{1,0},{2,1},{3,2},{0,3},{5,4},{6,5},{7,6},{4,7},{9,8},{10,9},{11,1... | collective-permute-start | bytes 221192 | tf_op jit(solution)/shard_map/ppermute | solution.py:15
  88.8 4.9 %collective-permute-done.16 = f32[16,1152]{1,0:T(8,128)S(1)} collective-permute-done((f32[16,1152]{1,0:T(8,128)S(1)}, f32[16,1152]{1,0:T(8,128)S(1)}, u32[]{:S(2)}, u32[]{:S(2)}) %collective-permute-start.16) | collective-permute-done | bytes 73760 | tf_op jit(solution)/shard_map/ppermute | solution.py:15
  100.6 2.5 %collective-permute-start.21 = (f32[16,1152]{1,0:T(8,128)S(1)}, f32[16,1152]{1,0:T(8,128)S(1)}, u32[]{:S(2)}, u32[]{:S(2)}) collective-permute-start(f32[16,1152]{1,0:T(8,128)S(1)} %get-tuple-element.10), channel_id=1, source_target_pairs={{32,0},{64,32},{96,64},{0,96},{33,1},{65,33},{97,65},{1,97},{34,2}... | collective-permute-start | bytes 221192 | tf_op jit(solution)/shard_map/ppermute | solution.py:15
  103.1 2.3 %collective-permute-start.23 = (f32[16,1152]{1,0:T(8,128)S(1)}, f32[16,1152]{1,0:T(8,128)S(1)}, u32[]{:S(2)}, u32[]{:S(2)}) collective-permute-start(f32[16,1152]{1,0:T(8,128)S(1)} %get-tuple-element.10), channel_id=1, source_target_pairs={{64,0},{96,32},{0,64},{32,96},{65,1},{97,33},{1,65},{33,97},{66,2}... | collective-permute-start | bytes 221192 | tf_op jit(solution)/shard_map/ppermute | solution.py:15
  107.1 2.3 %multiply_convert_fusion.1 = (f16[384,1152]{0,1:T(8,128)(2,1)S(1)}, f32[384,1152]{0,1:T(8,128)S(1)}) fusion(f32[384]{0:T(512)S(1)} %get-tuple-element.31, f32[384,1152]{0,1:T(8,128)S(1)} %collective-permute-done.8, f32[1536,1152]{0,1:T(8,128)} %copy-done.2), kind=kLoop, calls=%fused_computation.32 | loop fusion | flops 1327104 | bytes 7964160 | tf_op jit(solution)/shard_map/convert_element_type | solution.py:130
  109.4 2.8 %collective-permute-start.7 = (f32[384,1152]{0,1:T(8,128)S(1)}, f32[384,1152]{0,1:T(8,128)S(1)}, u32[]{:S(2)}, u32[]{:S(2)}) collective-permute-start(f32[384,1152]{0,1:T(8,128)S(1)} %get-tuple-element.22), channel_id=1, source_target_pairs={{8,0},{0,8},{9,1},{1,9},{10,2},{2,10},{11,3},{3,11},{12,4},{4,12},... | collective-permute-start | bytes 5308424 | tf_op jit(solution)/shard_map/ppermute | solution.py:15
  116.9 20.7 %collective-permute-done.10 = f32[384,128]{0,1:T(8,128)S(1)} collective-permute-done((f32[384,128]{0,1:T(8,128)S(1)}, f32[384,128]{0,1:T(8,128)S(1)}, u32[]{:S(2)}, u32[]{:S(2)}) %collective-permute-start.10) | collective-permute-done | bytes 196640 | tf_op jit(solution)/shard_map/ppermute | solution.py:15
  137.6 3.3 %fusion.11 = f32[1,384,1152]{1,2,0:T(8,128)} fusion(f32[384,1152]{0,1:T(8,128)S(1)} %collective-permute-done.7, f32[1536,1152]{0,1:T(8,128)} %copy-done.2, f16[384,1152]{0,1:T(8,128)(2,1)S(1)} %collective-permute-done.9, f32[384]{0:T(512)S(1)} %fusion.70), kind=kLoop, calls=%fused_computation.23 | loop fusion | flops 1769472 | bytes 6194688 | tf_op jit(solution)/shard_map/broadcast_in_dim | solution.py:135
  140.9 2.8 %copy.11 = f32[1,384,1152]{2,1,0:T(8,128)} copy(f32[1,384,1152]{1,2,0:T(8,128)} %fusion.11) | data formatting | bytes 3538944
  (102 shorter events, 41.4 us)
Async XLA Ops:
  0.6 35.2 %collective-permute-start.1 = (bf16[384,1152]{1,0:T(8,128)(2,1)}, bf16[384,1152]{1,0:T(8,128)(2,1)}, u32[]{:S(2)}, u32[]{:S(2)}) collective-permute-start(bf16[384,1152]{1,0:T(8,128)(2,1)} %bitcast.55), channel_id=1, source_target_pairs={{16,0},{0,16},{17,1},{1,17},{18,2},{2,18},{19,3},{3,19},{20,4},{4,... | collective-permute-start | bytes 2654216 | tf_op jit(solution)/shard_map/ppermute | solution.py:15
  2.9 37.7 %collective-permute-start = (bf16[384,1152]{1,0:T(8,128)(2,1)}, bf16[384,1152]{1,0:T(8,128)(2,1)}, u32[]{:S(2)}, u32[]{:S(2)}) collective-permute-start(bf16[384,1152]{1,0:T(8,128)(2,1)} %bitcast.56), channel_id=1, source_target_pairs={{8,0},{0,8},{9,1},{1,9},{10,2},{2,10},{11,3},{3,11},{12,4},{4,12},... | collective-permute-start | bytes 2654216 | tf_op jit(solution)/shard_map/ppermute | solution.py:15
  3.8 23.2 %collective-permute-start.3 = (bf16[384,1152]{1,0:T(8,128)(2,1)}, bf16[384,1152]{1,0:T(8,128)(2,1)}, u32[]{:S(2)}, u32[]{:S(2)}) collective-permute-start(bf16[384,1152]{1,0:T(8,128)(2,1)} %bitcast.53), channel_id=1, source_target_pairs={{32,0},{64,32},{96,64},{0,96},{33,1},{65,33},{97,65},{1,97},{34,2}... | collective-permute-start | bytes 2654216 | tf_op jit(solution)/shard_map/ppermute | solution.py:15
  7.6 23.9 %collective-permute-start.4 = (bf16[384,1152]{1,0:T(8,128)(2,1)}, bf16[384,1152]{1,0:T(8,128)(2,1)}, u32[]{:S(2)}, u32[]{:S(2)}) collective-permute-start(bf16[384,1152]{1,0:T(8,128)(2,1)} %bitcast.54), channel_id=1, source_target_pairs={{96,0},{0,32},{32,64},{64,96},{97,1},{1,33},{33,65},{65,97},{98,2}... | collective-permute-start | bytes 2654216 | tf_op jit(solution)/shard_map/ppermute | solution.py:15
  28.0 15.1 %collective-permute-start.5 = (bf16[192,1152]{1,0:T(8,128)(2,1)S(1)}, bf16[192,1152]{1,0:T(8,128)(2,1)S(1)}, u32[]{:S(2)}, u32[]{:S(2)}) collective-permute-start(bf16[192,1152]{1,0:T(8,128)(2,1)S(1)} %slice.84), channel_id=1, source_target_pairs={{32,0},{64,32},{96,64},{0,96},{33,1},{65,33},{97,65},{1,97},{34,2}... | collective-permute-start | bytes 1327112 | tf_op jit(solution)/shard_map/ppermute | solution.py:15
  32.6 11.9 %collective-permute-start.6 = (bf16[192,1152]{1,0:T(8,128)(2,1)S(1)}, bf16[192,1152]{1,0:T(8,128)(2,1)S(1)}, u32[]{:S(2)}, u32[]{:S(2)}) collective-permute-start(bf16[192,1152]{1,0:T(8,128)(2,1)S(1)} %slice.85), channel_id=1, source_target_pairs={{96,0},{0,32},{32,64},{64,96},{97,1},{1,33},{33,65},{65,97},{98,2}... | collective-permute-start | bytes 1327112 | tf_op jit(solution)/shard_map/ppermute | solution.py:15
  35.9 11.0 %collective-permute-start.2 = (bf16[384,1152]{1,0:T(8,128)(2,1)}, bf16[384,1152]{1,0:T(8,128)(2,1)S(1)}, u32[]{:S(2)}, u32[]{:S(2)}) collective-permute-start(bf16[384,1152]{1,0:T(8,128)(2,1)} %collective-permute-done.1), channel_id=1, source_target_pairs={{8,0},{0,8},{9,1},{1,9},{10,2},{2,10},{11,3},{3,11},{12,4},{4,12},... | collective-permute-start | bytes 2654216 | tf_op jit(solution)/shard_map/ppermute | solution.py:15
  71.3 4.1 %collective-permute-start.11 = (f32[64,1152]{1,0:T(8,128)S(1)}, f32[64,1152]{1,0:T(8,128)S(1)}, u32[]{:S(2)}, u32[]{:S(2)}) collective-permute-start(f32[64,1152]{1,0:T(8,128)S(1)} %get-tuple-element.11), channel_id=1, source_target_pairs={{8,0},{0,8},{9,1},{1,9},{10,2},{2,10},{11,3},{3,11},{12,4},{4,12},... | collective-permute-start | bytes 884744 | tf_op jit(solution)/shard_map/ppermute | solution.py:15
  75.6 8.6 %collective-permute-start.12 = (f32[16,1152]{1,0:T(8,128)S(1)}, f32[16,1152]{1,0:T(8,128)S(1)}, u32[]{:S(2)}, u32[]{:S(2)}) collective-permute-start(f32[16,1152]{1,0:T(8,128)S(1)} %get-tuple-element.27), channel_id=1, source_target_pairs={{32,0},{64,32},{96,64},{0,96},{33,1},{65,33},{97,65},{1,97},{34,2}... | collective-permute-start | bytes 221192 | tf_op jit(solution)/shard_map/ppermute | solution.py:15
  75.7 8.5 %collective-permute-start.13 = (f32[16,1152]{1,0:T(8,128)S(1)}, f32[16,1152]{1,0:T(8,128)S(1)}, u32[]{:S(2)}, u32[]{:S(2)}) collective-permute-start(f32[16,1152]{1,0:T(8,128)S(1)} %get-tuple-element.29), channel_id=1, source_target_pairs={{96,0},{0,32},{32,64},{64,96},{97,1},{1,33},{33,65},{65,97},{98,2}... | collective-permute-start | bytes 221192 | tf_op jit(solution)/shard_map/ppermute | solution.py:15
  77.1 7.1 %collective-permute-start.14 = (f32[16,1152]{1,0:T(8,128)S(1)}, f32[16,1152]{1,0:T(8,128)S(1)}, u32[]{:S(2)}, u32[]{:S(2)}) collective-permute-start(f32[16,1152]{1,0:T(8,128)S(1)} %get-tuple-element.28), channel_id=1, source_target_pairs={{64,0},{96,32},{0,64},{32,96},{65,1},{97,33},{1,65},{33,97},{66,2}... | collective-permute-start | bytes 221192 | tf_op jit(solution)/shard_map/ppermute | solution.py:15
  83.6 21.8 %collective-permute-start.8 = (f32[384,1152]{0,1:T(8,128)}, f32[384,1152]{0,1:T(8,128)S(1)}, u32[]{:S(2)}, u32[]{:S(2)}) collective-permute-start(f32[384,1152]{0,1:T(8,128)} %slice.89), channel_id=1, source_target_pairs={{8,0},{0,8},{9,1},{1,9},{10,2},{2,10},{11,3},{3,11},{12,4},{4,12},... | collective-permute-start | bytes 5308424 | tf_op jit(solution)/shard_map/ppermute | solution.py:15
  84.2 4.5 %collective-permute-start.15 = (f32[16,1152]{1,0:T(8,128)S(1)}, f32[16,1152]{1,0:T(8,128)S(1)}, u32[]{:S(2)}, u32[]{:S(2)}) collective-permute-start(f32[16,1152]{1,0:T(8,128)S(1)} %add_add_fusion.2), channel_id=1, source_target_pairs={{1,0},{2,1},{3,2},{0,3},{5,4},{6,5},{7,6},{4,7},{9,8},{10,9},{11,1... | collective-permute-start | bytes 221192 | tf_op jit(solution)/shard_map/ppermute | solution.py:15
  87.1 6.6 %collective-permute-start.16 = (f32[16,1152]{1,0:T(8,128)S(1)}, f32[16,1152]{1,0:T(8,128)S(1)}, u32[]{:S(2)}, u32[]{:S(2)}) collective-permute-start(f32[16,1152]{1,0:T(8,128)S(1)} %add_add_fusion.2), channel_id=1, source_target_pairs={{3,0},{0,1},{1,2},{2,3},{7,4},{4,5},{5,6},{6,7},{11,8},{8,9},{9,10... | collective-permute-start | bytes 221192 | tf_op jit(solution)/shard_map/ppermute | solution.py:15
  87.1 6.6 %collective-permute-start.17 = (f32[16,1152]{1,0:T(8,128)S(1)}, f32[16,1152]{1,0:T(8,128)S(1)}, u32[]{:S(2)}, u32[]{:S(2)}) collective-permute-start(f32[16,1152]{1,0:T(8,128)S(1)} %add_add_fusion.2), channel_id=1, source_target_pairs={{2,0},{3,1},{0,2},{1,3},{6,4},{7,5},{4,6},{5,7},{10,8},{11,9},{8,1... | collective-permute-start | bytes 221192 | tf_op jit(solution)/shard_map/ppermute | solution.py:15
  93.7 4.8 %collective-permute-start.18 = (f32[16,1152]{1,0:T(8,128)S(1)}, f32[16,1152]{1,0:T(8,128)S(1)}, u32[]{:S(2)}, u32[]{:S(2)}) collective-permute-start(f32[16,1152]{1,0:T(8,128)S(1)} %add_add_fusion.1), channel_id=1, source_target_pairs={{4,0},{16,4},{20,16},{0,20},{5,1},{17,5},{21,17},{1,21},{6,2},{18,... | collective-permute-start | bytes 221192 | tf_op jit(solution)/shard_map/ppermute | solution.py:15
  95.7 4.9 %collective-permute-start.19 = (f32[16,1152]{1,0:T(8,128)S(1)}, f32[16,1152]{1,0:T(8,128)S(1)}, u32[]{:S(2)}, u32[]{:S(2)}) collective-permute-start(f32[16,1152]{1,0:T(8,128)S(1)} %add_add_fusion.1), channel_id=1, source_target_pairs={{20,0},{0,4},{4,16},{16,20},{21,1},{1,5},{5,17},{17,21},{22,2},{2,... | collective-permute-start | bytes 221192 | tf_op jit(solution)/shard_map/ppermute | solution.py:15
  96.8 3.8 %collective-permute-start.20 = (f32[16,1152]{1,0:T(8,128)S(1)}, f32[16,1152]{1,0:T(8,128)S(1)}, u32[]{:S(2)}, u32[]{:S(2)}) collective-permute-start(f32[16,1152]{1,0:T(8,128)S(1)} %add_add_fusion.1), channel_id=1, source_target_pairs={{16,0},{20,4},{0,16},{4,20},{17,1},{21,5},{1,17},{5,21},{18,2},{22... | collective-permute-start | bytes 221192 | tf_op jit(solution)/shard_map/ppermute | solution.py:15
  100.6 4.8 %collective-permute-start.21 = (f32[16,1152]{1,0:T(8,128)S(1)}, f32[16,1152]{1,0:T(8,128)S(1)}, u32[]{:S(2)}, u32[]{:S(2)}) collective-permute-start(f32[16,1152]{1,0:T(8,128)S(1)} %get-tuple-element.10), channel_id=1, source_target_pairs={{32,0},{64,32},{96,64},{0,96},{33,1},{65,33},{97,65},{1,97},{34,2}... | collective-permute-start | bytes 221192 | tf_op jit(solution)/shard_map/ppermute | solution.py:15
  103.1 9.2 %collective-permute-start.22 = (f32[16,1152]{1,0:T(8,128)S(1)}, f32[16,1152]{1,0:T(8,128)S(1)}, u32[]{:S(2)}, u32[]{:S(2)}) collective-permute-start(f32[16,1152]{1,0:T(8,128)S(1)} %get-tuple-element.10), channel_id=1, source_target_pairs={{96,0},{0,32},{32,64},{64,96},{97,1},{1,33},{33,65},{65,97},{98,2}... | collective-permute-start | bytes 221192 | tf_op jit(solution)/shard_map/ppermute | solution.py:15
  103.1 9.2 %collective-permute-start.23 = (f32[16,1152]{1,0:T(8,128)S(1)}, f32[16,1152]{1,0:T(8,128)S(1)}, u32[]{:S(2)}, u32[]{:S(2)}) collective-permute-start(f32[16,1152]{1,0:T(8,128)S(1)} %get-tuple-element.10), channel_id=1, source_target_pairs={{64,0},{96,32},{0,64},{32,96},{65,1},{97,33},{1,65},{33,97},{66,2}... | collective-permute-start | bytes 221192 | tf_op jit(solution)/shard_map/ppermute | solution.py:15
  109.4 28.2 %collective-permute-start.7 = (f32[384,1152]{0,1:T(8,128)S(1)}, f32[384,1152]{0,1:T(8,128)S(1)}, u32[]{:S(2)}, u32[]{:S(2)}) collective-permute-start(f32[384,1152]{0,1:T(8,128)S(1)} %get-tuple-element.22), channel_id=1, source_target_pairs={{8,0},{0,8},{9,1},{1,9},{10,2},{2,10},{11,3},{3,11},{12,4},{4,12},... | collective-permute-start | bytes 5308424 | tf_op jit(solution)/shard_map/ppermute | solution.py:15
  112.5 25.1 %collective-permute-start.9 = (f16[384,1152]{0,1:T(8,128)(2,1)S(1)}, f16[384,1152]{0,1:T(8,128)(2,1)S(1)}, u32[]{:S(2)}, u32[]{:S(2)}) collective-permute-start(f16[384,1152]{0,1:T(8,128)(2,1)S(1)} %get-tuple-element.21), channel_id=1, source_target_pairs={{16,0},{0,16},{17,1},{1,17},{18,2},{2,18},{19,3},{3,19},{20,4},{4,... | collective-permute-start | bytes 2654216 | tf_op jit(solution)/shard_map/ppermute | solution.py:15
  113.1 24.5 %collective-permute-start.10 = (f32[384,128]{0,1:T(8,128)S(1)}, f32[384,128]{0,1:T(8,128)S(1)}, u32[]{:S(2)}, u32[]{:S(2)}) collective-permute-start(f32[384,128]{0,1:T(8,128)S(1)} %broadcast_in_dim.12), channel_id=1, source_target_pairs={{16,0},{0,16},{17,1},{1,17},{18,2},{2,18},{19,3},{3,19},{20,4},{4,... | collective-permute-start | bytes 589832 | tf_op jit(solution)/shard_map/ppermute | solution.py:15
  (11 other events, 44.6 us)

commit v2 on v1

v2 whole, which is shorter than its diff:
```python
import math

import jax
import jax.numpy as jnp
from jax import lax
from jax.experimental import pallas as pl
from jax.experimental.pallas import tpu as pltpu
from jax.sharding import Mesh, PartitionSpec as P

F32, BF16, F16 = jnp.float32, jnp.bfloat16, jnp.float16
AXES = ("z", "y", "c", "h", "x")
LOG2E = 1.4426950408889634
HEIGHT = 1024.0
MIB = 1 << 20


def from_ahead(block, axis, distance):
    n = lax.axis_size(axis)
    return lax.ppermute(block, axis, [((i + distance) % n, i) for i in range(n)])


def mm(a, b):
    return jnp.dot(a, b, preferred_element_type=F32)


def mm_nt(a, b):
    return lax.dot_general(a, b, (((1,), (1,)), ((), ())), preferred_element_type=F32)


def mm_tn(a, b):
    return lax.dot_general(a, b, (((0,), (0,)), ((), ())), preferred_element_type=F32)


def halves(a):
    high = a.astype(BF16)
    return high, (a - high.astype(F32)).astype(BF16)


def embed(images, at, both, proj, down, up):
    here = slice(at, at + images.shape[0])
    width, rank = proj.shape[1], down.shape[1]
    hidden = mm(images[...], down[...]).astype(BF16)
    both[here, :width] = (mm(images[...], proj[...]) + mm(hidden, up[...])).astype(BF16)
    both[here, width : width + rank] = hidden
    both[here, width + rank :] = jnp.zeros((images.shape[0], both.shape[1] - width - rank), BF16)


def gate(sims, consts):
    power = jnp.minimum(sims * consts[0] + consts[1], 126.0)
    return (consts[2] / (1.0 + jnp.exp2(power))).astype(BF16)


def gate_matching(sims, consts):
    power = sims * consts[0] + consts[1]
    other = consts[2] / (1.0 + jnp.exp2(jnp.minimum(power, 126.0)))
    match = -consts[2] / (1.0 + jnp.exp2(jnp.minimum(-power, 126.0)))
    row = lax.broadcasted_iota(jnp.int32, sims.shape, 0)
    col = lax.broadcasted_iota(jnp.int32, sims.shape, 1)
    return jnp.where(row == col, match, other).astype(BF16)


def text_ups(texts, up, out, at):
    high, low = halves(mm_nt(up[...], texts[...]))
    out[:, at : at + texts.shape[0]] = jnp.concatenate([high, low])


def down_share(inner, images):
    rank = inner.shape[0] // 2
    pair = jnp.concatenate(halves(inner[:rank] + inner[rank:]))
    grad = mm(pair, images)
    return grad[:rank] + grad[rank:]


def own_kernel(consts, own, t0, t1, proj, down, up, both, ups, s0, s1, h0, h1, inner, w):
    width, rows = proj.shape[1], own.shape[0]
    embed(own, 0, both, proj, down, up)
    for k, (texts, s, h) in enumerate(((t0, s0, h0), (t1, s1, h1))):
        text_ups(texts, up, ups, k * rows)
        sims = mm_nt(texts[...], both[:, :width])
        w[...] = gate(sims, consts) if k else gate_matching(sims, consts)
        sums = mm(w[...], both[...])
        s[...], h[...] = sums[:, :width], sums[:, width:]
        part = mm(ups[:, k * rows : (k + 1) * rows], w[...])
        inner[...] = inner[...] + part if k else part


def side_kernel(consts, a, b, t0, t1, ups, proj, down, up, s0, s1, h0, h1, both, o0, o1, g0, g1, inner, w):
    width, rows = proj.shape[1], a.shape[0]
    embed(a, 0, both, proj, down, up)
    embed(b, rows, both, proj, down, up)
    for k, (texts, s, h, o, g) in enumerate(((t0, s0, h0, o0, g0), (t1, s1, h1, o1, g1))):
        w[...] = gate(mm_nt(texts[...], both[:, :width]), consts)
        sums = mm(w[...], both[...])
        o[...], g[...] = s[...] + sums[:, :width], h[...] + sums[:, width:]
        part = mm(ups[:, k * rows : (k + 1) * rows], w[...])
        inner[...] = inner[...] + part if k else part


def far_text_kernel(consts, both0, both1, t0, t1, up, inner0, inner1, own, a, b, ups, s0, s1, h0, h1, grad, w0, w1):
    rows, width = own.shape
    sums0, sums1 = inner0[...], inner1[...]
    for k, (texts, s, h) in enumerate(((t0, s0, h0), (t1, s1, h1))):
        text_ups(texts, up, ups, k * rows)
        w0[...] = gate(mm_nt(texts[...], both0[:, :width]), consts)
        w1[...] = gate(mm_nt(texts[...], both1[:, :width]), consts)
        sums = mm(w0[...], both0[...]) + mm(w1[...], both1[...])
        s[...], h[...] = sums[:, :width], sums[:, width:]
        mine = ups[:, k * rows : (k + 1) * rows]
        sums0, sums1 = sums0 + mm(mine, w0[...]), sums1 + mm(mine, w1[...])
    grad[...] = down_share(sums0, own[...]) + down_share(sums1[:, :rows], a[...]) + down_share(sums1[:, rows:], b[...])


def last_kernel(consts, fa, fb, t0, t1, t2, t3, ups0, ups1, proj, down, up, h0, h1, h2, h3, grad, parts, both, w):
    half, rows, width, rank = fa.shape[0], t0.shape[0], proj.shape[1], down.shape[1]
    embed(fa, 0, both, proj, down, up)
    embed(fb, half, both, proj, down, up)
    inner, grad_up = None, None
    for k, (texts, h) in enumerate(((t0, h0), (t1, h1), (t2, h2), (t3, h3))):
        here = slice(k * rows, (k + 1) * rows)
        w[here] = gate(mm_nt(texts[...], both[:, :width]), consts)
        hidden = h[...] + mm(w[here], both[:, width:])
        high, low = halves(hidden[:, :rank])
        share = mm_tn(jnp.concatenate([high, low], axis=1), texts[...])
        ups = ups0 if k < 2 else ups1
        part = mm(ups[:, (k % 2) * rows : (k % 2 + 1) * rows], w[here])
        inner = part if inner is None else inner + part
        grad_up = share if grad_up is None else grad_up + share
    parts[:rank] = grad[...] + down_share(inner[:, :half], fa[...]) + down_share(inner[:, half:], fb[...])
    parts[rank:] = grad_up[:rank] + grad_up[rank:]


def add_kernel(first, w, both, s0, s1, o0, o1):
    rows, width = s0.shape
    for k, (s, o) in enumerate(((s0, o0), (s1, o1))):
        at = (first + k) * rows
        o[...] = s[...] + mm(w[at : at + rows], both[:, :width])


def run(kernel, name, operands, outs, scratch, flops, consts=True):
    spec = pl.BlockSpec(memory_space=pltpu.VMEM)
    ins = [spec] * len(operands)
    if consts:
        ins[0] = pl.BlockSpec(memory_space=pltpu.SMEM)
    size = sum(math.prod(o.shape) * o.dtype.itemsize for o in list(operands) + list(outs))
    return pl.pallas_call(
        kernel,
        in_specs=ins,
        out_specs=[spec] * len(outs),
        out_shape=outs,
        scratch_shapes=scratch,
        compiler_params=pltpu.CompilerParams(vmem_limit_bytes=30 * MIB),
        cost_estimate=pl.CostEstimate(flops=int(flops), bytes_accessed=size, transcendentals=0),
        name=name,
    )(*operands)


def scatter_sum(block, axis):
    n, here, part = 4, lax.axis_index(axis), block.shape[0] // 4
    piece = lambda d: lax.dynamic_slice_in_dim(block, ((here - d) % n) * part, part, 0)
    others = [from_ahead(piece(d), axis, d) for d in (1, 3, 2)]
    return piece(0) + others[0] + others[1] + others[2]


def gathered(block, axis):
    n, here, part = 4, lax.axis_index(axis), block.shape[0]
    whole = jnp.zeros((n * part,) + block.shape[1:], block.dtype)
    others = [(0, block)] + [(d, from_ahead(block, axis, d)) for d in (1, 3, 2)]
    for d, other in others:
        whole = lax.dynamic_update_slice_in_dim(whole, other, ((here + d) % n) * part, 0)
    return whole


def everyones(block, axis):
    return block + from_ahead(block, axis, 1) + from_ahead(block, axis, 3) + from_ahead(block, axis, 2)


def shards(images, texts, proj, down, up, scale, offset):
    own, texts = images[0], texts[0]
    rows, width = texts.shape
    rank = down.shape[1]
    half, wide = rows // 2, width + 128
    factor = scale[0] / math.sqrt(width)
    consts = jnp.stack([-factor * LOG2E, -offset[0] * LOG2E, factor])
    core = lax.axis_index("c")

    twin = from_ahead(texts, "c", 1)
    ahead = from_ahead(own, "z", 1)
    behind = from_ahead(own, "z", -1)
    across = from_ahead(texts, "y", 1)
    far_a = from_ahead(ahead[:half], "z", 1)
    far_b = from_ahead(behind[half:], "z", -1)
    across_twin = from_ahead(across, "c", 1)

    shape = jax.ShapeDtypeStruct
    sums, narrow = shape((rows, width), F32), shape((rows, 128), F32)
    unit = 2.0 * rows * rows * width
    pair_flops = 2.2 * unit

    both0, ups0, s0, s1, h0, h1, inner0 = run(
        own_kernel,
        "own_rows",
        [consts, own, texts, twin, proj, down, up],
        [shape((rows, wide), BF16), shape((2 * rank, 2 * rows), BF16), sums, sums, narrow, narrow, shape((2 * rank, rows), F32)],
        [pltpu.VMEM((rows, rows), BF16)],
        3.2 * unit + 2 * pair_flops,
    )
    both1, s0, s1, h0, h1, inner1 = run(
        side_kernel,
        "side_rows",
        [consts, ahead, behind, texts, twin, ups0, proj, down, up, s0, s1, h0, h1],
        [shape((2 * rows, wide), BF16), sums, sums, narrow, narrow, shape((2 * rank, 2 * rows), F32)],
        [pltpu.VMEM((rows, 2 * rows), BF16)],
        6.4 * unit + 4 * pair_flops,
    )
    ups1, s2, s3, h2, h3, grad = run(
        far_text_kernel,
        "far_texts",
        [consts, both0, both1, across, across_twin, up, inner0, inner1, own, ahead, behind],
        [shape((2 * rank, 2 * rows), BF16), sums, sums, narrow, narrow, shape((rank, width), F32)],
        [pltpu.VMEM((rows, rows), BF16), pltpu.VMEM((rows, 2 * rows), BF16)],
        6 * pair_flops,
    )
    parts, both2, weights = run(
        last_kernel,
        "far_rows",
        [consts, far_a, far_b, texts, twin, across, across_twin, ups0, ups1, proj, down, up, h0, h1, h2, h3, grad],
        [shape((2 * rank, width), F32), shape((rows, wide), BF16), shape((4 * rows, rows), BF16)],
        [],
        3.2 * unit + 5 * unit,
    )

    kept = lax.dynamic_slice_in_dim(parts, core * rank, rank, 0)
    kept = kept + from_ahead(lax.dynamic_slice_in_dim(parts, (1 - core) * rank, rank, 0), "c", 1)
    kept = scatter_sum(kept, "z")
    kept = everyones(kept, "x")
    kept = everyones(kept, ("y", "h"))
    kept = gathered(kept, "z") / (rows * 16)
    other = from_ahead(kept, "c", 1)
    first = core == 0
    grad_down = jnp.where(first, kept, other).T
    grad_up = jnp.where(first, other, kept)

    s2, s3 = run(
        lambda *refs: add_kernel(2, *refs), "far_sums", [weights, both2, s2, s3], [sums, sums], [], 2 * unit, False
    )
    s0, s1 = run(
        lambda *refs: add_kernel(0, *refs), "near_sums", [weights, both2, s0, s1], [sums, sums], [], 2 * unit, False
    )
    away = s2 + from_ahead(s3, "c", 1)
    height = jnp.maximum(jnp.max(jnp.abs(away), axis=1, keepdims=True), 1e-30)
    packed = (away * (HEIGHT / height)).astype(F16)
    packed = from_ahead(packed, "y", 1)
    height = from_ahead(jnp.broadcast_to(height, (rows, 128)), "y", 1)[:, :1]
    text_grad = s0 + from_ahead(s1, "c", 1) + packed.astype(F32) * (height / HEIGHT)
    return text_grad[None], grad_down, grad_up


def solution(mesh):
    grid = Mesh(mesh.devices.reshape(4, 2, 2, 2, 4), AXES)
    blk, dp = ("z", "y", "c"), ("h", "x")
    placed = (P(dp, blk, None), P(dp, blk, None), P(), P(), P(), P(), P())
    return jax.shard_map(
        shards,
        mesh=grid,
        in_specs=placed,
        out_specs=(P(dp, blk, None), P(), P()),
        check_vma=False,
    )
```

time: 144 us -> 149 us (1.035)
  matrix products: 41.6 us -> 0 us
  Pallas kernels: 0 us -> 40.5 us
  waiting for transfers between devices: 45.8 us -> 52.4 us
  starting transfers between devices: 33 us -> 35 us
    dot_general x27 -> x0, matrix products: 41.6 us -> none  [the longest x15 20.5 us: mm(): return jnp.dot(a, b, preferred_element_type=F32)]
    pallas_call x0 -> x6, Pallas kernels: none -> 40.5 us  [run(): pl.pallas_call(kernel, in_specs=ins, out_specs=[spec] * len(outs), out_sh...]
    ppermute x25, waiting for transfers between devices: 45.8 us -> 52.4 us  [from_ahead(): lax.ppermute(block, axis, [((i + distance) % n, i) for i in range(n)])]
    unnamed x23 -> x35, local copies, waits for them, and re-layouts: 7.3 us -> 11.3 us
    slice x3 -> x2, local copies, waits for them, and re-layouts: 3.46 us -> 0.07 us  [the longest x1 0.03 us: shards(): far_a = from_ahead(ahead[:half], 'z', 1)]
    convert_element_type x1, other arithmetic: 2.32 us -> 0.22 us  [shards(): packed = (away * (HEIGHT / height)).astype(F16)]
    ppermute x25, starting transfers between devices: 33 us -> 35 us  [from_ahead(): lax.ppermute(block, axis, [((i + distance) % n, i) for i in range(n)])]
  transfers between devices with their start and end apart: 25 -> 25, of which waited for: 7 -> 7; matrix products, arithmetic and copies ran while one was open for 20% -> 3% of each run, Pallas kernels for 0% -> 21%
where the time goes in v2:
time: 149 us
  waiting for transfers between devices  52.4 us (35%)
  Pallas kernels  40.5 us (27%)
  starting transfers between devices  35 us (23%)
  local copies, waits for them, and re-layouts  11.5 us (8%)
  other arithmetic  7.28 us (5%)
  between operations  2.25 us (2%)
    ppermute x25, waiting for transfers between devices, from_ahead(): lax.ppermute(block, axis, [((i + distance) % n, i) for i in range(n)])  52.4 us
    pallas_call x6, Pallas kernels, run(): pl.pallas_call(kernel, in_specs=ins, out_specs=[spec] * len(outs), out_sh...  40.5 us
    ppermute x25, starting transfers between devices, from_ahead(): lax.ppermute(block, axis, [((i + distance) % n, i) for i in range(n)])  35 us
    unnamed x35, local copies, waits for them, and re-layouts  11.3 us
    broadcast_in_dim x1, other arithmetic, shards(): return (text_grad[None], grad_down, grad_up)  3.26 us
  transfers between devices with their start and end apart: 25, of which 7 were waited for; matrix products, arithmetic and copies ran while one was open for 3% of the time, Pallas kernels for 21%

profile of v2, /device:TPU:1, one launch (start us, length us, event | category | flops | bytes accessed | tf_op | source)
XLA Modules:
  0.0 148.9 jit_solution(896453270250423578)
XLA Ops:
  0.7 2.2 %collective-permute-start.5 = (bf16[384,1152]{1,0:T(8,128)(2,1)}, bf16[384,1152]{1,0:T(8,128)(2,1)}, u32[]{:S(2)}, u32[]{:S(2)}) collective-permute-start(bf16[384,1152]{1,0:T(8,128)(2,1)} %bitcast.10), channel_id=1, source_target_pairs={{16,0},{0,16},{17,1},{1,17},{18,2},{2,18},{19,3},{3,19},{20,4},{4,... | collective-permute-start | bytes 2654216 | tf_op jit(solution)/shard_map/ppermute | solution.py:19
  2.9 3.8 %collective-permute-start = (bf16[384,1152]{1,0:T(8,128)(2,1)}, bf16[384,1152]{1,0:T(8,128)(2,1)S(1)}, u32[]{:S(2)}, u32[]{:S(2)}) collective-permute-start(bf16[384,1152]{1,0:T(8,128)(2,1)} %bitcast.6), channel_id=1, source_target_pairs={{32,0},{64,32},{96,64},{0,96},{33,1},{65,33},{97,65},{1,97},{34,2}... | collective-permute-start | bytes 2654216 | tf_op jit(solution)/shard_map/ppermute | solution.py:19
  7.9 14.3 %collective-permute-done.5.t0.t2 = bf16[384,1152]{1,0:T(8,128)(2,1)} collective-permute-done((bf16[384,1152]{1,0:T(8,128)(2,1)}, bf16[384,1152]{1,0:T(8,128)(2,1)}, u32[]{:S(2)}, u32[]{:S(2)}) %collective-permute-start.5) | collective-permute-done | bytes 884768 | tf_op jit(solution)/shard_map/ppermute | solution.py:19
  26.3 4.0 %collective-permute-start.1 = (bf16[192,1152]{1,0:T(8,128)(2,1)S(1)}, bf16[192,1152]{1,0:T(8,128)(2,1)S(1)}, u32[]{:S(2)}, u32[]{:S(2)}) collective-permute-start(bf16[192,1152]{1,0:T(8,128)(2,1)S(1)} %slice.12), channel_id=1, source_target_pairs={{32,0},{64,32},{96,64},{0,96},{33,1},{65,33},{97,65},{1,97},{34,2}... | collective-permute-start | bytes 1327112 | tf_op jit(solution)/shard_map/ppermute | solution.py:19
  30.7 1.7 %copy-done.12 = bf16[1152,1152]{1,0:T(8,128)(2,1)S(1)} copy-done((bf16[1152,1152]{1,0:T(8,128)(2,1)S(1)}, bf16[1152,1152]{1,0:T(8,128)(2,1)}, u32[]{:S(2)}) %copy-start.12) | copy-done | bytes 2654232
  32.4 7.3 %own_rows.1 = (bf16[384,1280]{1,0:T(8,128)(2,1)S(1)}, bf16[128,768]{1,0:T(8,128)(2,1)S(1)}, f32[384,1152]{1,0:T(8,128)S(1)}, f32[384,1152]{1,0:T(8,128)S(1)}, f3...) custom-call(f32[3]{0:T(128)S(1)} %pad_maximum_fusion.consts, bf16[384,1152]{1,0:T(8,128)(2,1)S(1)} %bitcast.8, ...), custom_call_target="tpu_custom_call" | custom-call | flops 2582013440 | bytes 10911756 | tf_op jit(solution)/shard_map/own_rows/pallas_call | solution.py:145
  39.7 9.0 %side_rows.1 = (bf16[768,1280]{1,0:T(8,128)(2,1)S(1)}, f32[384,1152]{1,0:T(8,128)S(1)}, f32[384,1152]{1,0:T(8,128)S(1)}, f32[384,128]{1,0:T(8,128)S(1)}, f32[384,128]{1,0:T(8,128)S(1)}, /*index=5*/f32[128,768]{1,0:T(8,128)S(1)}) custom-call(f32[3]{0:T(128)S(1)} %pad_maximum_fusion.consts, bf16[384,1152]{1,0:T(8,128)(2,1)S(1)} %collective-permute-done.a, ...), custom_call_target="tpu_custom_call" | custom-call | flops 5164026880 | bytes 16908300 | tf_op jit(solution)/shard_map/side_rows/pallas_call | solution.py:145
  48.7 10.3 %far_texts.1 = (bf16[128,768]{1,0:T(8,128)(2,1)S(1)}, f32[384,1152]{1,0:T(8,128)S(1)}, f32[384,1152]{1,0:T(8,128)S(1)}, f32[384,128]{1,0:T(8,128)S(1)}, f32[384,128]{1,0:T(8,128)S(1)}, /*index=5*/f32[64,1152]{1,0:T(8,128)S(1)}) custom-call(f32[3]{0:T(128)S(1)} %pad_maximum_fusion.consts, bf16[384,1280]{1,0:T(8,128)(2,1)S(1)} %get-tuple-element.30.both0, ...), custom_call_target="tpu_custom_call" | custom-call | flops 4484549632 | bytes 12533772 | tf_op jit(solution)/shard_map/far_texts/pallas_call | solution.py:145
  60.3 9.2 %far_rows.1 = (f32[128,1152]{1,0:T(8,128)S(1)}, bf16[384,1280]{1,0:T(8,128)(2,1)S(1)}, bf16[1536,384]{1,0:T(8,128)(2,1)S(1)}) custom-call(f32[3]{0:T(128)S(1)} %pad_maximum_fusion.consts, bf16[192,1152]{1,0:T(8,128)(2,1)S(1)} %collective-permute-done.1.fa, bf16[192,1152]{1,0:T(8,128)(2,1)S(1)} %collective-permute-done.3.fb, bf16[384,1152]{1,0:T(8,128)(2,1)S(1)} %bitcast.14, ...), custom_call_target="tpu_custom_call" | custom-call | flops 2785856768 | bytes 11599884 | tf_op jit(solution)/shard_map/far_rows/pallas_call | solution.py:145
  71.3 2.9 %collective-permute-start.12 = (f32[16,1152]{1,0:T(8,128)S(1)}, f32[16,1152]{1,0:T(8,128)S(1)}, u32[]{:S(2)}, u32[]{:S(2)}) collective-permute-start(f32[16,1152]{1,0:T(8,128)S(1)} %get-tuple-element.61), channel_id=1, source_target_pairs={{32,0},{64,32},{96,64},{0,96},{33,1},{65,33},{97,65},{1,97},{34,2}... | collective-permute-start | bytes 221192 | tf_op jit(solution)/shard_map/ppermute | solution.py:19
  75.6 5.3 %collective-permute-done.13 = f32[16,1152]{1,0:T(8,128)S(1)} collective-permute-done((f32[16,1152]{1,0:T(8,128)S(1)}, f32[16,1152]{1,0:T(8,128)S(1)}, u32[]{:S(2)}, u32[]{:S(2)}) %collective-permute-start.13) | collective-permute-done | bytes 73760 | tf_op jit(solution)/shard_map/ppermute | solution.py:19
  80.9 2.5 %collective-permute-start.15 = (f32[16,1152]{1,0:T(8,128)S(1)}, f32[16,1152]{1,0:T(8,128)S(1)}, u32[]{:S(2)}, u32[]{:S(2)}) collective-permute-start(f32[16,1152]{1,0:T(8,128)S(1)} %add_add_fusion.2), channel_id=1, source_target_pairs={{1,0},{2,1},{3,2},{0,3},{5,4},{6,5},{7,6},{4,7},{9,8},{10,9},{11,1... | collective-permute-start | bytes 221192 | tf_op jit(solution)/shard_map/ppermute | solution.py:19
  83.4 1.7 %collective-permute-start.17 = (f32[16,1152]{1,0:T(8,128)S(1)}, f32[16,1152]{1,0:T(8,128)S(1)}, u32[]{:S(2)}, u32[]{:S(2)}) collective-permute-start(f32[16,1152]{1,0:T(8,128)S(1)} %add_add_fusion.2), channel_id=1, source_target_pairs={{2,0},{3,1},{0,2},{1,3},{6,4},{7,5},{4,6},{5,7},{10,8},{11,9},{8,1... | collective-permute-start | bytes 221192 | tf_op jit(solution)/shard_map/ppermute | solution.py:19
  85.2 3.5 %collective-permute-done.16 = f32[16,1152]{1,0:T(8,128)S(1)} collective-permute-done((f32[16,1152]{1,0:T(8,128)S(1)}, f32[16,1152]{1,0:T(8,128)S(1)}, u32[]{:S(2)}, u32[]{:S(2)}) %collective-permute-start.16) | collective-permute-done | bytes 73760 | tf_op jit(solution)/shard_map/ppermute | solution.py:19
  88.7 2.8 %collective-permute-start.18 = (f32[16,1152]{1,0:T(8,128)S(1)}, f32[16,1152]{1,0:T(8,128)S(1)}, u32[]{:S(2)}, u32[]{:S(2)}) collective-permute-start(f32[16,1152]{1,0:T(8,128)S(1)} %add_add_fusion.1), channel_id=1, source_target_pairs={{4,0},{16,4},{20,16},{0,20},{5,1},{17,5},{21,17},{1,21},{6,2},{18,... | collective-permute-start | bytes 221192 | tf_op jit(solution)/shard_map/ppermute | solution.py:19
  95.9 2.3 %far_sums.1 = (f32[384,1152]{1,0:T(8,128)S(1)}, f32[384,1152]{1,0:T(8,128)}) custom-call(bf16[1536,384]{1,0:T(8,128)(2,1)S(1)} %get-tuple-element.44.refs_0_, bf16[384,1280]{1,0:T(8,128)(2,1)S(1)} %get-tuple-element.45.refs_1_, f32[384,1152]{1,0:T(8,128)S(1)} %copy-done.5, f32[384,1152]{1,0:T(8,128)S(1)} %copy-done.7), custom_call_target="tpu_custom_call" | custom-call | flops 679477248 | bytes 9240576 | tf_op jit(solution)/shard_map/far_sums/pallas_call | solution.py:145
  99.6 3.1 %collective-permute-start.8 = (f32[384,1152]{1,0:T(8,128)}, f32[384,1152]{1,0:T(8,128)}, u32[]{:S(2)}, u32[]{:S(2)}) collective-permute-start(f32[384,1152]{1,0:T(8,128)} %get-tuple-element.53), channel_id=1, source_target_pairs={{8,0},{0,8},{9,1},{1,9},{10,2},{2,10},{11,3},{3,11},{12,4},{4,12},... | collective-permute-start | bytes 5308424 | tf_op jit(solution)/shard_map/ppermute | solution.py:19
  102.7 2.0 %collective-permute-start.21 = (f32[16,1152]{1,0:T(8,128)S(1)}, f32[16,1152]{1,0:T(8,128)S(1)}, u32[]{:S(2)}, u32[]{:S(2)}) collective-permute-start(f32[16,1152]{1,0:T(8,128)S(1)} %get-tuple-element.56), channel_id=1, source_target_pairs={{32,0},{64,32},{96,64},{0,96},{33,1},{65,33},{97,65},{1,97},{34,2}... | collective-permute-start | bytes 221192 | tf_op jit(solution)/shard_map/ppermute | solution.py:19
  107.7 2.4 %near_sums.1 = (f32[384,1152]{1,0:T(8,128)S(1)}, f32[384,1152]{1,0:T(8,128)}) custom-call(bf16[1536,384]{1,0:T(8,128)(2,1)S(1)} %get-tuple-element.44.refs_0_, bf16[384,1280]{1,0:T(8,128)(2,1)S(1)} %get-tuple-element.45.refs_1_, f32[384,1152]{1,0:T(8,128)S(1)} %copy-done.1, f32[384,1152]{1,0:T(8,128)S(1)} %copy-done.3), custom_call_target="tpu_custom_call" | custom-call | flops 679477248 | bytes 9240576 | tf_op jit(solution)/shard_map/near_sums/pallas_call | solution.py:145
  111.4 5.8 %collective-permute-done.22 = f32[16,1152]{1,0:T(8,128)S(1)} collective-permute-done((f32[16,1152]{1,0:T(8,128)S(1)}, f32[16,1152]{1,0:T(8,128)S(1)}, u32[]{:S(2)}, u32[]{:S(2)}) %collective-permute-start.22) | collective-permute-done | bytes 73760 | tf_op jit(solution)/shard_map/ppermute | solution.py:19
  118.0 1.8 %abs_reduce_fusion = (f32[384]{0:T(512)S(1)}, f32[384,1152]{1,0:T(8,128)S(1)}) fusion(f32[384,1152]{1,0:T(8,128)S(1)} %copy-done.9, f32[384,1152]{1,0:T(8,128)} %collective-permute-done.8), kind=kLoop, calls=%fused_computation.2 | loop fusion | flops 1326720 | bytes 5309952 | tf_op jit(solution)/shard_map/reduce_max | solution.py:250
  121.7 1.8 %broadcast_select_fusion = (f32[64,1152]{1,0:T(8,128)}, f32[1152,64]{0,1:T(8,128)}) fusion(f32[64,1152]{1,0:T(8,128)} %collective-permute-done.24, pred[]{:T(512)S(6)} %eq.12, f32[64,1152]{1,0:T(8,128)S(1)} %constant_dynamic-update-slice_fusion), kind=kLoop, calls=%fused_computation.6 | loop fusion | flops 221184 | bytes 1179649 | tf_op jit(solution)/shard_map/jit(_where)/select_n | solution.py:241
  123.5 22.1 %collective-permute-done.10 = f32[384,128]{0,1:T(8,128)S(1)} collective-permute-done((f32[384,128]{0,1:T(8,128)S(1)}, f32[384,128]{0,1:T(8,128)S(1)}, u32[]{:S(2)}, u32[]{:S(2)}) %collective-permute-start.10) | collective-permute-done | bytes 196640 | tf_op jit(solution)/shard_map/ppermute | solution.py:19
  145.6 3.3 %add_bitcast_fusion = f32[1,384,1152]{2,1,0:T(8,128)} fusion(f16[384,1152]{1,0:T(8,128)(2,1)} %collective-permute-done.9, f32[384,1152]{1,0:T(8,128)S(1)} %copy-done.11, f32[384,1152]{1,0:T(8,128)} %collective-permute-done.7, f32[384]{0:T(512)S(1)} %fusion), kind=kLoop, calls=%fused_computation | loop fusion | flops 1769472 | bytes 6194688 | tf_op jit(solution)/shard_map/broadcast_in_dim | solution.py:255
  (88 shorter events, 21.7 us)
Async XLA Ops:
  0.7 21.5 %collective-permute-start.5 = (bf16[384,1152]{1,0:T(8,128)(2,1)}, bf16[384,1152]{1,0:T(8,128)(2,1)}, u32[]{:S(2)}, u32[]{:S(2)}) collective-permute-start(bf16[384,1152]{1,0:T(8,128)(2,1)} %bitcast.10), channel_id=1, source_target_pairs={{16,0},{0,16},{17,1},{1,17},{18,2},{2,18},{19,3},{3,19},{20,4},{4,... | collective-permute-start | bytes 2654216 | tf_op jit(solution)/shard_map/ppermute | solution.py:19
  2.9 23.4 %collective-permute-start = (bf16[384,1152]{1,0:T(8,128)(2,1)}, bf16[384,1152]{1,0:T(8,128)(2,1)S(1)}, u32[]{:S(2)}, u32[]{:S(2)}) collective-permute-start(bf16[384,1152]{1,0:T(8,128)(2,1)} %bitcast.6), channel_id=1, source_target_pairs={{32,0},{64,32},{96,64},{0,96},{33,1},{65,33},{97,65},{1,97},{34,2}... | collective-permute-start | bytes 2654216 | tf_op jit(solution)/shard_map/ppermute | solution.py:19
  6.6 23.7 %collective-permute-start.2 = (bf16[384,1152]{1,0:T(8,128)(2,1)}, bf16[384,1152]{1,0:T(8,128)(2,1)S(1)}, u32[]{:S(2)}, u32[]{:S(2)}) collective-permute-start(bf16[384,1152]{1,0:T(8,128)(2,1)} %bitcast.7), channel_id=1, source_target_pairs={{96,0},{0,32},{32,64},{64,96},{97,1},{1,33},{33,65},{65,97},{98,2}... | collective-permute-start | bytes 2654216 | tf_op jit(solution)/shard_map/ppermute | solution.py:19
  6.6 24.0 %collective-permute-start.4 = (bf16[384,1152]{1,0:T(8,128)(2,1)}, bf16[384,1152]{1,0:T(8,128)(2,1)}, u32[]{:S(2)}, u32[]{:S(2)}) collective-permute-start(bf16[384,1152]{1,0:T(8,128)(2,1)} %bitcast.11), channel_id=1, source_target_pairs={{8,0},{0,8},{9,1},{1,9},{10,2},{2,10},{11,3},{3,11},{12,4},{4,12},... | collective-permute-start | bytes 2654216 | tf_op jit(solution)/shard_map/ppermute | solution.py:19
  22.1 26.6 %collective-permute-start.6 = (bf16[384,1152]{1,0:T(8,128)(2,1)}, bf16[384,1152]{1,0:T(8,128)(2,1)}, u32[]{:S(2)}, u32[]{:S(2)}) collective-permute-start(bf16[384,1152]{1,0:T(8,128)(2,1)} %collective-permute-done.5.t0.t2), channel_id=1, source_target_pairs={{8,0},{0,8},{9,1},{1,9},{10,2},{2,10},{11,3},{3,11},{12,4},{4,12},... | collective-permute-start | bytes 2654216 | tf_op jit(solution)/shard_map/ppermute | solution.py:19
  26.3 33.9 %collective-permute-start.1 = (bf16[192,1152]{1,0:T(8,128)(2,1)S(1)}, bf16[192,1152]{1,0:T(8,128)(2,1)S(1)}, u32[]{:S(2)}, u32[]{:S(2)}) collective-permute-start(bf16[192,1152]{1,0:T(8,128)(2,1)S(1)} %slice.12), channel_id=1, source_target_pairs={{32,0},{64,32},{96,64},{0,96},{33,1},{65,33},{97,65},{1,97},{34,2}... | collective-permute-start | bytes 1327112 | tf_op jit(solution)/shard_map/ppermute | solution.py:19
  30.4 29.9 %collective-permute-start.3 = (bf16[192,1152]{1,0:T(8,128)(2,1)S(1)}, bf16[192,1152]{1,0:T(8,128)(2,1)S(1)}, u32[]{:S(2)}, u32[]{:S(2)}) collective-permute-start(bf16[192,1152]{1,0:T(8,128)(2,1)S(1)} %slice.13), channel_id=1, source_target_pairs={{96,0},{0,32},{32,64},{64,96},{97,1},{1,33},{33,65},{65,97},{98,2}... | collective-permute-start | bytes 1327112 | tf_op jit(solution)/shard_map/ppermute | solution.py:19
  71.3 4.3 %collective-permute-start.12 = (f32[16,1152]{1,0:T(8,128)S(1)}, f32[16,1152]{1,0:T(8,128)S(1)}, u32[]{:S(2)}, u32[]{:S(2)}) collective-permute-start(f32[16,1152]{1,0:T(8,128)S(1)} %get-tuple-element.61), channel_id=1, source_target_pairs={{32,0},{64,32},{96,64},{0,96},{33,1},{65,33},{97,65},{1,97},{34,2}... | collective-permute-start | bytes 221192 | tf_op jit(solution)/shard_map/ppermute | solution.py:19
  74.2 6.7 %collective-permute-start.13 = (f32[16,1152]{1,0:T(8,128)S(1)}, f32[16,1152]{1,0:T(8,128)S(1)}, u32[]{:S(2)}, u32[]{:S(2)}) collective-permute-start(f32[16,1152]{1,0:T(8,128)S(1)} %get-tuple-element.63), channel_id=1, source_target_pairs={{96,0},{0,32},{32,64},{64,96},{97,1},{1,33},{33,65},{65,97},{98,2}... | collective-permute-start | bytes 221192 | tf_op jit(solution)/shard_map/ppermute | solution.py:19
  74.2 6.7 %collective-permute-start.14 = (f32[16,1152]{1,0:T(8,128)S(1)}, f32[16,1152]{1,0:T(8,128)S(1)}, u32[]{:S(2)}, u32[]{:S(2)}) collective-permute-start(f32[16,1152]{1,0:T(8,128)S(1)} %get-tuple-element.62), channel_id=1, source_target_pairs={{64,0},{96,32},{0,64},{32,96},{65,1},{97,33},{1,65},{33,97},{66,2}... | collective-permute-start | bytes 221192 | tf_op jit(solution)/shard_map/ppermute | solution.py:19
  80.9 4.3 %collective-permute-start.15 = (f32[16,1152]{1,0:T(8,128)S(1)}, f32[16,1152]{1,0:T(8,128)S(1)}, u32[]{:S(2)}, u32[]{:S(2)}) collective-permute-start(f32[16,1152]{1,0:T(8,128)S(1)} %add_add_fusion.2), channel_id=1, source_target_pairs={{1,0},{2,1},{3,2},{0,3},{5,4},{6,5},{7,6},{4,7},{9,8},{10,9},{11,1... | collective-permute-start | bytes 221192 | tf_op jit(solution)/shard_map/ppermute | solution.py:19
  83.4 5.2 %collective-permute-start.16 = (f32[16,1152]{1,0:T(8,128)S(1)}, f32[16,1152]{1,0:T(8,128)S(1)}, u32[]{:S(2)}, u32[]{:S(2)}) collective-permute-start(f32[16,1152]{1,0:T(8,128)S(1)} %add_add_fusion.2), channel_id=1, source_target_pairs={{3,0},{0,1},{1,2},{2,3},{7,4},{4,5},{5,6},{6,7},{11,8},{8,9},{9,10... | collective-permute-start | bytes 221192 | tf_op jit(solution)/shard_map/ppermute | solution.py:19
  83.4 5.2 %collective-permute-start.17 = (f32[16,1152]{1,0:T(8,128)S(1)}, f32[16,1152]{1,0:T(8,128)S(1)}, u32[]{:S(2)}, u32[]{:S(2)}) collective-permute-start(f32[16,1152]{1,0:T(8,128)S(1)} %add_add_fusion.2), channel_id=1, source_target_pairs={{2,0},{3,1},{0,2},{1,3},{6,4},{7,5},{4,6},{5,7},{10,8},{11,9},{8,1... | collective-permute-start | bytes 221192 | tf_op jit(solution)/shard_map/ppermute | solution.py:19
  88.7 14.0 %collective-permute-start.18 = (f32[16,1152]{1,0:T(8,128)S(1)}, f32[16,1152]{1,0:T(8,128)S(1)}, u32[]{:S(2)}, u32[]{:S(2)}) collective-permute-start(f32[16,1152]{1,0:T(8,128)S(1)} %add_add_fusion.1), channel_id=1, source_target_pairs={{4,0},{16,4},{20,16},{0,20},{5,1},{17,5},{21,17},{1,21},{6,2},{18,... | collective-permute-start | bytes 221192 | tf_op jit(solution)/shard_map/ppermute | solution.py:19
  91.5 11.2 %collective-permute-start.19 = (f32[16,1152]{1,0:T(8,128)S(1)}, f32[16,1152]{1,0:T(8,128)S(1)}, u32[]{:S(2)}, u32[]{:S(2)}) collective-permute-start(f32[16,1152]{1,0:T(8,128)S(1)} %add_add_fusion.1), channel_id=1, source_target_pairs={{20,0},{0,4},{4,16},{16,20},{21,1},{1,5},{5,17},{17,21},{22,2},{2,... | collective-permute-start | bytes 221192 | tf_op jit(solution)/shard_map/ppermute | solution.py:19
  91.7 11.0 %collective-permute-start.20 = (f32[16,1152]{1,0:T(8,128)S(1)}, f32[16,1152]{1,0:T(8,128)S(1)}, u32[]{:S(2)}, u32[]{:S(2)}) collective-permute-start(f32[16,1152]{1,0:T(8,128)S(1)} %add_add_fusion.1), channel_id=1, source_target_pairs={{16,0},{20,4},{0,16},{4,20},{17,1},{21,5},{1,17},{5,21},{18,2},{22... | collective-permute-start | bytes 221192 | tf_op jit(solution)/shard_map/ppermute | solution.py:19
  99.6 18.5 %collective-permute-start.8 = (f32[384,1152]{1,0:T(8,128)}, f32[384,1152]{1,0:T(8,128)}, u32[]{:S(2)}, u32[]{:S(2)}) collective-permute-start(f32[384,1152]{1,0:T(8,128)} %get-tuple-element.53), channel_id=1, source_target_pairs={{8,0},{0,8},{9,1},{1,9},{10,2},{2,10},{11,3},{3,11},{12,4},{4,12},... | collective-permute-start | bytes 5308424 | tf_op jit(solution)/shard_map/ppermute | solution.py:19
  102.7 8.6 %collective-permute-start.21 = (f32[16,1152]{1,0:T(8,128)S(1)}, f32[16,1152]{1,0:T(8,128)S(1)}, u32[]{:S(2)}, u32[]{:S(2)}) collective-permute-start(f32[16,1152]{1,0:T(8,128)S(1)} %get-tuple-element.56), channel_id=1, source_target_pairs={{32,0},{64,32},{96,64},{0,96},{33,1},{65,33},{97,65},{1,97},{34,2}... | collective-permute-start | bytes 221192 | tf_op jit(solution)/shard_map/ppermute | solution.py:19
  110.1 35.5 %collective-permute-start.7 = (f32[384,1152]{1,0:T(8,128)}, f32[384,1152]{1,0:T(8,128)}, u32[]{:S(2)}, u32[]{:S(2)}) collective-permute-start(f32[384,1152]{1,0:T(8,128)} %get-tuple-element.49), channel_id=1, source_target_pairs={{8,0},{0,8},{9,1},{1,9},{10,2},{2,10},{11,3},{3,11},{12,4},{4,12},... | collective-permute-start | bytes 5308424 | tf_op jit(solution)/shard_map/ppermute | solution.py:19
  110.4 6.7 %collective-permute-start.22 = (f32[16,1152]{1,0:T(8,128)S(1)}, f32[16,1152]{1,0:T(8,128)S(1)}, u32[]{:S(2)}, u32[]{:S(2)}) collective-permute-start(f32[16,1152]{1,0:T(8,128)S(1)} %get-tuple-element.56), channel_id=1, source_target_pairs={{96,0},{0,32},{32,64},{64,96},{97,1},{1,33},{33,65},{65,97},{98,2}... | collective-permute-start | bytes 221192 | tf_op jit(solution)/shard_map/ppermute | solution.py:19
  110.4 6.7 %collective-permute-start.23 = (f32[16,1152]{1,0:T(8,128)S(1)}, f32[16,1152]{1,0:T(8,128)S(1)}, u32[]{:S(2)}, u32[]{:S(2)}) collective-permute-start(f32[16,1152]{1,0:T(8,128)S(1)} %get-tuple-element.56), channel_id=1, source_target_pairs={{64,0},{96,32},{0,64},{32,96},{65,1},{97,33},{1,65},{33,97},{66,2}... | collective-permute-start | bytes 221192 | tf_op jit(solution)/shard_map/ppermute | solution.py:19
  117.2 4.5 %collective-permute-start.24 = (f32[64,1152]{1,0:T(8,128)S(1)}, f32[64,1152]{1,0:T(8,128)}, u32[]{:S(2)}, u32[]{:S(2)}) collective-permute-start(f32[64,1152]{1,0:T(8,128)S(1)} %broadcast_multiply_fusion), channel_id=1, source_target_pairs={{8,0},{0,8},{9,1},{1,9},{10,2},{2,10},{11,3},{3,11},{12,4},{4,12},... | collective-permute-start | bytes 884744 | tf_op jit(solution)/shard_map/ppermute | solution.py:19
  120.0 25.6 %collective-permute-start.9 = (f16[384,1152]{1,0:T(8,128)(2,1)S(1)}, f16[384,1152]{1,0:T(8,128)(2,1)}, u32[]{:S(2)}, u32[]{:S(2)}) collective-permute-start(f16[384,1152]{1,0:T(8,128)(2,1)S(1)} %multiply_convert_fusion), channel_id=1, source_target_pairs={{16,0},{0,16},{17,1},{1,17},{18,2},{2,18},{19,3},{3,19},{20,4},{4,... | collective-permute-start | bytes 2654216 | tf_op jit(solution)/shard_map/ppermute | solution.py:19
  120.3 25.3 %collective-permute-start.10 = (f32[384,128]{0,1:T(8,128)S(1)}, f32[384,128]{0,1:T(8,128)S(1)}, u32[]{:S(2)}, u32[]{:S(2)}) collective-permute-start(f32[384,128]{0,1:T(8,128)S(1)} %broadcast_in_dim.12), channel_id=1, source_target_pairs={{16,0},{0,16},{17,1},{1,17},{18,2},{2,18},{19,3},{3,19},{20,4},{4,... | collective-permute-start | bytes 589832 | tf_op jit(solution)/shard_map/ppermute | solution.py:19
  (18 other events, 159.3 us)

commit v3 on v2

v3 whole, which is shorter than its diff:
```python
import functools
import math

import jax
import jax.numpy as jnp
from jax import lax
from jax.experimental import pallas as pl
from jax.experimental.pallas import tpu as pltpu
from jax.sharding import Mesh, PartitionSpec as P

F32, BF16, F16 = jnp.float32, jnp.bfloat16, jnp.float16
AXES = ("z", "y", "c", "h", "x")
LOG2E = 1.4426950408889634
REACH = 14.0
MIB = 1 << 20


def tied(*values):
    return lax.optimization_barrier(values)


def from_ahead(block, axis, distance):
    n = lax.axis_size(axis)
    return lax.ppermute(block, axis, [((i + distance) % n, i) for i in range(n)])


def mm(a, b):
    return jnp.dot(a, b, preferred_element_type=F32)


def mm_nt(a, b):
    return lax.dot_general(a, b, (((1,), (1,)), ((), ())), preferred_element_type=F32)


def mm_tn(a, b):
    return lax.dot_general(a, b, (((0,), (0,)), ((), ())), preferred_element_type=F32)


def halves(a):
    high = a.astype(BF16)
    return high, (a - high.astype(F32)).astype(BF16)


def embed(images, at, both, proj, down, up):
    here = slice(at, at + images.shape[0])
    width, rank = proj.shape[1], down.shape[0]
    hidden = mm_nt(images[...], down[...]).astype(BF16)
    both[here, :width] = (mm(images[...], proj[...]) + mm(hidden, up[...])).astype(BF16)
    both[here, width : width + rank] = hidden
    both[here, width + rank :] = jnp.zeros((images.shape[0], both.shape[1] - width - rank), BF16)


def gate(sims, consts):
    power = jnp.minimum(sims * consts[0] + consts[1], 126.0)
    return (consts[2] / (1.0 + jnp.exp2(power))).astype(BF16)


def gate_matching(sims, consts):
    power = sims * consts[0] + consts[1]
    other = consts[2] / (1.0 + jnp.exp2(jnp.minimum(power, 126.0)))
    match = -consts[2] / (1.0 + jnp.exp2(jnp.minimum(-power, 126.0)))
    row = lax.broadcasted_iota(jnp.int32, sims.shape, 0)
    col = lax.broadcasted_iota(jnp.int32, sims.shape, 1)
    return jnp.where(row == col, match, other).astype(BF16)


def text_ups(texts, up, out, at):
    high, low = halves(mm_nt(up[...], texts[...]))
    out[:, at : at + texts.shape[0]] = jnp.concatenate([high, low])


def down_share(inner, images):
    rank = inner.shape[0] // 2
    pair = jnp.concatenate(halves(inner[:rank] + inner[rank:]))
    grad = mm(pair, images)
    return grad[:rank] + grad[rank:]


def up_share(hidden, texts, rank):
    pair = jnp.concatenate(halves(hidden[:, :rank]), axis=1)
    grad = mm_tn(pair, texts)
    return grad[:rank] + grad[rank:]


def own_kernel(consts, own, t0, t1, proj, down, up, both, ups, s0, s1, h0, h1, inner, w):
    width, rows = proj.shape[1], own.shape[0]
    embed(own, 0, both, proj, down, up)
    for k, (texts, s, h) in enumerate(((t0, s0, h0), (t1, s1, h1))):
        text_ups(texts, up, ups, k * rows)
        sims = mm_nt(texts[...], both[:, :width])
        w[...] = gate(sims, consts) if k else gate_matching(sims, consts)
        sums = mm(w[...], both[...])
        s[...], h[...] = sums[:, :width], sums[:, width:]
        part = mm(ups[:, k * rows : (k + 1) * rows], w[...])
        inner[...] = inner[...] + part if k else part


def side_kernel(consts, a, b, t0, t1, ups, proj, down, up, s0, s1, h0, h1, both, o0, o1, g0, g1, inner, w):
    width, rows = proj.shape[1], a.shape[0]
    embed(a, 0, both, proj, down, up)
    embed(b, rows, both, proj, down, up)
    for k, (texts, s, h, o, g) in enumerate(((t0, s0, h0, o0, g0), (t1, s1, h1, o1, g1))):
        w[...] = gate(mm_nt(texts[...], both[:, :width]), consts)
        sums = mm(w[...], both[...])
        o[...], g[...] = s[...] + sums[:, :width], h[...] + sums[:, width:]
        part = mm(ups[:, k * rows : (k + 1) * rows], w[...])
        inner[...] = inner[...] + part if k else part


def far_text_kernel(
    consts, both0, both1, t0, t1, up, inner0, inner1, own, a, b, near, h1, ups, s0, s1, h0, grad_down, grad_up, w0, w1
):
    rows, width = own.shape
    rank = up.shape[0]
    sums0, sums1 = inner0[...], inner1[...]
    for k, (texts, s) in enumerate(((t0, s0), (t1, s1))):
        text_ups(texts, up, ups, k * rows)
        w0[...] = gate(mm_nt(texts[...], both0[:, :width]), consts)
        w1[...] = gate(mm_nt(texts[...], both1[:, :width]), consts)
        sums = mm(w0[...], both0[...]) + mm(w1[...], both1[...])
        s[...] = sums[:, :width]
        if k == 0:
            h0[...] = sums[:, width:]
        else:
            grad_up[...] = up_share(sums[:, width:], texts[...], rank) + up_share(h1[...], near[...], rank)
        mine = ups[:, k * rows : (k + 1) * rows]
        sums0, sums1 = sums0 + mm(mine, w0[...]), sums1 + mm(mine, w1[...])
    grad_down[...] = (
        down_share(sums0, own[...]) + down_share(sums1[:, :rows], a[...]) + down_share(sums1[:, rows:], b[...])
    )


def last_kernel(
    consts, far, far_twin, t0, t1, ups0, ups1, proj, down, up, h0, h1, grad_down, grad_up, kept, sent, both, w0, w1
):
    rows, width, rank = t0.shape[0], proj.shape[1], up.shape[0]
    at, blocks = 0, (far, far_twin)
    for block in blocks:
        embed(block, at, both, proj, down, up)
        at += block.shape[0]
    inner, up_sum = None, grad_up[...]
    for texts, ups, h, w in ((t0, ups0, h0, w0), (t1, ups1, h1, w1)):
        w[...] = gate(mm_nt(texts[...], both[:, :width]), consts)
        up_sum = up_sum + up_share(h[...] + mm(w[...], both[:, width:]), texts[...], rank)
        part = mm(ups[:, :rows], w[...])
        inner = part if inner is None else inner + part
    down_sum, at = grad_down[...], 0
    for block in blocks:
        down_sum = down_sum + down_share(inner[:, at : at + block.shape[0]], block[...])
        at += block.shape[0]
    first = lax.axis_index("c") == 0
    kept[...] = jnp.where(first, down_sum, up_sum)
    sent[...] = jnp.where(first, up_sum, down_sum)


def near_kernel(w, both, s, twin, out):
    out[...] = s[...] + twin[...] + mm(w[...], both[:, : s.shape[1]])


def away_kernel(w, both, s, twin, *outs):
    rows, width = s.shape
    value = s[...] + twin[...] + mm(w[...], both[:, :width])
    top = jnp.maximum(jnp.max(jnp.abs(value), keepdims=True), 1e-30)
    power = jnp.ceil(jnp.log2(top))
    value = value * jnp.exp2(REACH - power)
    part = rows // len(outs)
    for k, out in enumerate(outs):
        out[:part] = value[k * part : (k + 1) * part]
        if k == 0:
            out[part:] = jnp.broadcast_to(power, (out.shape[0] - part, width))


def finish_kernel(near, c0, c1, c2, c3, out):
    part = c1.shape[0]
    scale = jnp.exp2(c0[part : part + 1, :] - REACH)
    for k, chunk in enumerate((c0, c1, c2, c3)):
        here = slice(k * part, (k + 1) * part)
        out[here] = near[here] + chunk[:part] * scale


def quarter_kernel(a, b, o0, o1, o2, o3, total):
    total[...] = a[...] + b[...]
    here, part = lax.axis_index("z"), o0.shape[0]
    for out, d in ((o0, 0), (o1, 1), (o2, 3), (o3, 2)):
        out[...] = total[pl.ds(pl.multiple_of(((here + 4 - d) % 4) * part, part), part), :]


def sum_kernel(a, b, c, d, out):
    out[...] = a[...] + b[...] + c[...] + d[...]


def place_kernel(pairs, a, b, c, d, out):
    here, part = lax.axis_index("z"), a.shape[0]
    for block, k in ((a, 0), (b, 1), (c, 3), (d, 2)):
        out[pl.ds(pl.multiple_of(((here + k) % 4) * part, part), part), :] = block[...] / pairs


def join_kernel(a, b, down, up):
    first = lax.axis_index("c") == 0
    down[...] = jnp.where(first, a[...], b[...])
    up[...] = jnp.where(first, b[...], a[...])


def run(kernel, name, operands, outs, scratch, flops, consts=True):
    spec = pl.BlockSpec(memory_space=pltpu.VMEM)
    ins = [spec] * len(operands)
    if consts:
        ins[0] = pl.BlockSpec(memory_space=pltpu.SMEM)
    size = sum(math.prod(o.shape) * o.dtype.itemsize for o in list(operands) + list(outs))
    return pl.pallas_call(
        kernel,
        in_specs=ins,
        out_specs=[spec] * len(outs),
        out_shape=outs,
        scratch_shapes=scratch,
        compiler_params=pltpu.CompilerParams(vmem_limit_bytes=16 * MIB),
        cost_estimate=pl.CostEstimate(flops=int(flops), bytes_accessed=size, transcendentals=0),
        name=name,
    )(*operands)


def shards(images, texts, proj, down, up, scale, offset):
    own, texts = images[0], texts[0]
    rows, width = texts.shape
    rank = down.shape[1]
    wide = width + 128
    factor = scale[0] / math.sqrt(width)
    consts = jnp.stack([-factor * LOG2E, -offset[0] * LOG2E, factor])
    down = down.T

    def turned(block, way):
        n = lax.axis_size("z")
        step = lambda z, c: (z + (way if c == 0 else -way)) % n
        return lax.ppermute(block, ("z", "c"), [(2 * step(z, c) + c, 2 * z + c) for z in range(n) for c in range(2)])

    twin = from_ahead(texts, "c", 1)
    ahead = turned(own, 1)
    behind = turned(own, -1)
    across = from_ahead(texts, "y", 1)

    shape = jax.ShapeDtypeStruct
    sums, narrow, grads = shape((rows, width), F32), shape((rows, 128), F32), shape((rank, width), F32)
    unit = 2.0 * rows * rows * width
    pair_flops = 2.2 * unit

    both0, ups0, s0, s1, h0, h1, inner0 = run(
        own_kernel,
        "own_rows",
        [consts, own, texts, twin, proj, down, up],
        [shape((rows, wide), BF16), shape((2 * rank, 2 * rows), BF16), sums, sums, narrow, narrow, shape((2 * rank, rows), F32)],
        [pltpu.VMEM((rows, rows), BF16)],
        3.2 * unit + 2 * pair_flops,
    )
    ups0, across, ahead, behind = tied(ups0, across, ahead, behind)
    far = turned(ahead, 1)
    across_twin = from_ahead(across, "c", 1)
    both1, s0, s1, h0, h1, inner1 = run(
        side_kernel,
        "side_rows",
        [consts, ahead, behind, texts, twin, ups0, proj, down, up, s0, s1, h0, h1],
        [shape((2 * rows, wide), BF16), sums, sums, narrow, narrow, shape((2 * rank, 2 * rows), F32)],
        [pltpu.VMEM((rows, 2 * rows), BF16)],
        6.4 * unit + 4 * pair_flops,
    )
    ups1, s2, s3, h2, grad_down, grad_up = run(
        far_text_kernel,
        "far_texts",
        [consts, both0, both1, across, across_twin, up, inner0, inner1, own, ahead, behind, twin, h1],
        [shape((2 * rank, 2 * rows), BF16), sums, sums, narrow, grads, grads],
        [pltpu.VMEM((rows, rows), BF16), pltpu.VMEM((rows, 2 * rows), BF16)],
        6 * pair_flops,
    )
    far_twin = from_ahead(far, "c", 1)
    s1 = from_ahead(s1, "c", 1)
    s3 = from_ahead(s3, "c", 1)
    kept, sent, both2, w0, w2 = run(
        last_kernel,
        "far_rows",
        [consts, far, far_twin, texts, across, ups0, ups1, proj, down, up, h0, h2, grad_down, grad_up],
        [grads, grads, shape((2 * rows, wide), BF16)] + [shape((rows, 2 * rows), BF16)] * 2,
        [],
        6.4 * unit + 5 * unit,
    )

    def small(kernel, name, operands, outs, scratch=()):
        return run(kernel, name, operands, outs, scratch, 1, False)

    part = rows // 4
    chunks = small(
        away_kernel, "away_sums", [w2, both2, s2, s3], [shape((part + (16 if k == 0 else 0), width), F32) for k in range(4)]
    )
    chunks = [chunk.astype(F16) for chunk in chunks]

    def beside(k, value):
        moved = from_ahead(chunks[k], "y", 1).astype(F32)
        return tied(value, moved)

    def everyones(block, axis):
        others = [from_ahead(block, axis, d) for d in (1, 3, 2)]
        return small(sum_kernel, "sums", [block] + others, [quarter])[0]

    quarter = shape((rank // 4, width), F32)
    sent = from_ahead(sent, "c", 1)
    sent, *chunks = tied(sent, *chunks)
    pieces = small(quarter_kernel, "quarters", [kept, sent], [quarter] * 4, [pltpu.VMEM((rank, width), F32)])
    pieces = [pieces[0]] + [from_ahead(p, "z", d) for p, d in zip(pieces[1:], (1, 3, 2))]
    (kept,) = small(sum_kernel, "sums", pieces, [quarter])
    kept, c0 = beside(0, kept)
    kept = everyones(kept, "x")
    kept, c1 = beside(1, kept)
    (near,) = small(near_kernel, "near_sums", [w0, both2, s0, s1], [sums])
    kept, near = tied(kept, near)
    kept = everyones(kept, ("y", "h"))
    kept, c2 = beside(2, kept)
    pieces = [kept] + [from_ahead(kept, "z", d) for d in (1, 3, 2)]
    (kept,) = small(functools.partial(place_kernel, float(rows * 16)), "places", pieces, [grads])
    kept, c3 = beside(3, kept)
    other = from_ahead(kept, "c", 1)
    (text_grad,) = small(finish_kernel, "finish", [near, c0, c1, c2, c3], [sums])
    grad_down, grad_up = small(join_kernel, "joined", [kept, other], [grads, grads])
    grad_down = grad_down.T
    return text_grad[None], grad_down, grad_up


def solution(mesh):
    grid = Mesh(mesh.devices.reshape(4, 2, 2, 2, 4), AXES)
    blk, dp = ("z", "y", "c"), ("h", "x")
    placed = (P(dp, blk, None), P(dp, blk, None), P(), P(), P(), P(), P())
    return jax.shard_map(
        shards,
        mesh=grid,
        in_specs=placed,
        out_specs=(P(dp, blk, None), P(), P()),
        check_vma=False,
    )
```

time: 149 us -> 104 us (0.70)
  waiting for transfers between devices: 52.4 us -> 27.2 us
  other arithmetic: 7.28 us -> 0.32 us
  local copies, waits for them, and re-layouts: 11.5 us -> 5.93 us
  Pallas kernels: 40.5 us -> 36.4 us
  starting transfers between devices: 35 us -> 32 us
    ppermute x25 -> x24, waiting for transfers between devices: 52.4 us -> 24.5 us  [from_ahead(): lax.ppermute(block, axis, [((i + distance) % n, i) for i in range(n)])]
    ppermute x25 -> x24, starting transfers between devices: 35 us -> 28.2 us  [from_ahead(): lax.ppermute(block, axis, [((i + distance) % n, i) for i in range(n)])]
    unnamed x35 -> x20, local copies, waits for them, and re-layouts: 11.3 us -> 5.93 us
    pallas_call x6 -> x13, Pallas kernels: 40.5 us -> 36.4 us  [run(): pl.pallas_call(kernel, in_specs=ins, out_specs=[spec] * len(outs), out_sh...]
    ppermute x0 -> x3, starting transfers between devices: none -> 3.76 us  [turned(): lax.ppermute(block, ('z', 'c'), [(2 * step(z, c) + c, 2 * z + c) for z in...]
    broadcast_in_dim x1 -> x0, other arithmetic: 3.26 us -> none  [shards(): return (text_grad[None], grad_down, grad_up)]
    ppermute x0 -> x3, waiting for transfers between devices: none -> 2.73 us  [turned(): lax.ppermute(block, ('z', 'c'), [(2 * step(z, c) + c, 2 * z + c) for z in...]
    select_n x1 -> x0, other arithmetic: 1.81 us -> none  [shards(): grad_up = jnp.where(first, other, kept)]
  transfers between devices with their start and end apart: 25 -> 27, of which waited for: 7 -> 12; matrix products, arithmetic and copies ran while one was open for 3% -> 0% of each run, Pallas kernels for 21% -> 34%
where the time goes in v3:
time: 104 us
  Pallas kernels  36.4 us (35%)
  starting transfers between devices  32 us (31%)
  waiting for transfers between devices  27.2 us (26%)
  local copies, waits for them, and re-layouts  5.93 us (6%)
  between operations  2.15 us (2%)
    pallas_call x13, Pallas kernels, run(): pl.pallas_call(kernel, in_specs=ins, out_specs=[spec] * len(outs), out_sh...  36.4 us
    ppermute x24, starting transfers between devices, from_ahead(): lax.ppermute(block, axis, [((i + distance) % n, i) for i in range(n)])  28.2 us
    ppermute x24, waiting for transfers between devices, from_ahead(): lax.ppermute(block, axis, [((i + distance) % n, i) for i in range(n)])  24.5 us
    unnamed x20, local copies, waits for them, and re-layouts  5.93 us
    ppermute x3, starting transfers between devices, turned(): lax.ppermute(block, ('z', 'c'), [(2 * step(z, c) + c, 2 * z + c) for z in...  3.76 us
    ppermute x3, waiting for transfers between devices, turned(): lax.ppermute(block, ('z', 'c'), [(2 * step(z, c) + c, 2 * z + c) for z in...  2.73 us
  transfers between devices with their start and end apart: 27, of which 12 were waited for; matrix products, arithmetic and copies ran while one was open for 0% of the time, Pallas kernels for 34%

profile of v3, /device:TPU:1, one launch (start us, length us, event | category | flops | bytes accessed | tf_op | source)
XLA Modules:
  0.0 103.9 jit_solution(15678509814495942009)
XLA Ops:
  0.6 1.5 %collective-permute-start = (bf16[384,1152]{1,0:T(8,128)(2,1)}, bf16[384,1152]{1,0:T(8,128)(2,1)S(1)}, u32[]{:S(2)}, u32[]{:S(2)}) collective-permute-start(bf16[384,1152]{1,0:T(8,128)(2,1)} %bitcast.9), channel_id=1, source_target_pairs={{8,0},{0,8},{9,1},{1,9},{10,2},{2,10},{11,3},{3,11},{12,4},{4,12},... | collective-permute-start | bytes 2654216 | tf_op jit(solution)/shard_map/ppermute | solution.py:24
  3.5 1.6 %collective-permute-start.2 = (bf16[384,1152]{1,0:T(8,128)(2,1)}, bf16[384,1152]{1,0:T(8,128)(2,1)S(1)}, u32[]{:S(2)}, u32[]{:S(2)}) collective-permute-start(bf16[384,1152]{1,0:T(8,128)(2,1)} %bitcast.5), channel_id=1, source_target_pairs={{32,0},{104,8},{64,32},{8,40},{96,64},{40,72},{0,96},{72,104},{33,... | collective-permute-start | bytes 2654216 | tf_op jit(solution)/shard_map/ppermute | solution.py:234
  5.2 2.1 %collective-permute-start.3 = (bf16[384,1152]{1,0:T(8,128)(2,1)}, bf16[384,1152]{1,0:T(8,128)(2,1)S(1)}, u32[]{:S(2)}, u32[]{:S(2)}) collective-permute-start(bf16[384,1152]{1,0:T(8,128)(2,1)} %bitcast.6), channel_id=1, source_target_pairs={{96,0},{40,8},{0,32},{72,40},{32,64},{104,72},{64,96},{8,104},{97,... | collective-permute-start | bytes 2654216 | tf_op jit(solution)/shard_map/ppermute | solution.py:234
  8.7 1.8 %copy-done = bf16[1152,1152]{1,0:T(8,128)(2,1)S(1)} copy-done((bf16[1152,1152]{1,0:T(8,128)(2,1)S(1)}, bf16[1152,1152]{1,0:T(8,128)(2,1)}, u32[]{:S(2)}) %copy-start) | copy-done | bytes 2654232
  14.6 6.6 %own_rows.1 = (bf16[384,1280]{1,0:T(8,128)(2,1)S(1)}, bf16[128,768]{1,0:T(8,128)(2,1)S(1)}, f32[384,1152]{1,0:T(8,128)S(1)}, f32[384,1152]{1,0:T(8,128)S(1)}, f3...) custom-call(f32[3]{0:T(128)S(1)} %pad_maximum_fusion.consts, bf16[384,1152]{1,0:T(8,128)(2,1)S(1)} %bitcast.7, ...), custom_call_target="tpu_custom_call" | custom-call | flops 2582013440 | bytes 10911756 | tf_op jit(solution)/shard_map/own_rows/pallas_call | solution.py:210
  21.2 2.4 %collective-permute-done.1.t0.t1 = bf16[384,1152]{1,0:T(8,128)(2,1)S(1)} collective-permute-done((bf16[384,1152]{1,0:T(8,128)(2,1)}, bf16[384,1152]{1,0:T(8,128)(2,1)S(1)}, u32[]{:S(2)}, u32[]{:S(2)}) %collective-permute-start.1) | collective-permute-done | bytes 884768 | tf_op jit(solution)/shard_map/ppermute | solution.py:24
  23.9 2.4 %collective-permute-done.3.b = bf16[384,1152]{1,0:T(8,128)(2,1)S(1)} collective-permute-done((bf16[384,1152]{1,0:T(8,128)(2,1)}, bf16[384,1152]{1,0:T(8,128)(2,1)S(1)}, u32[]{:S(2)}, u32[]{:S(2)}) %collective-permute-start.3) | collective-permute-done | bytes 884768 | tf_op jit(solution)/shard_map/ppermute | solution.py:234
  26.3 1.8 %collective-permute-start.6 = (bf16[384,1152]{1,0:T(8,128)(2,1)S(1)}, bf16[384,1152]{1,0:T(8,128)(2,1)S(1)}, u32[]{:S(2)}, u32[]{:S(2)}) collective-permute-start(bf16[384,1152]{1,0:T(8,128)(2,1)S(1)} %collective-permute-done.1.t0.t1), channel_id=1, source_target_pairs={{8,0},{0,8},{9,1},{1,9},{10,2},{2,10},{11,3},{3,11},{12,4},{4,12},... | collective-permute-start | bytes 2654216 | tf_op jit(solution)/shard_map/ppermute | solution.py:24
  28.1 8.3 %side_rows.1 = (bf16[768,1280]{1,0:T(8,128)(2,1)S(1)}, f32[384,1152]{1,0:T(8,128)S(1)}, f32[384,1152]{1,0:T(8,128)S(1)}, f32[384,128]{1,0:T(8,128)S(1)}, f32[384,128]{1,0:T(8,128)S(1)}, /*index=5*/f32[128,768]{1,0:T(8,128)S(1)}) custom-call(f32[3]{0:T(128)S(1)} %pad_maximum_fusion.consts, bf16[384,1152]{1,0:T(8,128)(2,1)S(1)} %collective-permute-done.2.a, ...), custom_call_target="tpu_custom_call" | custom-call | flops 5164026880 | bytes 16908300 | tf_op jit(solution)/shard_map/side_rows/pallas_call | solution.py:210
  36.5 8.3 %far_texts.1 = (bf16[128,768]{1,0:T(8,128)(2,1)S(1)}, f32[384,1152]{1,0:T(8,128)S(1)}, f32[384,1152]{1,0:T(8,128)S(1)}, f32[384,128]{1,0:T(8,128)S(1)}, f32[64,1152]{1,0:T(8,128)S(1)}, /*index=5*/f32[64,1152]{1,0:T(8,128)S(1)}) custom-call(f32[3]{0:T(128)S(1)} %pad_maximum_fusion.consts, bf16[384,1280]{1,0:T(8,128)(2,1)S(1)} %get-tuple-element.60.both0, ...), custom_call_target="tpu_custom_call" | custom-call | flops 4484549632 | bytes 13713420 | tf_op jit(solution)/shard_map/far_texts/pallas_call | solution.py:210
  44.7 3.0 %collective-permute-start.8 = (f32[384,1152]{1,0:T(8,128)S(1)}, f32[384,1152]{1,0:T(8,128)S(1)}, u32[]{:S(2)}, u32[]{:S(2)}) collective-permute-start(f32[384,1152]{1,0:T(8,128)S(1)} %get-tuple-element.80), channel_id=1, source_target_pairs={{8,0},{0,8},{9,1},{1,9},{10,2},{2,10},{11,3},{3,11},{12,4},{4,12},... | collective-permute-start | bytes 5308424 | tf_op jit(solution)/shard_map/ppermute | solution.py:24
  48.3 4.1 %collective-permute-done.5.far_twin = bf16[384,1152]{1,0:T(8,128)(2,1)S(1)} collective-permute-done((bf16[384,1152]{1,0:T(8,128)(2,1)S(1)}, bf16[384,1152]{1,0:T(8,128)(2,1)S(1)}, u32[]{:S(2)}, u32[]{:S(2)}) %collective-permute-start.5) | collective-permute-done | bytes 884768 | tf_op jit(solution)/shard_map/ppermute | solution.py:24
  52.4 8.4 %far_rows.1 = (f32[64,1152]{1,0:T(8,128)S(1)}, f32[64,1152]{1,0:T(8,128)S(1)}, bf16[768,1280]{1,0:T(8,128)(2,1)S(1)}, bf16[384,768]{1,0:T(8,128)(2,1)S(1)}, bf16[384,768]{1,0:T(8,128)(2,1)S(1)}) custom-call(f32[3]{0:T(128)S(1)} %pad_maximum_fusion.consts, bf16[384,1152]{1,0:T(8,128)(2,1)S(1)} %collective-permute-done.4.far, ...), custom_call_target="tpu_custom_call" | custom-call | flops 3873020416 | bytes 11599884 | tf_op jit(solution)/shard_map/far_rows/pallas_call | solution.py:210
  61.2 1.4 %away_sums.1 = (f32[112,1152]{1,0:T(8,128)S(1)}, f32[96,1152]{1,0:T(8,128)S(1)}, f32[96,1152]{1,0:T(8,128)S(1)}, f32[96,1152]{1,0:T(8,128)S(1)}) custom-call(bf16[384,768]{1,0:T(8,128)(2,1)S(1)} %get-tuple-element.77.w, bf16[768,1280]{1,0:T(8,128)(2,1)S(1)} %get-tuple-element.78.both, f32[384,1152]{1,0:T(8,128)S(1)} %get-tuple-element.79.s, ...), custom_call_target="tpu_custom_call" | custom-call | flops 1 | bytes 7938048 | tf_op jit(solution)/shard_map/away_sums/pallas_call | solution.py:210
  65.6 5.3 %collective-permute-done.10.c = f32[16,1152]{1,0:T(8,128)S(1)} collective-permute-done((f32[16,1152]{1,0:T(8,128)S(1)}, f32[16,1152]{1,0:T(8,128)S(1)}, u32[]{:S(2)}, u32[]{:S(2)}) %collective-permute-start.10) | collective-permute-done | bytes 73760 | tf_op jit(solution)/shard_map/ppermute | solution.py:24
  71.1 3.3 %collective-permute-done.9.b = f32[16,1152]{1,0:T(8,128)S(1)} collective-permute-done((f32[16,1152]{1,0:T(8,128)S(1)}, f32[16,1152]{1,0:T(8,128)S(1)}, u32[]{:S(2)}, u32[]{:S(2)}) %collective-permute-start.9) | collective-permute-done | bytes 73760 | tf_op jit(solution)/shard_map/ppermute | solution.py:24
  74.5 2.5 %collective-permute-start.13 = (f32[16,1152]{1,0:T(8,128)S(1)}, f32[16,1152]{1,0:T(8,128)S(1)}, u32[]{:S(2)}, u32[]{:S(2)}) collective-permute-start(f32[16,1152]{1,0:T(8,128)S(1)} %sums.3.a), channel_id=1, source_target_pairs={{1,0},{2,1},{3,2},{0,3},{5,4},{6,5},{7,6},{4,7},{9,8},{10,9},{11,1... | collective-permute-start | bytes 221192 | tf_op jit(solution)/shard_map/ppermute | solution.py:24
  77.1 1.8 %collective-permute-start.15 = (f32[16,1152]{1,0:T(8,128)S(1)}, f32[16,1152]{1,0:T(8,128)S(1)}, u32[]{:S(2)}, u32[]{:S(2)}) collective-permute-start(f32[16,1152]{1,0:T(8,128)S(1)} %sums.3.a), channel_id=1, source_target_pairs={{2,0},{3,1},{0,2},{1,3},{6,4},{7,5},{4,6},{5,7},{10,8},{11,9},{8,1... | collective-permute-start | bytes 221192 | tf_op jit(solution)/shard_map/ppermute | solution.py:24
  80.0 2.3 %collective-permute-done.14.c = f32[16,1152]{1,0:T(8,128)S(1)} collective-permute-done((f32[16,1152]{1,0:T(8,128)S(1)}, f32[16,1152]{1,0:T(8,128)S(1)}, u32[]{:S(2)}, u32[]{:S(2)}) %collective-permute-start.14) | collective-permute-done | bytes 73760 | tf_op jit(solution)/shard_map/ppermute | solution.py:24
  82.3 2.0 %collective-permute-start.18 = (f32[16,1152]{1,0:T(8,128)S(1)}, f32[16,1152]{1,0:T(8,128)S(1)}, u32[]{:S(2)}, u32[]{:S(2)}) collective-permute-start(f32[16,1152]{1,0:T(8,128)S(1)} %sums.4.a), channel_id=1, source_target_pairs={{4,0},{16,4},{20,16},{0,20},{5,1},{17,5},{21,17},{1,21},{6,2},{18,... | collective-permute-start | bytes 221192 | tf_op jit(solution)/shard_map/ppermute | solution.py:24
  85.5 2.3 %collective-permute-done.18.b = f32[16,1152]{1,0:T(8,128)S(1)} collective-permute-done((f32[16,1152]{1,0:T(8,128)S(1)}, f32[16,1152]{1,0:T(8,128)S(1)}, u32[]{:S(2)}, u32[]{:S(2)}) %collective-permute-start.18) | collective-permute-done | bytes 73760 | tf_op jit(solution)/shard_map/ppermute | solution.py:24
  92.3 1.8 %collective-permute-done.23.c = f32[16,1152]{1,0:T(8,128)S(1)} collective-permute-done((f32[16,1152]{1,0:T(8,128)S(1)}, f32[16,1152]{1,0:T(8,128)S(1)}, u32[]{:S(2)}, u32[]{:S(2)}) %collective-permute-start.23) | collective-permute-done | bytes 73760 | tf_op jit(solution)/shard_map/ppermute | solution.py:24
  95.0 6.6 %collective-permute-start.26 = (f32[64,1152]{1,0:T(8,128)S(1)}, f32[64,1152]{1,0:T(8,128)S(1)}, u32[]{:S(2)}, u32[]{:S(2)}) collective-permute-start(f32[64,1152]{1,0:T(8,128)S(1)} %places.1.a), channel_id=1, source_target_pairs={{8,0},{0,8},{9,1},{1,9},{10,2},{2,10},{11,3},{3,11},{12,4},{4,12},... | collective-permute-start | bytes 884744 | tf_op jit(solution)/shard_map/ppermute | solution.py:24
  101.6 1.4 %finish.1 = f32[384,1152]{1,0:T(8,128)} custom-call(f32[384,1152]{1,0:T(8,128)S(1)} %near_sums.1.near, f32[112,1152]{1,0:T(8,128)S(1)} %convert_element_type.28.c0, f32[96,1152]{1,0:T(8,128)S(1)} %convert_element_type.29.c1, f32[96,1152]{1,0:T(8,128)S(1)} %convert_element_type.30.c2, f32[96,1152]{1,0:T(8,128)S(1)} %convert_element_type.31.c3), custom_call_target="tpu_custom_call" | custom-call | flops 1 | bytes 5382144 | tf_op jit(solution)/shard_map/finish/pallas_call | solution.py:210
  (72 shorter events, 18.7 us)
Async XLA Ops:
  0.6 8.0 %collective-permute-start = (bf16[384,1152]{1,0:T(8,128)(2,1)}, bf16[384,1152]{1,0:T(8,128)(2,1)S(1)}, u32[]{:S(2)}, u32[]{:S(2)}) collective-permute-start(bf16[384,1152]{1,0:T(8,128)(2,1)} %bitcast.9), channel_id=1, source_target_pairs={{8,0},{0,8},{9,1},{1,9},{10,2},{2,10},{11,3},{3,11},{12,4},{4,12},... | collective-permute-start | bytes 2654216 | tf_op jit(solution)/shard_map/ppermute | solution.py:24
  2.1 21.4 %collective-permute-start.1 = (bf16[384,1152]{1,0:T(8,128)(2,1)}, bf16[384,1152]{1,0:T(8,128)(2,1)S(1)}, u32[]{:S(2)}, u32[]{:S(2)}) collective-permute-start(bf16[384,1152]{1,0:T(8,128)(2,1)} %bitcast.10), channel_id=1, source_target_pairs={{16,0},{0,16},{17,1},{1,17},{18,2},{2,18},{19,3},{3,19},{20,4},{4,... | collective-permute-start | bytes 2654216 | tf_op jit(solution)/shard_map/ppermute | solution.py:24
  3.5 20.3 %collective-permute-start.2 = (bf16[384,1152]{1,0:T(8,128)(2,1)}, bf16[384,1152]{1,0:T(8,128)(2,1)S(1)}, u32[]{:S(2)}, u32[]{:S(2)}) collective-permute-start(bf16[384,1152]{1,0:T(8,128)(2,1)} %bitcast.5), channel_id=1, source_target_pairs={{32,0},{104,8},{64,32},{8,40},{96,64},{40,72},{0,96},{72,104},{33,... | collective-permute-start | bytes 2654216 | tf_op jit(solution)/shard_map/ppermute | solution.py:234
  5.2 21.1 %collective-permute-start.3 = (bf16[384,1152]{1,0:T(8,128)(2,1)}, bf16[384,1152]{1,0:T(8,128)(2,1)S(1)}, u32[]{:S(2)}, u32[]{:S(2)}) collective-permute-start(bf16[384,1152]{1,0:T(8,128)(2,1)} %bitcast.6), channel_id=1, source_target_pairs={{96,0},{40,8},{0,32},{72,40},{32,64},{104,72},{64,96},{8,104},{97,... | collective-permute-start | bytes 2654216 | tf_op jit(solution)/shard_map/ppermute | solution.py:234
  26.3 10.2 %collective-permute-start.6 = (bf16[384,1152]{1,0:T(8,128)(2,1)S(1)}, bf16[384,1152]{1,0:T(8,128)(2,1)S(1)}, u32[]{:S(2)}, u32[]{:S(2)}) collective-permute-start(bf16[384,1152]{1,0:T(8,128)(2,1)S(1)} %collective-permute-done.1.t0.t1), channel_id=1, source_target_pairs={{8,0},{0,8},{9,1},{1,9},{10,2},{2,10},{11,3},{3,11},{12,4},{4,12},... | collective-permute-start | bytes 2654216 | tf_op jit(solution)/shard_map/ppermute | solution.py:24
  28.1 19.7 %collective-permute-start.4 = (bf16[384,1152]{1,0:T(8,128)(2,1)S(1)}, bf16[384,1152]{1,0:T(8,128)(2,1)S(1)}, u32[]{:S(2)}, u32[]{:S(2)}) collective-permute-start(bf16[384,1152]{1,0:T(8,128)(2,1)S(1)} %collective-permute-done.2.a), channel_id=1, source_target_pairs={{32,0},{104,8},{64,32},{8,40},{96,64},{40,72},{0,96},{72,104},{33,... | collective-permute-start | bytes 2654216 | tf_op jit(solution)/shard_map/ppermute | solution.py:234
  44.7 16.5 %collective-permute-start.8 = (f32[384,1152]{1,0:T(8,128)S(1)}, f32[384,1152]{1,0:T(8,128)S(1)}, u32[]{:S(2)}, u32[]{:S(2)}) collective-permute-start(f32[384,1152]{1,0:T(8,128)S(1)} %get-tuple-element.80), channel_id=1, source_target_pairs={{8,0},{0,8},{9,1},{1,9},{10,2},{2,10},{11,3},{3,11},{12,4},{4,12},... | collective-permute-start | bytes 5308424 | tf_op jit(solution)/shard_map/ppermute | solution.py:24
  47.8 4.6 %collective-permute-start.5 = (bf16[384,1152]{1,0:T(8,128)(2,1)S(1)}, bf16[384,1152]{1,0:T(8,128)(2,1)S(1)}, u32[]{:S(2)}, u32[]{:S(2)}) collective-permute-start(bf16[384,1152]{1,0:T(8,128)(2,1)S(1)} %collective-permute-done.4.far), channel_id=1, source_target_pairs={{8,0},{0,8},{9,1},{1,9},{10,2},{2,10},{11,3},{3,11},{12,4},{4,12},... | collective-permute-start | bytes 2654216 | tf_op jit(solution)/shard_map/ppermute | solution.py:24
  48.1 29.0 %collective-permute-start.17 = (f32[384,1152]{1,0:T(8,128)S(1)}, f32[384,1152]{1,0:T(8,128)S(1)}, u32[]{:S(2)}, u32[]{:S(2)}) collective-permute-start(f32[384,1152]{1,0:T(8,128)S(1)} %get-tuple-element.96), channel_id=1, source_target_pairs={{8,0},{0,8},{9,1},{1,9},{10,2},{2,10},{11,3},{3,11},{12,4},{4,12},... | collective-permute-start | bytes 5308424 | tf_op jit(solution)/shard_map/ppermute | solution.py:24
  62.8 11.6 %collective-permute-start.12 = (f16[112,1152]{1,0:T(8,128)(2,1)S(1)}, f16[112,1152]{1,0:T(8,128)(2,1)S(1)}, u32[]{:S(2)}, u32[]{:S(2)}) collective-permute-start(f16[112,1152]{1,0:T(8,128)(2,1)S(1)} %convert_element_type.24), channel_id=1, source_target_pairs={{16,0},{0,16},{17,1},{1,17},{18,2},{2,18},{19,3},{3,19},{20,4},{4,... | collective-permute-start | bytes 774152 | tf_op jit(solution)/shard_map/ppermute | solution.py:24
  63.1 15.8 %collective-permute-start.16 = (f16[96,1152]{1,0:T(8,128)(2,1)S(1)}, f16[96,1152]{1,0:T(8,128)(2,1)S(1)}, u32[]{:S(2)}, u32[]{:S(2)}) collective-permute-start(f16[96,1152]{1,0:T(8,128)(2,1)S(1)} %convert_element_type.25), channel_id=1, source_target_pairs={{16,0},{0,16},{17,1},{1,17},{18,2},{2,18},{19,3},{3,19},{20,4},{4,... | collective-permute-start | bytes 663560 | tf_op jit(solution)/shard_map/ppermute | solution.py:24
  64.4 6.5 %collective-permute-start.10 = (f32[16,1152]{1,0:T(8,128)S(1)}, f32[16,1152]{1,0:T(8,128)S(1)}, u32[]{:S(2)}, u32[]{:S(2)}) collective-permute-start(f32[16,1152]{1,0:T(8,128)S(1)} %get-tuple-element.88), channel_id=1, source_target_pairs={{96,0},{0,32},{32,64},{64,96},{97,1},{1,33},{33,65},{65,97},{98,2}... | collective-permute-start | bytes 221192 | tf_op jit(solution)/shard_map/ppermute | solution.py:24
  64.5 6.4 %collective-permute-start.11 = (f32[16,1152]{1,0:T(8,128)S(1)}, f32[16,1152]{1,0:T(8,128)S(1)}, u32[]{:S(2)}, u32[]{:S(2)}) collective-permute-start(f32[16,1152]{1,0:T(8,128)S(1)} %get-tuple-element.89), channel_id=1, source_target_pairs={{64,0},{96,32},{0,64},{32,96},{65,1},{97,33},{1,65},{33,97},{66,2}... | collective-permute-start | bytes 221192 | tf_op jit(solution)/shard_map/ppermute | solution.py:24
  70.9 14.6 %collective-permute-start.21 = (f16[96,1152]{1,0:T(8,128)(2,1)S(1)}, f16[96,1152]{1,0:T(8,128)(2,1)S(1)}, u32[]{:S(2)}, u32[]{:S(2)}) collective-permute-start(f16[96,1152]{1,0:T(8,128)(2,1)S(1)} %convert_element_type.26), channel_id=1, source_target_pairs={{16,0},{0,16},{17,1},{1,17},{18,2},{2,18},{19,3},{3,19},{20,4},{4,... | collective-permute-start | bytes 663560 | tf_op jit(solution)/shard_map/ppermute | solution.py:24
  74.5 5.5 %collective-permute-start.13 = (f32[16,1152]{1,0:T(8,128)S(1)}, f32[16,1152]{1,0:T(8,128)S(1)}, u32[]{:S(2)}, u32[]{:S(2)}) collective-permute-start(f32[16,1152]{1,0:T(8,128)S(1)} %sums.3.a), channel_id=1, source_target_pairs={{1,0},{2,1},{3,2},{0,3},{5,4},{6,5},{7,6},{4,7},{9,8},{10,9},{11,1... | collective-permute-start | bytes 221192 | tf_op jit(solution)/shard_map/ppermute | solution.py:24
  77.1 5.2 %collective-permute-start.14 = (f32[16,1152]{1,0:T(8,128)S(1)}, f32[16,1152]{1,0:T(8,128)S(1)}, u32[]{:S(2)}, u32[]{:S(2)}) collective-permute-start(f32[16,1152]{1,0:T(8,128)S(1)} %sums.3.a), channel_id=1, source_target_pairs={{3,0},{0,1},{1,2},{2,3},{7,4},{4,5},{5,6},{6,7},{11,8},{8,9},{9,10... | collective-permute-start | bytes 221192 | tf_op jit(solution)/shard_map/ppermute | solution.py:24
  77.1 5.2 %collective-permute-start.15 = (f32[16,1152]{1,0:T(8,128)S(1)}, f32[16,1152]{1,0:T(8,128)S(1)}, u32[]{:S(2)}, u32[]{:S(2)}) collective-permute-start(f32[16,1152]{1,0:T(8,128)S(1)} %sums.3.a), channel_id=1, source_target_pairs={{2,0},{3,1},{0,2},{1,3},{6,4},{7,5},{4,6},{5,7},{10,8},{11,9},{8,1... | collective-permute-start | bytes 221192 | tf_op jit(solution)/shard_map/ppermute | solution.py:24
  78.8 12.1 %collective-permute-start.25 = (f16[96,1152]{1,0:T(8,128)(2,1)S(1)}, f16[96,1152]{1,0:T(8,128)(2,1)S(1)}, u32[]{:S(2)}, u32[]{:S(2)}) collective-permute-start(f16[96,1152]{1,0:T(8,128)(2,1)S(1)} %convert_element_type.27), channel_id=1, source_target_pairs={{16,0},{0,16},{17,1},{1,17},{18,2},{2,18},{19,3},{3,19},{20,4},{4,... | collective-permute-start | bytes 663560 | tf_op jit(solution)/shard_map/ppermute | solution.py:24
  82.3 5.6 %collective-permute-start.18 = (f32[16,1152]{1,0:T(8,128)S(1)}, f32[16,1152]{1,0:T(8,128)S(1)}, u32[]{:S(2)}, u32[]{:S(2)}) collective-permute-start(f32[16,1152]{1,0:T(8,128)S(1)} %sums.4.a), channel_id=1, source_target_pairs={{4,0},{16,4},{20,16},{0,20},{5,1},{17,5},{21,17},{1,21},{6,2},{18,... | collective-permute-start | bytes 221192 | tf_op jit(solution)/shard_map/ppermute | solution.py:24
  84.3 4.4 %collective-permute-start.19 = (f32[16,1152]{1,0:T(8,128)S(1)}, f32[16,1152]{1,0:T(8,128)S(1)}, u32[]{:S(2)}, u32[]{:S(2)}) collective-permute-start(f32[16,1152]{1,0:T(8,128)S(1)} %sums.4.a), channel_id=1, source_target_pairs={{20,0},{0,4},{4,16},{16,20},{21,1},{1,5},{5,17},{17,21},{22,2},{2,... | collective-permute-start | bytes 221192 | tf_op jit(solution)/shard_map/ppermute | solution.py:24
  88.7 3.6 %collective-permute-start.22 = (f32[16,1152]{1,0:T(8,128)S(1)}, f32[16,1152]{1,0:T(8,128)S(1)}, u32[]{:S(2)}, u32[]{:S(2)}) collective-permute-start(f32[16,1152]{1,0:T(8,128)S(1)} %sums.5.a), channel_id=1, source_target_pairs={{32,0},{64,32},{96,64},{0,96},{33,1},{65,33},{97,65},{1,97},{34,2}... | collective-permute-start | bytes 221192 | tf_op jit(solution)/shard_map/ppermute | solution.py:24
  89.7 4.4 %collective-permute-start.23 = (f32[16,1152]{1,0:T(8,128)S(1)}, f32[16,1152]{1,0:T(8,128)S(1)}, u32[]{:S(2)}, u32[]{:S(2)}) collective-permute-start(f32[16,1152]{1,0:T(8,128)S(1)} %sums.5.a), channel_id=1, source_target_pairs={{96,0},{0,32},{32,64},{64,96},{97,1},{1,33},{33,65},{65,97},{98,2}... | collective-permute-start | bytes 221192 | tf_op jit(solution)/shard_map/ppermute | solution.py:24
  90.2 4.7 %collective-permute-start.24 = (f32[16,1152]{1,0:T(8,128)S(1)}, f32[16,1152]{1,0:T(8,128)S(1)}, u32[]{:S(2)}, u32[]{:S(2)}) collective-permute-start(f32[16,1152]{1,0:T(8,128)S(1)} %sums.5.a), channel_id=1, source_target_pairs={{64,0},{96,32},{0,64},{32,96},{65,1},{97,33},{1,65},{33,97},{66,2}... | collective-permute-start | bytes 221192 | tf_op jit(solution)/shard_map/ppermute | solution.py:24
  95.0 8.1 %collective-permute-start.26 = (f32[64,1152]{1,0:T(8,128)S(1)}, f32[64,1152]{1,0:T(8,128)S(1)}, u32[]{:S(2)}, u32[]{:S(2)}) collective-permute-start(f32[64,1152]{1,0:T(8,128)S(1)} %places.1.a), channel_id=1, source_target_pairs={{8,0},{0,8},{9,1},{1,9},{10,2},{2,10},{11,3},{3,11},{12,4},{4,12},... | collective-permute-start | bytes 884744 | tf_op jit(solution)/shard_map/ppermute | solution.py:24
  (13 other events, 77.3 us)

commit v4 on v3

--- a/solution.py
+++ b/solution.py
@@ -80,6 +80,13 @@
     pair = jnp.concatenate(halves(hidden[:, :rank]), axis=1)
     grad = mm_tn(pair, texts)
     return grad[:rank] + grad[rank:]
+
+
+def consts_kernel(root, scale, offset, out):
+    factor = scale[0] / root
+    out[0] = -factor * LOG2E
+    out[1] = -offset[0] * LOG2E
+    out[2] = factor
 
 
 def own_kernel(consts, own, t0, t1, proj, down, up, both, ups, s0, s1, h0, h1, inner, w):
@@ -107,26 +114,30 @@
         inner[...] = inner[...] + part if k else part
 
 
-def far_text_kernel(
-    consts, both0, both1, t0, t1, up, inner0, inner1, own, a, b, near, h1, ups, s0, s1, h0, grad_down, grad_up, w0, w1
-):
-    rows, width = own.shape
-    rank = up.shape[0]
-    sums0, sums1 = inner0[...], inner1[...]
-    for k, (texts, s) in enumerate(((t0, s0), (t1, s1))):
-        text_ups(texts, up, ups, k * rows)
-        w0[...] = gate(mm_nt(texts[...], both0[:, :width]), consts)
-        w1[...] = gate(mm_nt(texts[...], both1[:, :width]), consts)
-        sums = mm(w0[...], both0[...]) + mm(w1[...], both1[...])
-        s[...] = sums[:, :width]
-        if k == 0:
-            h0[...] = sums[:, width:]
-        else:
-            grad_up[...] = up_share(sums[:, width:], texts[...], rank) + up_share(h1[...], near[...], rank)
-        mine = ups[:, k * rows : (k + 1) * rows]
-        sums0, sums1 = sums0 + mm(mine, w0[...]), sums1 + mm(mine, w1[...])
+def own_far_kernel(consts, both, texts, up, inner0, ups, s, h, inner, w):
+    width = texts.shape[1]
+    text_ups(texts, up, ups, 0)
+    w[...] = gate(mm_nt(texts[...], both[:, :width]), consts)
+    sums = mm(w[...], both[...])
+    s[...], h[...] = sums[:, :width], sums[:, width:]
+    inner[...] = inner0[...] + mm(ups[...], w[...])
+
+
+def side_far_kernel(consts, both, texts, ups, inner0, s0, h0, s, h, inner, w):
+    width = texts.shape[1]
+    w[...] = gate(mm_nt(texts[...], both[:, :width]), consts)
+    sums = mm(w[...], both[...])
+    s[...], h[...] = s0[...] + sums[:, :width], h0[...] + sums[:, width:]
+    inner[...] = inner0[...] + mm(ups[...], w[...])
+
+
+def shares_kernel(inner0, inner1, own, a, b, h1, h3, t1, t3, grad_down, grad_up):
+    rows, rank = own.shape[0], grad_up.shape[0]
+    grad_up[...] = up_share(h1[...], t1[...], rank) + up_share(h3[...], t3[...], rank)
     grad_down[...] = (
-        down_share(sums0, own[...]) + down_share(sums1[:, :rows], a[...]) + down_share(sums1[:, rows:], b[...])
+        down_share(inner0[...], own[...])
+        + down_share(inner1[:, :rows], a[...])
+        + down_share(inner1[:, rows:], b[...])
     )
 
 
@@ -163,19 +174,21 @@
     top = jnp.maximum(jnp.max(jnp.abs(value), keepdims=True), 1e-30)
     power = jnp.ceil(jnp.log2(top))
     value = value * jnp.exp2(REACH - power)
-    part = rows // len(outs)
+    tail, at = outs[0].shape[0] - 16, 0
     for k, out in enumerate(outs):
-        out[:part] = value[k * part : (k + 1) * part]
-        if k == 0:
-            out[part:] = jnp.broadcast_to(power, (out.shape[0] - part, width))
-
-
-def finish_kernel(near, c0, c1, c2, c3, out):
-    part = c1.shape[0]
-    scale = jnp.exp2(c0[part : part + 1, :] - REACH)
-    for k, chunk in enumerate((c0, c1, c2, c3)):
-        here = slice(k * part, (k + 1) * part)
-        out[here] = near[here] + chunk[:part] * scale
+        part = out.shape[0] if k else tail
+        out[:part] = value[at : at + part]
+        at += part
+    outs[0][tail:] = jnp.broadcast_to(power, (16, width))
+
+
+def finish_kernel(near, c0, c1, c2, out):
+    tail, at = c0.shape[0] - 16, 0
+    scale = jnp.exp2(c0[tail : tail + 1, :] - REACH)
+    for k, chunk in enumerate((c0, c1, c2)):
+        part = chunk.shape[0] if k else tail
+        out[at : at + part] = near[at : at + part] + chunk[:part] * scale
+        at += part
 
 
 def quarter_kernel(a, b, o0, o1, o2, o3, total):
@@ -224,8 +237,14 @@
     rows, width = texts.shape
     rank = down.shape[1]
     wide = width + 128
-    factor = scale[0] / math.sqrt(width)
-    consts = jnp.stack([-factor * LOG2E, -offset[0] * LOG2E, factor])
+    scalar = pl.BlockSpec(memory_space=pltpu.SMEM)
+    consts = pl.pallas_call(
+        functools.partial(consts_kernel, math.sqrt(width)),
+        in_specs=[scalar, scalar],
+        out_specs=scalar,
+        out_shape=jax.ShapeDtypeStruct((3,), F32),
+        name="consts",
+    )(scale, offset)
     down = down.T
 
     def turned(block, way):
@@ -233,10 +252,10 @@
         step = lambda z, c: (z + (way if c == 0 else -way)) % n
         return lax.ppermute(block, ("z", "c"), [(2 * step(z, c) + c, 2 * z + c) for z in range(n) for c in range(2)])
 
-    twin = from_ahead(texts, "c", 1)
     ahead = turned(own, 1)
     behind = turned(own, -1)
     across = from_ahead(texts, "y", 1)
+    twin = from_ahead(texts, "c", 1)
 
     shape = jax.ShapeDtypeStruct
     sums, narrow, grads = shape((rows, width), F32), shape((rows, 128), F32), shape((rank, width), F32)
@@ -251,32 +270,63 @@
         [pltpu.VMEM((rows, rows), BF16)],
         3.2 * unit + 2 * pair_flops,
     )
-    ups0, across, ahead, behind = tied(ups0, across, ahead, behind)
+    ups0, across = tied(ups0, across)
+    across_twin = from_ahead(across, "c", 1)
+    square, block = pltpu.VMEM((rows, rows), BF16), shape((2 * rank, rows), BF16)
+    inner_own, inner_sides = shape((2 * rank, rows), F32), shape((2 * rank, 2 * rows), F32)
+
+    def own_far(texts, inner):
+        return run(
+            own_far_kernel,
+            "own_far",
+            [consts, both0, texts, up, inner],
+            [block, sums, narrow, inner_own],
+            [square],
+            pair_flops,
+        )
+
+    def side_far(texts, ups, inner, s, h):
+        return run(
+            side_far_kernel,
+            "side_far",
+            [consts, both1, texts, ups, inner, s, h],
+            [sums, narrow, inner_sides],
+            [pltpu.VMEM((rows, 2 * rows), BF16)],
+            2 * pair_flops,
+        )
+
+    ups2, s2, h2, inner0 = own_far(across, inner0)
+    inner0, ahead, behind, across_twin = tied(inner0, ahead, behind, across_twin)
     far = turned(ahead, 1)
-    across_twin = from_ahead(across, "c", 1)
     both1, s0, s1, h0, h1, inner1 = run(
         side_kernel,
         "side_rows",
         [consts, ahead, behind, texts, twin, ups0, proj, down, up, s0, s1, h0, h1],
-        [shape((2 * rows, wide), BF16), sums, sums, narrow, narrow, shape((2 * rank, 2 * rows), F32)],
+        [shape((2 * rows, wide), BF16), sums, sums, narrow, narrow, inner_sides],
         [pltpu.VMEM((rows, 2 * rows), BF16)],
         6.4 * unit + 4 * pair_flops,
     )
-    ups1, s2, s3, h2, grad_down, grad_up = run(
-        far_text_kernel,
-        "far_texts",
-        [consts, both0, both1, across, across_twin, up, inner0, inner1, own, ahead, behind, twin, h1],
-        [shape((2 * rank, 2 * rows), BF16), sums, sums, narrow, grads, grads],
-        [pltpu.VMEM((rows, rows), BF16), pltpu.VMEM((rows, 2 * rows), BF16)],
-        6 * pair_flops,
-    )
+    ups3, s3, h3, inner0 = own_far(across_twin, inner0)
+    s3, h3, inner1 = side_far(across_twin, ups3, inner1, s3, h3)
+    inner1, far = tied(inner1, far)
     far_twin = from_ahead(far, "c", 1)
     s1 = from_ahead(s1, "c", 1)
     s3 = from_ahead(s3, "c", 1)
+    s2, h2, inner1 = side_far(across, ups2, inner1, s2, h2)
+    grad_down, grad_up = run(
+        shares_kernel,
+        "shares",
+        [inner0, inner1, own, ahead, behind, h1, h3, twin, across_twin],
+        [grads, grads],
+        [],
+        unit,
+        False,
+    )
+    grad_up, far_twin = tied(grad_up, far_twin)
     kept, sent, both2, w0, w2 = run(
         last_kernel,
         "far_rows",
-        [consts, far, far_twin, texts, across, ups0, ups1, proj, down, up, h0, h2, grad_down, grad_up],
+        [consts, far, far_twin, texts, across, ups0, ups2, proj, down, up, h0, h2, grad_down, grad_up],
         [grads, grads, shape((2 * rows, wide), BF16)] + [shape((rows, 2 * rows), BF16)] * 2,
         [],
         6.4 * unit + 5 * unit,
@@ -285,39 +335,44 @@
     def small(kernel, name, operands, outs, scratch=()):
         return run(kernel, name, operands, outs, scratch, 1, False)
 
-    part = rows // 4
+    sizes = (112, 144, 128)
     chunks = small(
-        away_kernel, "away_sums", [w2, both2, s2, s3], [shape((part + (16 if k == 0 else 0), width), F32) for k in range(4)]
+        away_kernel, "away_sums", [w2, both2, s2, s3], [shape((n + (16 if k == 0 else 0), width), F32) for k, n in enumerate(sizes)]
     )
     chunks = [chunk.astype(F16) for chunk in chunks]
 
-    def beside(k, value):
-        moved = from_ahead(chunks[k], "y", 1).astype(F32)
-        return tied(value, moved)
-
-    def everyones(block, axis):
-        others = [from_ahead(block, axis, d) for d in (1, 3, 2)]
-        return small(sum_kernel, "sums", [block] + others, [quarter])[0]
+    def beside(k, value, summed):
+        value, chunk = tied(value, chunks[k])
+        moved = from_ahead(chunk, "y", 1).astype(F32)
+        return tied(summed(value), moved)
+
+    def everyones(axis):
+        def summed(block):
+            others = [from_ahead(block, axis, d) for d in (1, 3, 2)]
+            return small(sum_kernel, "sums", [block] + others, [quarter])[0]
+
+        return summed
+
+    def scattered(sent):
+        pieces = small(quarter_kernel, "quarters", [kept, sent], [quarter] * 4, [pltpu.VMEM((rank, width), F32)])
+        pieces = [pieces[0]] + [from_ahead(p, "z", d) for p, d in zip(pieces[1:], (1, 3, 2))]
+        return small(sum_kernel, "sums", pieces, [quarter])[0]
+
+    def gathered(block):
+        pieces = [block] + [from_ahead(block, "z", d) for d in (1, 3, 2)]
+        return small(functools.partial(place_kernel, float(rows * 16)), "places", pieces, [grads])[0]
 
     quarter = shape((rank // 4, width), F32)
     sent = from_ahead(sent, "c", 1)
-    sent, *chunks = tied(sent, *chunks)
-    pieces = small(quarter_kernel, "quarters", [kept, sent], [quarter] * 4, [pltpu.VMEM((rank, width), F32)])
-    pieces = [pieces[0]] + [from_ahead(p, "z", d) for p, d in zip(pieces[1:], (1, 3, 2))]
-    (kept,) = small(sum_kernel, "sums", pieces, [quarter])
-    kept, c0 = beside(0, kept)
-    kept = everyones(kept, "x")
-    kept, c1 = beside(1, kept)
+    total, c0 = beside(0, sent, scattered)
+    total = everyones(("y", "h"))(total)
+    total, c1 = beside(1, total, everyones("x"))
     (near,) = small(near_kernel, "near_sums", [w0, both2, s0, s1], [sums])
-    kept, near = tied(kept, near)
-    kept = everyones(kept, ("y", "h"))
-    kept, c2 = beside(2, kept)
-    pieces = [kept] + [from_ahead(kept, "z", d) for d in (1, 3, 2)]
-    (kept,) = small(functools.partial(place_kernel, float(rows * 16)), "places", pieces, [grads])
-    kept, c3 = beside(3, kept)
-    other = from_ahead(kept, "c", 1)
-    (text_grad,) = small(finish_kernel, "finish", [near, c0, c1, c2, c3], [sums])
-    grad_down, grad_up = small(join_kernel, "joined", [kept, other], [grads, grads])
+    total, near = tied(total, near)
+    total, c2 = beside(2, total, gathered)
+    other = from_ahead(total, "c", 1)
+    (text_grad,) = small(finish_kernel, "finish", [near, c0, c1, c2], [sums])
+    grad_down, grad_up = small(join_kernel, "joined", [total, other], [grads, grads])
     grad_down = grad_down.T
     return text_grad[None], grad_down, grad_up
 

time: 104 us -> 99.4 us (0.956)
  waiting for transfers between devices: 27.2 us -> 15 us
  starting transfers between devices: 32 us -> 35.7 us
  Pallas kernels: 36.4 us -> 39.4 us
    ppermute x24 -> x23, waiting for transfers between devices: 24.5 us -> 14.9 us  [from_ahead(): lax.ppermute(block, axis, [((i + distance) % n, i) for i in range(n)])]
    ppermute x3, waiting for transfers between devices: 2.73 us -> 0.01 us  [turned(): lax.ppermute(block, ('z', 'c'), [(2 * step(z, c) + c, 2 * z + c) for z in...]
    pallas_call x13 -> x17, Pallas kernels: 36.4 us -> 38.8 us  [run(): pl.pallas_call(kernel, in_specs=ins, out_specs=[spec] * len(outs), out_sh...]
    ppermute x3, starting transfers between devices: 3.76 us -> 5.73 us  [turned(): lax.ppermute(block, ('z', 'c'), [(2 * step(z, c) + c, 2 * z + c) for z in...]
    ppermute x24 -> x23, starting transfers between devices: 28.2 us -> 30 us  [from_ahead(): lax.ppermute(block, axis, [((i + distance) % n, i) for i in range(n)])]
    unnamed x20 -> x22, local copies, waits for them, and re-layouts: 5.93 us -> 6.58 us
  transfers between devices with their start and end apart: 27 -> 26, of which waited for: 12 -> 12; matrix products, arithmetic and copies ran while one was open for 0% -> 0% of each run, Pallas kernels for 34% -> 39%
where the time goes in v4:
time: 99.4 us; the launch traced here: 99.1 us
  Pallas kernels  39.4 us (40%)
  starting transfers between devices  35.7 us (36%)
  waiting for transfers between devices  15 us (15%)
  local copies, waits for them, and re-layouts  6.58 us (7%)
  between operations  2.2 us (2%)
    pallas_call x17, Pallas kernels, run(): pl.pallas_call(kernel, in_specs=ins, out_specs=[spec] * len(outs), out_sh...  38.8 us
    ppermute x23, starting transfers between devices, from_ahead(): lax.ppermute(block, axis, [((i + distance) % n, i) for i in range(n)])  30 us
    ppermute x23, waiting for transfers between devices, from_ahead(): lax.ppermute(block, axis, [((i + distance) % n, i) for i in range(n)])  14.9 us
    unnamed x22, local copies, waits for them, and re-layouts  6.58 us
    ppermute x3, starting transfers between devices, turned(): lax.ppermute(block, ('z', 'c'), [(2 * step(z, c) + c, 2 * z + c) for z in...  5.73 us
  transfers between devices with their start and end apart: 26, of which 12 were waited for; matrix products, arithmetic and copies ran while one was open for 0% of the time, Pallas kernels for 39%

profile of v4, /device:TPU:1, one launch (start us, length us, event | category | flops | bytes accessed | tf_op | source)
XLA Modules:
  0.0 99.1 jit_solution(5662403110562489676)
XLA Ops:
  0.6 1.5 %collective-permute-start = (bf16[384,1152]{1,0:T(8,128)(2,1)}, bf16[384,1152]{1,0:T(8,128)(2,1)S(1)}, u32[]{:S(2)}, u32[]{:S(2)}) collective-permute-start(bf16[384,1152]{1,0:T(8,128)(2,1)} %bitcast.9), channel_id=1, source_target_pairs={{8,0},{0,8},{9,1},{1,9},{10,2},{2,10},{11,3},{3,11},{12,4},{4,12},... | collective-permute-start | bytes 2654216 | tf_op jit(solution)/shard_map/ppermute | solution.py:24
  2.1 1.4 %collective-permute-start.1 = (bf16[384,1152]{1,0:T(8,128)(2,1)}, bf16[384,1152]{1,0:T(8,128)(2,1)S(1)}, u32[]{:S(2)}, u32[]{:S(2)}) collective-permute-start(bf16[384,1152]{1,0:T(8,128)(2,1)} %bitcast.10), channel_id=1, source_target_pairs={{16,0},{0,16},{17,1},{1,17},{18,2},{2,18},{19,3},{3,19},{20,4},{4,... | collective-permute-start | bytes 2654216 | tf_op jit(solution)/shard_map/ppermute | solution.py:24
  3.5 1.6 %collective-permute-start.2 = (bf16[384,1152]{1,0:T(8,128)(2,1)}, bf16[384,1152]{1,0:T(8,128)(2,1)S(1)}, u32[]{:S(2)}, u32[]{:S(2)}) collective-permute-start(bf16[384,1152]{1,0:T(8,128)(2,1)} %bitcast.5), channel_id=1, source_target_pairs={{32,0},{104,8},{64,32},{8,40},{96,64},{40,72},{0,96},{72,104},{33,... | collective-permute-start | bytes 2654216 | tf_op jit(solution)/shard_map/ppermute | solution.py:253
  5.2 2.1 %collective-permute-start.3 = (bf16[384,1152]{1,0:T(8,128)(2,1)}, bf16[384,1152]{1,0:T(8,128)(2,1)S(1)}, u32[]{:S(2)}, u32[]{:S(2)}) collective-permute-start(bf16[384,1152]{1,0:T(8,128)(2,1)} %bitcast.6), channel_id=1, source_target_pairs={{96,0},{40,8},{0,32},{72,40},{32,64},{104,72},{64,96},{8,104},{97,... | collective-permute-start | bytes 2654216 | tf_op jit(solution)/shard_map/ppermute | solution.py:253
  10.3 1.7 %copy-done.2 = bf16[1152,1152]{1,0:T(8,128)(2,1)S(1)} copy-done((bf16[1152,1152]{1,0:T(8,128)(2,1)S(1)}, bf16[1152,1152]{1,0:T(8,128)(2,1)}, u32[]{:S(2)}) %copy-start.2) | copy-done | bytes 2654232
  15.7 6.5 %own_rows.1 = (bf16[384,1280]{1,0:T(8,128)(2,1)S(1)}, bf16[128,768]{1,0:T(8,128)(2,1)S(1)}, f32[384,1152]{1,0:T(8,128)S(1)}, f32[384,1152]{1,0:T(8,128)S(1)}, f3...) custom-call(f32[3]{0:T(128)S(1)} %copy-done.10, bf16[384,1152]{1,0:T(8,128)(2,1)S(1)} %bitcast.7, ...), custom_call_target="tpu_custom_call" | custom-call | flops 2582013440 | bytes 10911756 | tf_op jit(solution)/shard_map/own_rows/pallas_call | solution.py:223
  24.4 2.1 %own_far.2 = (bf16[128,384]{1,0:T(8,128)(2,1)S(1)}, f32[384,1152]{1,0:T(8,128)S(1)}, f32[384,128]{1,0:T(8,128)S(1)}, f32[128,384]{1,0:T(8,128)S(1)}) custom-call(f32[3]{0:T(128)S(1)} %copy-done.10, bf16[384,1280]{1,0:T(8,128)(2,1)S(1)} %get-tuple-element.70.both, bf16[384,1152]{1,0:T(8,128)(2,1)S(1)} %collective-permute-done.1.texts.t1, ...), custom_call_target="tpu_custom_call" | custom-call | flops 747424960 | bytes 4472844 | tf_op jit(solution)/shard_map/own_far/pallas_call | solution.py:223
  26.6 2.0 %collective-permute-start.5 = (bf16[384,1152]{1,0:T(8,128)(2,1)S(1)}, bf16[384,1152]{1,0:T(8,128)(2,1)S(1)}, u32[]{:S(2)}, u32[]{:S(2)}) collective-permute-start(bf16[384,1152]{1,0:T(8,128)(2,1)S(1)} %collective-permute-done.2.a), channel_id=1, source_target_pairs={{32,0},{104,8},{64,32},{8,40},{96,64},{40,72},{0,96},{72,104},{33,... | collective-permute-start | bytes 2654216 | tf_op jit(solution)/shard_map/ppermute | solution.py:253
  28.6 2.1 %own_far.3 = (bf16[128,384]{1,0:T(8,128)(2,1)S(1)}, f32[384,1152]{1,0:T(8,128)S(1)}, f32[384,128]{1,0:T(8,128)S(1)}, f32[128,384]{1,0:T(8,128)S(1)}) custom-call(f32[3]{0:T(128)S(1)} %copy-done.10, bf16[384,1280]{1,0:T(8,128)(2,1)S(1)} %get-tuple-element.70.both, bf16[384,1152]{1,0:T(8,128)(2,1)S(1)} %collective-permute-done.4.texts.t3, ...), custom_call_target="tpu_custom_call" | custom-call | flops 747424960 | bytes 4472844 | tf_op jit(solution)/shard_map/own_far/pallas_call | solution.py:223
  30.7 8.3 %side_rows.1 = (bf16[768,1280]{1,0:T(8,128)(2,1)S(1)}, f32[384,1152]{1,0:T(8,128)S(1)}, f32[384,1152]{1,0:T(8,128)S(1)}, f32[384,128]{1,0:T(8,128)S(1)}, f32[384,128]{1,0:T(8,128)S(1)}, /*index=5*/f32[128,768]{1,0:T(8,128)S(1)}) custom-call(f32[3]{0:T(128)S(1)} %copy-done.10, bf16[384,1152]{1,0:T(8,128)(2,1)S(1)} %collective-permute-done.2.a, ...), custom_call_target="tpu_custom_call" | custom-call | flops 5164026880 | bytes 16908300 | tf_op jit(solution)/shard_map/side_rows/pallas_call | solution.py:223
  39.0 2.8 %side_far.2 = (f32[384,1152]{1,0:T(8,128)S(1)}, f32[384,128]{1,0:T(8,128)S(1)}, f32[128,768]{1,0:T(8,128)S(1)}) custom-call(f32[3]{0:T(128)S(1)} %copy-done.10, bf16[768,1280]{1,0:T(8,128)(2,1)S(1)} %get-tuple-element.82.both, bf16[384,1152]{1,0:T(8,128)(2,1)S(1)} %collective-permute-done.4.texts.t3, bf16[128,384]{1,0:T(8,128)(2,1)S(1)} %get-tuple-element.85.ups, ...), custom_call_target="tpu_custom_call" | custom-call | flops 1494849920 | bytes 7667724 | tf_op jit(solution)/shard_map/side_far/pallas_call | solution.py:223
  41.8 2.6 %collective-permute-start.8 = (f32[384,1152]{1,0:T(8,128)S(1)}, f32[384,1152]{1,0:T(8,128)S(1)}, u32[]{:S(2)}, u32[]{:S(2)}) collective-permute-start(f32[384,1152]{1,0:T(8,128)S(1)} %get-tuple-element.110), channel_id=1, source_target_pairs={{8,0},{0,8},{9,1},{1,9},{10,2},{2,10},{11,3},{3,11},{12,4},{4,12},... | collective-permute-start | bytes 5308424 | tf_op jit(solution)/shard_map/ppermute | solution.py:24
  44.9 2.8 %side_far.3 = (f32[384,1152]{1,0:T(8,128)S(1)}, f32[384,128]{1,0:T(8,128)S(1)}, f32[128,768]{1,0:T(8,128)S(1)}) custom-call(f32[3]{0:T(128)S(1)} %copy-done.10, bf16[768,1280]{1,0:T(8,128)(2,1)S(1)} %get-tuple-element.82.both, bf16[384,1152]{1,0:T(8,128)(2,1)S(1)} %collective-permute-done.1.texts.t1, bf16[128,384]{1,0:T(8,128)(2,1)S(1)} %get-tuple-element.92.ups.ups1, ...), custom_call_target="tpu_custom_call" | custom-call | flops 1494849920 | bytes 7667724 | tf_op jit(solution)/shard_map/side_far/pallas_call | solution.py:223
  49.0 8.4 %far_rows.1 = (f32[64,1152]{1,0:T(8,128)S(1)}, f32[64,1152]{1,0:T(8,128)S(1)}, bf16[768,1280]{1,0:T(8,128)(2,1)S(1)}, bf16[384,768]{1,0:T(8,128)(2,1)S(1)}, bf16[384,768]{1,0:T(8,128)(2,1)S(1)}) custom-call(f32[3]{0:T(128)S(1)} %copy-done.10, bf16[384,1152]{1,0:T(8,128)(2,1)S(1)} %collective-permute-done.5.far, ...), custom_call_target="tpu_custom_call" | custom-call | flops 3873020416 | bytes 11501580 | tf_op jit(solution)/shard_map/far_rows/pallas_call | solution.py:223
  57.8 1.4 %away_sums.1 = (f32[128,1152]{1,0:T(8,128)S(1)}, f32[144,1152]{1,0:T(8,128)S(1)}, f32[128,1152]{1,0:T(8,128)S(1)}) custom-call(bf16[384,768]{1,0:T(8,128)(2,1)S(1)} %get-tuple-element.107.w, bf16[768,1280]{1,0:T(8,128)(2,1)S(1)} %get-tuple-element.108.both, f32[384,1152]{1,0:T(8,128)S(1)} %get-tuple-element.109.s, f32[384,1152]{1,0:T(8,128)S(1)} %collective-permute-done.8.twin), custom_call_target="tpu_custom_call" | custom-call | flops 1 | bytes 7938048 | tf_op jit(solution)/shard_map/away_sums/pallas_call | solution.py:223
  65.3 1.9 %collective-permute-done.11.d = f32[16,1152]{1,0:T(8,128)S(1)} collective-permute-done((f32[16,1152]{1,0:T(8,128)S(1)}, f32[16,1152]{1,0:T(8,128)S(1)}, u32[]{:S(2)}, u32[]{:S(2)}) %collective-permute-start.11) | collective-permute-done | bytes 73760 | tf_op jit(solution)/shard_map/ppermute | solution.py:24
  67.9 2.7 %collective-permute-start.13 = (f32[16,1152]{1,0:T(8,128)S(1)}, f32[16,1152]{1,0:T(8,128)S(1)}, u32[]{:S(2)}, u32[]{:S(2)}) collective-permute-start(f32[16,1152]{1,0:T(8,128)S(1)} %sums.3.a), channel_id=1, source_target_pairs={{4,0},{16,4},{20,16},{0,20},{5,1},{17,5},{21,17},{1,21},{6,2},{18,... | collective-permute-start | bytes 221192 | tf_op jit(solution)/shard_map/ppermute | solution.py:24
  72.6 2.4 %collective-permute-done.14.c = f32[16,1152]{1,0:T(8,128)S(1)} collective-permute-done((f32[16,1152]{1,0:T(8,128)S(1)}, f32[16,1152]{1,0:T(8,128)S(1)}, u32[]{:S(2)}, u32[]{:S(2)}) %collective-permute-start.14) | collective-permute-done | bytes 73760 | tf_op jit(solution)/shard_map/ppermute | solution.py:24
  75.7 2.5 %collective-permute-start.16 = (f32[16,1152]{1,0:T(8,128)S(1)}, f32[16,1152]{1,0:T(8,128)S(1)}, u32[]{:S(2)}, u32[]{:S(2)}) collective-permute-start(f32[16,1152]{1,0:T(8,128)S(1)} %sums.4.a), channel_id=1, source_target_pairs={{1,0},{2,1},{3,2},{0,3},{5,4},{6,5},{7,6},{4,7},{9,8},{10,9},{11,1... | collective-permute-start | bytes 221192 | tf_op jit(solution)/shard_map/ppermute | solution.py:24
  78.2 1.8 %collective-permute-start.18 = (f32[16,1152]{1,0:T(8,128)S(1)}, f32[16,1152]{1,0:T(8,128)S(1)}, u32[]{:S(2)}, u32[]{:S(2)}) collective-permute-start(f32[16,1152]{1,0:T(8,128)S(1)} %sums.4.a), channel_id=1, source_target_pairs={{2,0},{3,1},{0,2},{1,3},{6,4},{7,5},{4,6},{5,7},{10,8},{11,9},{8,1... | collective-permute-start | bytes 221192 | tf_op jit(solution)/shard_map/ppermute | solution.py:24
  81.0 2.4 %collective-permute-done.17.c = f32[16,1152]{1,0:T(8,128)S(1)} collective-permute-done((f32[16,1152]{1,0:T(8,128)S(1)}, f32[16,1152]{1,0:T(8,128)S(1)}, u32[]{:S(2)}, u32[]{:S(2)}) %collective-permute-start.17) | collective-permute-done | bytes 73760 | tf_op jit(solution)/shard_map/ppermute | solution.py:24
  87.7 2.2 %collective-permute-done.22.c = f32[16,1152]{1,0:T(8,128)S(1)} collective-permute-done((f32[16,1152]{1,0:T(8,128)S(1)}, f32[16,1152]{1,0:T(8,128)S(1)}, u32[]{:S(2)}, u32[]{:S(2)}) %collective-permute-start.22) | collective-permute-done | bytes 73760 | tf_op jit(solution)/shard_map/ppermute | solution.py:24
  90.8 6.0 %collective-permute-start.25 = (f32[64,1152]{1,0:T(8,128)S(1)}, f32[64,1152]{1,0:T(8,128)S(1)}, u32[]{:S(2)}, u32[]{:S(2)}) collective-permute-start(f32[64,1152]{1,0:T(8,128)S(1)} %places.1.a), channel_id=1, source_target_pairs={{8,0},{0,8},{9,1},{1,9},{10,2},{2,10},{11,3},{3,11},{12,4},{4,12},... | collective-permute-start | bytes 884744 | tf_op jit(solution)/shard_map/ppermute | solution.py:24
  96.8 1.4 %finish.1 = f32[384,1152]{1,0:T(8,128)} custom-call(f32[384,1152]{1,0:T(8,128)S(1)} %near_sums.1.near, f32[128,1152]{1,0:T(8,128)S(1)} %convert_element_type.19.c0, f32[144,1152]{1,0:T(8,128)S(1)} %convert_element_type.21.c1, f32[128,1152]{1,0:T(8,128)S(1)} %convert_element_type.23.c2), custom_call_target="tpu_custom_call" | custom-call | flops 1 | bytes 5382144 | tf_op jit(solution)/shard_map/finish/pallas_call | solution.py:223
  (74 shorter events, 26.3 us)
Async XLA Ops:
  0.6 8.5 %collective-permute-start = (bf16[384,1152]{1,0:T(8,128)(2,1)}, bf16[384,1152]{1,0:T(8,128)(2,1)S(1)}, u32[]{:S(2)}, u32[]{:S(2)}) collective-permute-start(bf16[384,1152]{1,0:T(8,128)(2,1)} %bitcast.9), channel_id=1, source_target_pairs={{8,0},{0,8},{9,1},{1,9},{10,2},{2,10},{11,3},{3,11},{12,4},{4,12},... | collective-permute-start | bytes 2654216 | tf_op jit(solution)/shard_map/ppermute | solution.py:24
  2.1 21.4 %collective-permute-start.1 = (bf16[384,1152]{1,0:T(8,128)(2,1)}, bf16[384,1152]{1,0:T(8,128)(2,1)S(1)}, u32[]{:S(2)}, u32[]{:S(2)}) collective-permute-start(bf16[384,1152]{1,0:T(8,128)(2,1)} %bitcast.10), channel_id=1, source_target_pairs={{16,0},{0,16},{17,1},{1,17},{18,2},{2,18},{19,3},{3,19},{20,4},{4,... | collective-permute-start | bytes 2654216 | tf_op jit(solution)/shard_map/ppermute | solution.py:24
  3.5 23.0 %collective-permute-start.2 = (bf16[384,1152]{1,0:T(8,128)(2,1)}, bf16[384,1152]{1,0:T(8,128)(2,1)S(1)}, u32[]{:S(2)}, u32[]{:S(2)}) collective-permute-start(bf16[384,1152]{1,0:T(8,128)(2,1)} %bitcast.5), channel_id=1, source_target_pairs={{32,0},{104,8},{64,32},{8,40},{96,64},{40,72},{0,96},{72,104},{33,... | collective-permute-start | bytes 2654216 | tf_op jit(solution)/shard_map/ppermute | solution.py:253
  5.2 21.4 %collective-permute-start.3 = (bf16[384,1152]{1,0:T(8,128)(2,1)}, bf16[384,1152]{1,0:T(8,128)(2,1)S(1)}, u32[]{:S(2)}, u32[]{:S(2)}) collective-permute-start(bf16[384,1152]{1,0:T(8,128)(2,1)} %bitcast.6), channel_id=1, source_target_pairs={{96,0},{40,8},{0,32},{72,40},{32,64},{104,72},{64,96},{8,104},{97,... | collective-permute-start | bytes 2654216 | tf_op jit(solution)/shard_map/ppermute | solution.py:253
  26.6 17.8 %collective-permute-start.5 = (bf16[384,1152]{1,0:T(8,128)(2,1)S(1)}, bf16[384,1152]{1,0:T(8,128)(2,1)S(1)}, u32[]{:S(2)}, u32[]{:S(2)}) collective-permute-start(bf16[384,1152]{1,0:T(8,128)(2,1)S(1)} %collective-permute-done.2.a), channel_id=1, source_target_pairs={{32,0},{104,8},{64,32},{8,40},{96,64},{40,72},{0,96},{72,104},{33,... | collective-permute-start | bytes 2654216 | tf_op jit(solution)/shard_map/ppermute | solution.py:253
  41.8 16.0 %collective-permute-start.8 = (f32[384,1152]{1,0:T(8,128)S(1)}, f32[384,1152]{1,0:T(8,128)S(1)}, u32[]{:S(2)}, u32[]{:S(2)}) collective-permute-start(f32[384,1152]{1,0:T(8,128)S(1)} %get-tuple-element.110), channel_id=1, source_target_pairs={{8,0},{0,8},{9,1},{1,9},{10,2},{2,10},{11,3},{3,11},{12,4},{4,12},... | collective-permute-start | bytes 5308424 | tf_op jit(solution)/shard_map/ppermute | solution.py:24
  44.4 4.6 %collective-permute-start.6 = (bf16[384,1152]{1,0:T(8,128)(2,1)S(1)}, bf16[384,1152]{1,0:T(8,128)(2,1)S(1)}, u32[]{:S(2)}, u32[]{:S(2)}) collective-permute-start(bf16[384,1152]{1,0:T(8,128)(2,1)S(1)} %collective-permute-done.5.far), channel_id=1, source_target_pairs={{8,0},{0,8},{9,1},{1,9},{10,2},{2,10},{11,3},{3,11},{12,4},{4,12},... | collective-permute-start | bytes 2654216 | tf_op jit(solution)/shard_map/ppermute | solution.py:24
  44.5 35.5 %collective-permute-start.20 = (f32[384,1152]{1,0:T(8,128)S(1)}, f32[384,1152]{1,0:T(8,128)S(1)}, u32[]{:S(2)}, u32[]{:S(2)}) collective-permute-start(f32[384,1152]{1,0:T(8,128)S(1)} %get-tuple-element.125), channel_id=1, source_target_pairs={{8,0},{0,8},{9,1},{1,9},{10,2},{2,10},{11,3},{3,11},{12,4},{4,12},... | collective-permute-start | bytes 5308424 | tf_op jit(solution)/shard_map/ppermute | solution.py:24
  59.3 8.5 %collective-permute-start.12 = (f16[128,1152]{1,0:T(8,128)(2,1)S(1)}, f16[128,1152]{1,0:T(8,128)(2,1)S(1)}, u32[]{:S(2)}, u32[]{:S(2)}) collective-permute-start(f16[128,1152]{1,0:T(8,128)(2,1)S(1)} %convert_element_type.18), channel_id=1, source_target_pairs={{16,0},{0,16},{17,1},{1,17},{18,2},{2,18},{19,3},{3,19},{20,4},{4,... | collective-permute-start | bytes 884744 | tf_op jit(solution)/shard_map/ppermute | solution.py:24
  60.6 3.6 %collective-permute-start.9 = (f32[16,1152]{1,0:T(8,128)S(1)}, f32[16,1152]{1,0:T(8,128)S(1)}, u32[]{:S(2)}, u32[]{:S(2)}) collective-permute-start(f32[16,1152]{1,0:T(8,128)S(1)} %get-tuple-element.114), channel_id=1, source_target_pairs={{32,0},{64,32},{96,64},{0,96},{33,1},{65,33},{97,65},{1,97},{34,2}... | collective-permute-start | bytes 221192 | tf_op jit(solution)/shard_map/ppermute | solution.py:24
  60.9 4.4 %collective-permute-start.10 = (f32[16,1152]{1,0:T(8,128)S(1)}, f32[16,1152]{1,0:T(8,128)S(1)}, u32[]{:S(2)}, u32[]{:S(2)}) collective-permute-start(f32[16,1152]{1,0:T(8,128)S(1)} %get-tuple-element.115), channel_id=1, source_target_pairs={{96,0},{0,32},{32,64},{64,96},{97,1},{1,33},{33,65},{65,97},{98,2}... | collective-permute-start | bytes 221192 | tf_op jit(solution)/shard_map/ppermute | solution.py:24
  62.1 5.0 %collective-permute-start.11 = (f32[16,1152]{1,0:T(8,128)S(1)}, f32[16,1152]{1,0:T(8,128)S(1)}, u32[]{:S(2)}, u32[]{:S(2)}) collective-permute-start(f32[16,1152]{1,0:T(8,128)S(1)} %get-tuple-element.116), channel_id=1, source_target_pairs={{64,0},{96,32},{0,64},{32,96},{65,1},{97,33},{1,65},{33,97},{66,2}... | collective-permute-start | bytes 221192 | tf_op jit(solution)/shard_map/ppermute | solution.py:24
  67.9 4.8 %collective-permute-start.13 = (f32[16,1152]{1,0:T(8,128)S(1)}, f32[16,1152]{1,0:T(8,128)S(1)}, u32[]{:S(2)}, u32[]{:S(2)}) collective-permute-start(f32[16,1152]{1,0:T(8,128)S(1)} %sums.3.a), channel_id=1, source_target_pairs={{4,0},{16,4},{20,16},{0,20},{5,1},{17,5},{21,17},{1,21},{6,2},{18,... | collective-permute-start | bytes 221192 | tf_op jit(solution)/shard_map/ppermute | solution.py:24
  70.5 4.6 %collective-permute-start.14 = (f32[16,1152]{1,0:T(8,128)S(1)}, f32[16,1152]{1,0:T(8,128)S(1)}, u32[]{:S(2)}, u32[]{:S(2)}) collective-permute-start(f32[16,1152]{1,0:T(8,128)S(1)} %sums.3.a), channel_id=1, source_target_pairs={{20,0},{0,4},{4,16},{16,20},{21,1},{1,5},{5,17},{17,21},{22,2},{2,... | collective-permute-start | bytes 221192 | tf_op jit(solution)/shard_map/ppermute | solution.py:24
  70.9 4.2 %collective-permute-start.15 = (f32[16,1152]{1,0:T(8,128)S(1)}, f32[16,1152]{1,0:T(8,128)S(1)}, u32[]{:S(2)}, u32[]{:S(2)}) collective-permute-start(f32[16,1152]{1,0:T(8,128)S(1)} %sums.3.a), channel_id=1, source_target_pairs={{16,0},{20,4},{0,16},{4,20},{17,1},{21,5},{1,17},{5,21},{18,2},{22... | collective-permute-start | bytes 221192 | tf_op jit(solution)/shard_map/ppermute | solution.py:24
  75.1 8.3 %collective-permute-start.19 = (f16[144,1152]{1,0:T(8,128)(2,1)S(1)}, f16[144,1152]{1,0:T(8,128)(2,1)S(1)}, u32[]{:S(2)}, u32[]{:S(2)}) collective-permute-start(f16[144,1152]{1,0:T(8,128)(2,1)S(1)} %convert_element_type.20), channel_id=1, source_target_pairs={{16,0},{0,16},{17,1},{1,17},{18,2},{2,18},{19,3},{3,19},{20,4},{4,... | collective-permute-start | bytes 995336 | tf_op jit(solution)/shard_map/ppermute | solution.py:24
  75.7 5.3 %collective-permute-start.16 = (f32[16,1152]{1,0:T(8,128)S(1)}, f32[16,1152]{1,0:T(8,128)S(1)}, u32[]{:S(2)}, u32[]{:S(2)}) collective-permute-start(f32[16,1152]{1,0:T(8,128)S(1)} %sums.4.a), channel_id=1, source_target_pairs={{1,0},{2,1},{3,2},{0,3},{5,4},{6,5},{7,6},{4,7},{9,8},{10,9},{11,1... | collective-permute-start | bytes 221192 | tf_op jit(solution)/shard_map/ppermute | solution.py:24
  78.2 5.2 %collective-permute-start.17 = (f32[16,1152]{1,0:T(8,128)S(1)}, f32[16,1152]{1,0:T(8,128)S(1)}, u32[]{:S(2)}, u32[]{:S(2)}) collective-permute-start(f32[16,1152]{1,0:T(8,128)S(1)} %sums.4.a), channel_id=1, source_target_pairs={{3,0},{0,1},{1,2},{2,3},{7,4},{4,5},{5,6},{6,7},{11,8},{8,9},{9,10... | collective-permute-start | bytes 221192 | tf_op jit(solution)/shard_map/ppermute | solution.py:24
  78.2 5.2 %collective-permute-start.18 = (f32[16,1152]{1,0:T(8,128)S(1)}, f32[16,1152]{1,0:T(8,128)S(1)}, u32[]{:S(2)}, u32[]{:S(2)}) collective-permute-start(f32[16,1152]{1,0:T(8,128)S(1)} %sums.4.a), channel_id=1, source_target_pairs={{2,0},{3,1},{0,2},{1,3},{6,4},{7,5},{4,6},{5,7},{10,8},{11,9},{8,1... | collective-permute-start | bytes 221192 | tf_op jit(solution)/shard_map/ppermute | solution.py:24
  83.5 7.2 %collective-permute-start.24 = (f16[128,1152]{1,0:T(8,128)(2,1)S(1)}, f16[128,1152]{1,0:T(8,128)(2,1)S(1)}, u32[]{:S(2)}, u32[]{:S(2)}) collective-permute-start(f16[128,1152]{1,0:T(8,128)(2,1)S(1)} %convert_element_type.22), channel_id=1, source_target_pairs={{16,0},{0,16},{17,1},{1,17},{18,2},{2,18},{19,3},{3,19},{20,4},{4,... | collective-permute-start | bytes 884744 | tf_op jit(solution)/shard_map/ppermute | solution.py:24
  84.5 3.2 %collective-permute-start.21 = (f32[16,1152]{1,0:T(8,128)S(1)}, f32[16,1152]{1,0:T(8,128)S(1)}, u32[]{:S(2)}, u32[]{:S(2)}) collective-permute-start(f32[16,1152]{1,0:T(8,128)S(1)} %sums.5.a), channel_id=1, source_target_pairs={{32,0},{64,32},{96,64},{0,96},{33,1},{65,33},{97,65},{1,97},{34,2}... | collective-permute-start | bytes 221192 | tf_op jit(solution)/shard_map/ppermute | solution.py:24
  85.5 4.4 %collective-permute-start.22 = (f32[16,1152]{1,0:T(8,128)S(1)}, f32[16,1152]{1,0:T(8,128)S(1)}, u32[]{:S(2)}, u32[]{:S(2)}) collective-permute-start(f32[16,1152]{1,0:T(8,128)S(1)} %sums.5.a), channel_id=1, source_target_pairs={{96,0},{0,32},{32,64},{64,96},{97,1},{1,33},{33,65},{65,97},{98,2}... | collective-permute-start | bytes 221192 | tf_op jit(solution)/shard_map/ppermute | solution.py:24
  86.0 4.7 %collective-permute-start.23 = (f32[16,1152]{1,0:T(8,128)S(1)}, f32[16,1152]{1,0:T(8,128)S(1)}, u32[]{:S(2)}, u32[]{:S(2)}) collective-permute-start(f32[16,1152]{1,0:T(8,128)S(1)} %sums.5.a), channel_id=1, source_target_pairs={{64,0},{96,32},{0,64},{32,96},{65,1},{97,33},{1,65},{33,97},{66,2}... | collective-permute-start | bytes 221192 | tf_op jit(solution)/shard_map/ppermute | solution.py:24
  90.8 7.4 %collective-permute-start.25 = (f32[64,1152]{1,0:T(8,128)S(1)}, f32[64,1152]{1,0:T(8,128)S(1)}, u32[]{:S(2)}, u32[]{:S(2)}) collective-permute-start(f32[64,1152]{1,0:T(8,128)S(1)} %places.1.a), channel_id=1, source_target_pairs={{8,0},{0,8},{9,1},{1,9},{10,2},{2,10},{11,3},{3,11},{12,4},{4,12},... | collective-permute-start | bytes 884744 | tf_op jit(solution)/shard_map/ppermute | solution.py:24
  (13 other events, 32.2 us)

commit v5 on v4

--- a/solution.py
+++ b/solution.py
@@ -41,13 +41,13 @@
     return high, (a - high.astype(F32)).astype(BF16)
 
 
-def embed(images, at, both, proj, down, up):
+def embed(images, at, both, packed, up):
     here = slice(at, at + images.shape[0])
-    width, rank = proj.shape[1], down.shape[0]
-    hidden = mm_nt(images[...], down[...]).astype(BF16)
-    both[here, :width] = (mm(images[...], proj[...]) + mm(hidden, up[...])).astype(BF16)
-    both[here, width : width + rank] = hidden
-    both[here, width + rank :] = jnp.zeros((images.shape[0], both.shape[1] - width - rank), BF16)
+    width, rank = up.shape[1], up.shape[0]
+    products = mm(images[...], packed[...])
+    hidden = products[:, width:].astype(BF16)
+    both[here, :width] = (products[:, :width] + mm(hidden[:, :rank], up[...])).astype(BF16)
+    both[here, width:] = hidden
 
 
 def gate(sims, consts):
@@ -89,9 +89,12 @@
     out[2] = factor
 
 
-def own_kernel(consts, own, t0, t1, proj, down, up, both, ups, s0, s1, h0, h1, inner, w):
-    width, rows = proj.shape[1], own.shape[0]
-    embed(own, 0, both, proj, down, up)
+def own_kernel(consts, own, t0, t1, proj, down, up, both, packed, ups, s0, s1, h0, h1, inner, w):
+    width, rows, rank = proj.shape[1], own.shape[0], up.shape[0]
+    packed[:, :width] = proj[...]
+    packed[:, width : width + rank] = down[...].T
+    packed[:, width + rank :] = jnp.zeros((packed.shape[0], packed.shape[1] - width - rank), BF16)
+    embed(own, 0, both, packed, up)
     for k, (texts, s, h) in enumerate(((t0, s0, h0), (t1, s1, h1))):
         text_ups(texts, up, ups, k * rows)
         sims = mm_nt(texts[...], both[:, :width])
@@ -102,10 +105,10 @@
         inner[...] = inner[...] + part if k else part
 
 
-def side_kernel(consts, a, b, t0, t1, ups, proj, down, up, s0, s1, h0, h1, both, o0, o1, g0, g1, inner, w):
-    width, rows = proj.shape[1], a.shape[0]
-    embed(a, 0, both, proj, down, up)
-    embed(b, rows, both, proj, down, up)
+def side_kernel(consts, a, b, t0, t1, ups, packed, up, s0, s1, h0, h1, both, o0, o1, g0, g1, inner, w):
+    width, rows = up.shape[1], a.shape[0]
+    embed(a, 0, both, packed, up)
+    embed(b, rows, both, packed, up)
     for k, (texts, s, h, o, g) in enumerate(((t0, s0, h0, o0, g0), (t1, s1, h1, o1, g1))):
         w[...] = gate(mm_nt(texts[...], both[:, :width]), consts)
         sums = mm(w[...], both[...])
@@ -141,14 +144,16 @@
     )
 
 
+def embed_kernel(images, packed, up, both):
+    embed(images, 0, both, packed, up)
+
+
 def last_kernel(
-    consts, far, far_twin, t0, t1, ups0, ups1, proj, down, up, h0, h1, grad_down, grad_up, kept, sent, both, w0, w1
+    consts, x0, x1, e0, e1, t0, t1, ups0, ups1, h0, h1, grad_down, grad_up, kept, sent, both, w0, w1
 ):
-    rows, width, rank = t0.shape[0], proj.shape[1], up.shape[0]
-    at, blocks = 0, (far, far_twin)
-    for block in blocks:
-        embed(block, at, both, proj, down, up)
-        at += block.shape[0]
+    rows, width = t0.shape
+    rank, blocks = grad_up.shape[0], (x0, x1)
+    both[:rows], both[rows:] = e0[...], e1[...]
     inner, up_sum = None, grad_up[...]
     for texts, ups, h, w in ((t0, ups0, h0, w0), (t1, ups1, h1, w1)):
         w[...] = gate(mm_nt(texts[...], both[:, :width]), consts)
@@ -182,10 +187,10 @@
     outs[0][tail:] = jnp.broadcast_to(power, (16, width))
 
 
-def finish_kernel(near, c0, c1, c2, out):
+def finish_kernel(near, c0, c1, out):
     tail, at = c0.shape[0] - 16, 0
     scale = jnp.exp2(c0[tail : tail + 1, :] - REACH)
-    for k, chunk in enumerate((c0, c1, c2)):
+    for k, chunk in enumerate((c0, c1)):
         part = chunk.shape[0] if k else tail
         out[at : at + part] = near[at : at + part] + chunk[:part] * scale
         at += part
@@ -259,21 +264,21 @@
 
     shape = jax.ShapeDtypeStruct
     sums, narrow, grads = shape((rows, width), F32), shape((rows, 128), F32), shape((rank, width), F32)
+    inner_own, inner_sides = shape((2 * rank, rows), F32), shape((2 * rank, 2 * rows), F32)
     unit = 2.0 * rows * rows * width
     pair_flops = 2.2 * unit
 
-    both0, ups0, s0, s1, h0, h1, inner0 = run(
+    both0, packed, ups0, s0, s1, h0, h1, inner0 = run(
         own_kernel,
         "own_rows",
         [consts, own, texts, twin, proj, down, up],
-        [shape((rows, wide), BF16), shape((2 * rank, 2 * rows), BF16), sums, sums, narrow, narrow, shape((2 * rank, rows), F32)],
+        [shape((rows, wide), BF16), shape((width, wide), BF16), shape((2 * rank, 2 * rows), BF16), sums, sums, narrow, narrow, inner_own],
         [pltpu.VMEM((rows, rows), BF16)],
         3.2 * unit + 2 * pair_flops,
     )
     ups0, across = tied(ups0, across)
     across_twin = from_ahead(across, "c", 1)
     square, block = pltpu.VMEM((rows, rows), BF16), shape((2 * rank, rows), BF16)
-    inner_own, inner_sides = shape((2 * rank, rows), F32), shape((2 * rank, 2 * rows), F32)
 
     def own_far(texts, inner):
         return run(
@@ -301,7 +306,7 @@
     both1, s0, s1, h0, h1, inner1 = run(
         side_kernel,
         "side_rows",
-        [consts, ahead, behind, texts, twin, ups0, proj, down, up, s0, s1, h0, h1],
+        [consts, ahead, behind, texts, twin, ups0, packed, up, s0, s1, h0, h1],
         [shape((2 * rows, wide), BF16), sums, sums, narrow, narrow, inner_sides],
         [pltpu.VMEM((rows, 2 * rows), BF16)],
         6.4 * unit + 4 * pair_flops,
@@ -310,8 +315,11 @@
     s3, h3, inner1 = side_far(across_twin, ups3, inner1, s3, h3)
     inner1, far = tied(inner1, far)
     far_twin = from_ahead(far, "c", 1)
+    (far_both,) = run(embed_kernel, "embed_far", [far, packed, up], [shape((rows, wide), BF16)], [], 3.2 * unit, False)
+    far_both_twin = from_ahead(far_both, "c", 1)
     s1 = from_ahead(s1, "c", 1)
     s3 = from_ahead(s3, "c", 1)
+    inner1, far_both = tied(inner1, far_both)
     s2, h2, inner1 = side_far(across, ups2, inner1, s2, h2)
     grad_down, grad_up = run(
         shares_kernel,
@@ -322,29 +330,24 @@
         unit,
         False,
     )
-    grad_up, far_twin = tied(grad_up, far_twin)
+    grad_up, far_twin, far_both_twin = tied(grad_up, far_twin, far_both_twin)
     kept, sent, both2, w0, w2 = run(
         last_kernel,
         "far_rows",
-        [consts, far, far_twin, texts, across, ups0, ups2, proj, down, up, h0, h2, grad_down, grad_up],
+        [consts, far, far_twin, far_both, far_both_twin, texts, across, ups0, ups2, h0, h2, grad_down, grad_up],
         [grads, grads, shape((2 * rows, wide), BF16)] + [shape((rows, 2 * rows), BF16)] * 2,
         [],
-        6.4 * unit + 5 * unit,
+        5 * unit,
     )
 
     def small(kernel, name, operands, outs, scratch=()):
         return run(kernel, name, operands, outs, scratch, 1, False)
 
-    sizes = (112, 144, 128)
+    sizes = (256, 128)
     chunks = small(
         away_kernel, "away_sums", [w2, both2, s2, s3], [shape((n + (16 if k == 0 else 0), width), F32) for k, n in enumerate(sizes)]
     )
     chunks = [chunk.astype(F16) for chunk in chunks]
-
-    def beside(k, value, summed):
-        value, chunk = tied(value, chunks[k])
-        moved = from_ahead(chunk, "y", 1).astype(F32)
-        return tied(summed(value), moved)
 
     def everyones(axis):
         def summed(block):
@@ -364,14 +367,19 @@
 
     quarter = shape((rank // 4, width), F32)
     sent = from_ahead(sent, "c", 1)
-    total, c0 = beside(0, sent, scattered)
-    total = everyones(("y", "h"))(total)
-    total, c1 = beside(1, total, everyones("x"))
+    sent, *chunks = tied(sent, *chunks)
+    total = scattered(sent)
+    moved = from_ahead(chunks[0], "y", 1).astype(F32)
     (near,) = small(near_kernel, "near_sums", [w0, both2, s0, s1], [sums])
     total, near = tied(total, near)
-    total, c2 = beside(2, total, gathered)
+    total = everyones("x")(total)
+    total, c0, chunk = tied(total, moved, chunks[1])
+    total = everyones(("y", "h"))(total)
+    total, chunk = tied(total, chunk)
+    moved = from_ahead(chunk, "y", 1).astype(F32)
+    total, c1 = tied(gathered(total), moved)
     other = from_ahead(total, "c", 1)
-    (text_grad,) = small(finish_kernel, "finish", [near, c0, c1, c2], [sums])
+    (text_grad,) = small(finish_kernel, "finish", [near, c0, c1], [sums])
     grad_down, grad_up = small(join_kernel, "joined", [total, other], [grads, grads])
     grad_down = grad_down.T
     return text_grad[None], grad_down, grad_up

time: 99.4 us -> 98 us (0.986)
  Pallas kernels: 39.4 us -> 36.1 us
  starting transfers between devices: 35.7 us -> 36.9 us
    pallas_call x17 -> x18, Pallas kernels: 38.8 us -> 35.6 us  [run(): pl.pallas_call(kernel, in_specs=ins, out_specs=[spec] * len(outs), out_sh...]
    ppermute x23, starting transfers between devices: 30 us -> 31.1 us  [from_ahead(): lax.ppermute(block, axis, [((i + distance) % n, i) for i in range(n)])]
    unnamed x22 -> x18, local copies, waits for them, and re-layouts: 6.58 us -> 6.57 us
  transfers between devices with their start and end apart: 26 -> 26, of which waited for: 12 -> 11; matrix products, arithmetic and copies ran while one was open for 0% -> 0% of each run, Pallas kernels for 39% -> 36%
where the time goes in v5:
time: 98 us; the launch traced here: 97.7 us
  starting transfers between devices  36.9 us (38%)
  Pallas kernels  36.1 us (37%)
  waiting for transfers between devices  15.8 us (16%)
  local copies, waits for them, and re-layouts  6.57 us (7%)
  between operations  2.18 us (2%)
    pallas_call x18, Pallas kernels, run(): pl.pallas_call(kernel, in_specs=ins, out_specs=[spec] * len(outs), out_sh...  35.6 us
    ppermute x23, starting transfers between devices, from_ahead(): lax.ppermute(block, axis, [((i + distance) % n, i) for i in range(n)])  31.1 us
    ppermute x23, waiting for transfers between devices, from_ahead(): lax.ppermute(block, axis, [((i + distance) % n, i) for i in range(n)])  15.7 us
    unnamed x18, local copies, waits for them, and re-layouts  6.57 us
    ppermute x3, starting transfers between devices, turned(): lax.ppermute(block, ('z', 'c'), [(2 * step(z, c) + c, 2 * z + c) for z in...  5.73 us
  transfers between devices with their start and end apart: 26, of which 11 were waited for; matrix products, arithmetic and copies ran while one was open for 0% of the time, Pallas kernels for 36%

profile of v5, /device:TPU:1, one launch (start us, length us, event | category | flops | bytes accessed | tf_op | source)
XLA Modules:
  0.0 97.7 jit_solution(13468031986304326639)
XLA Ops:
  0.6 1.5 %collective-permute-start = (bf16[384,1152]{1,0:T(8,128)(2,1)}, bf16[384,1152]{1,0:T(8,128)(2,1)S(1)}, u32[]{:S(2)}, u32[]{:S(2)}) collective-permute-start(bf16[384,1152]{1,0:T(8,128)(2,1)} %bitcast.9), channel_id=1, source_target_pairs={{8,0},{0,8},{9,1},{1,9},{10,2},{2,10},{11,3},{3,11},{12,4},{4,12},... | collective-permute-start | bytes 2654216 | tf_op jit(solution)/shard_map/ppermute | solution.py:24
  3.5 1.6 %collective-permute-start.2 = (bf16[384,1152]{1,0:T(8,128)(2,1)}, bf16[384,1152]{1,0:T(8,128)(2,1)S(1)}, u32[]{:S(2)}, u32[]{:S(2)}) collective-permute-start(bf16[384,1152]{1,0:T(8,128)(2,1)} %bitcast.5), channel_id=1, source_target_pairs={{32,0},{104,8},{64,32},{8,40},{96,64},{40,72},{0,96},{72,104},{33,... | collective-permute-start | bytes 2654216 | tf_op jit(solution)/shard_map/ppermute | solution.py:258
  5.2 2.1 %collective-permute-start.3 = (bf16[384,1152]{1,0:T(8,128)(2,1)}, bf16[384,1152]{1,0:T(8,128)(2,1)S(1)}, u32[]{:S(2)}, u32[]{:S(2)}) collective-permute-start(bf16[384,1152]{1,0:T(8,128)(2,1)} %bitcast.6), channel_id=1, source_target_pairs={{96,0},{40,8},{0,32},{72,40},{32,64},{104,72},{64,96},{8,104},{97,... | collective-permute-start | bytes 2654216 | tf_op jit(solution)/shard_map/ppermute | solution.py:258
  13.0 1.7 %copy-done.7 = bf16[1152,1152]{1,0:T(8,128)(2,1)S(1)} copy-done((bf16[1152,1152]{1,0:T(8,128)(2,1)S(1)}, bf16[1152,1152]{1,0:T(8,128)(2,1)}, u32[]{:S(2)}) %copy-start.7) | copy-done | bytes 2654232
  15.7 5.5 %own_rows.1 = (bf16[384,1280]{1,0:T(8,128)(2,1)S(1)}, bf16[1152,1280]{1,0:T(8,128)(2,1)S(1)}, bf16[128,768]{1,0:T(8,128)(2,1)S(1)}, f32[384,1152]{1,0:T(8,128)S(...) custom-call(f32[3]{0:T(128)S(1)} %copy-done.6, ...), custom_call_target="tpu_custom_call" | custom-call | flops 2582013440 | bytes 13860876 | tf_op jit(solution)/shard_map/own_rows/pallas_call | solution.py:228
  21.2 2.4 %collective-permute-done.1.texts.t1 = bf16[384,1152]{1,0:T(8,128)(2,1)S(1)} collective-permute-done((bf16[384,1152]{1,0:T(8,128)(2,1)}, bf16[384,1152]{1,0:T(8,128)(2,1)S(1)}, u32[]{:S(2)}, u32[]{:S(2)}) %collective-permute-start.1) | collective-permute-done | bytes 884768 | tf_op jit(solution)/shard_map/ppermute | solution.py:24
  24.4 2.1 %own_far.2 = (bf16[128,384]{1,0:T(8,128)(2,1)S(1)}, f32[384,1152]{1,0:T(8,128)S(1)}, f32[384,128]{1,0:T(8,128)S(1)}, f32[128,384]{1,0:T(8,128)S(1)}) custom-call(f32[3]{0:T(128)S(1)} %copy-done.6, bf16[384,1280]{1,0:T(8,128)(2,1)S(1)} %get-tuple-element.71.both, bf16[384,1152]{1,0:T(8,128)(2,1)S(1)} %collective-permute-done.1.texts.t1, ...), custom_call_target="tpu_custom_call" | custom-call | flops 747424960 | bytes 4472844 | tf_op jit(solution)/shard_map/own_far/pallas_call | solution.py:228
  26.6 2.0 %collective-permute-start.5 = (bf16[384,1152]{1,0:T(8,128)(2,1)S(1)}, bf16[384,1152]{1,0:T(8,128)(2,1)S(1)}, u32[]{:S(2)}, u32[]{:S(2)}) collective-permute-start(bf16[384,1152]{1,0:T(8,128)(2,1)S(1)} %collective-permute-done.2.a), channel_id=1, source_target_pairs={{32,0},{104,8},{64,32},{8,40},{96,64},{40,72},{0,96},{72,104},{33,... | collective-permute-start | bytes 2654216 | tf_op jit(solution)/shard_map/ppermute | solution.py:258
  28.6 2.1 %own_far.3 = (bf16[128,384]{1,0:T(8,128)(2,1)S(1)}, f32[384,1152]{1,0:T(8,128)S(1)}, f32[384,128]{1,0:T(8,128)S(1)}, f32[128,384]{1,0:T(8,128)S(1)}) custom-call(f32[3]{0:T(128)S(1)} %copy-done.6, bf16[384,1280]{1,0:T(8,128)(2,1)S(1)} %get-tuple-element.71.both, bf16[384,1152]{1,0:T(8,128)(2,1)S(1)} %collective-permute-done.4.texts.t3, ...), custom_call_target="tpu_custom_call" | custom-call | flops 747424960 | bytes 4472844 | tf_op jit(solution)/shard_map/own_far/pallas_call | solution.py:228
  30.7 8.0 %side_rows.1 = (bf16[768,1280]{1,0:T(8,128)(2,1)S(1)}, f32[384,1152]{1,0:T(8,128)S(1)}, f32[384,1152]{1,0:T(8,128)S(1)}, f32[384,128]{1,0:T(8,128)S(1)}, f32[384,128]{1,0:T(8,128)S(1)}, /*index=5*/f32[128,768]{1,0:T(8,128)S(1)}) custom-call(f32[3]{0:T(128)S(1)} %copy-done.6, bf16[384,1152]{1,0:T(8,128)(2,1)S(1)} %collective-permute-done.2.a, ...), custom_call_target="tpu_custom_call" | custom-call | flops 5164026880 | bytes 17055756 | tf_op jit(solution)/shard_map/side_rows/pallas_call | solution.py:228
  38.7 2.8 %side_far.2 = (f32[384,1152]{1,0:T(8,128)S(1)}, f32[384,128]{1,0:T(8,128)S(1)}, f32[128,768]{1,0:T(8,128)S(1)}) custom-call(f32[3]{0:T(128)S(1)} %copy-done.6, bf16[768,1280]{1,0:T(8,128)(2,1)S(1)} %get-tuple-element.84.both, bf16[384,1152]{1,0:T(8,128)(2,1)S(1)} %collective-permute-done.4.texts.t3, bf16[128,384]{1,0:T(8,128)(2,1)S(1)} %get-tuple-element.87.ups, ...), custom_call_target="tpu_custom_call" | custom-call | flops 1494849920 | bytes 7667724 | tf_op jit(solution)/shard_map/side_far/pallas_call | solution.py:228
  41.5 2.6 %collective-permute-start.9 = (f32[384,1152]{1,0:T(8,128)S(1)}, f32[384,1152]{1,0:T(8,128)S(1)}, u32[]{:S(2)}, u32[]{:S(2)}) collective-permute-start(f32[384,1152]{1,0:T(8,128)S(1)} %get-tuple-element.115), channel_id=1, source_target_pairs={{8,0},{0,8},{9,1},{1,9},{10,2},{2,10},{11,3},{3,11},{12,4},{4,12},... | collective-permute-start | bytes 5308424 | tf_op jit(solution)/shard_map/ppermute | solution.py:24
  44.1 1.8 %embed_far.1.e0 = bf16[384,1280]{1,0:T(8,128)(2,1)S(1)} custom-call(bf16[384,1152]{1,0:T(8,128)(2,1)S(1)} %collective-permute-done.5.images.x0, bf16[1152,1280]{1,0:T(8,128)(2,1)S(1)} %get-tuple-element.79.packed, bf16[64,1152]{1,0:T(8,128)(2,1)S(1)} %copy-done.5), custom_call_target="tpu_custom_call" | custom-call | flops 1087163648 | bytes 4964352 | tf_op jit(solution)/shard_map/embed_far/pallas_call | solution.py:228
  46.6 2.8 %side_far.3 = (f32[384,1152]{1,0:T(8,128)S(1)}, f32[384,128]{1,0:T(8,128)S(1)}, f32[128,768]{1,0:T(8,128)S(1)}) custom-call(f32[3]{0:T(128)S(1)} %copy-done.6, bf16[768,1280]{1,0:T(8,128)(2,1)S(1)} %get-tuple-element.84.both, bf16[384,1152]{1,0:T(8,128)(2,1)S(1)} %collective-permute-done.1.texts.t1, bf16[128,384]{1,0:T(8,128)(2,1)S(1)} %get-tuple-element.94.ups.ups1, ...), custom_call_target="tpu_custom_call" | custom-call | flops 1494849920 | bytes 7667724 | tf_op jit(solution)/shard_map/side_far/pallas_call | solution.py:228
  50.5 4.7 %far_rows.1 = (f32[64,1152]{1,0:T(8,128)S(1)}, f32[64,1152]{1,0:T(8,128)S(1)}, bf16[768,1280]{1,0:T(8,128)(2,1)S(1)}, bf16[384,768]{1,0:T(8,128)(2,1)S(1)}, bf16[384,768]{1,0:T(8,128)(2,1)S(1)}) custom-call(f32[3]{0:T(128)S(1)} %copy-done.6, bf16[384,1152]{1,0:T(8,128)(2,1)S(1)} %collective-permute-done.5.images.x0, ...), custom_call_target="tpu_custom_call" | custom-call | flops 1698693120 | bytes 10518540 | tf_op jit(solution)/shard_map/far_rows/pallas_call | solution.py:228
  62.2 1.4 %collective-permute-done.11.c = f32[16,1152]{1,0:T(8,128)S(1)} collective-permute-done((f32[16,1152]{1,0:T(8,128)S(1)}, f32[16,1152]{1,0:T(8,128)S(1)}, u32[]{:S(2)}, u32[]{:S(2)}) %collective-permute-start.11) | collective-permute-done | bytes 73760 | tf_op jit(solution)/shard_map/ppermute | solution.py:24
  63.6 1.6 %collective-permute-done.12.d = f32[16,1152]{1,0:T(8,128)S(1)} collective-permute-done((f32[16,1152]{1,0:T(8,128)S(1)}, f32[16,1152]{1,0:T(8,128)S(1)}, u32[]{:S(2)}, u32[]{:S(2)}) %collective-permute-start.12) | collective-permute-done | bytes 73760 | tf_op jit(solution)/shard_map/ppermute | solution.py:24
  65.2 2.5 %collective-permute-start.14 = (f32[16,1152]{1,0:T(8,128)S(1)}, f32[16,1152]{1,0:T(8,128)S(1)}, u32[]{:S(2)}, u32[]{:S(2)}) collective-permute-start(f32[16,1152]{1,0:T(8,128)S(1)} %sums.3.a), channel_id=1, source_target_pairs={{1,0},{2,1},{3,2},{0,3},{5,4},{6,5},{7,6},{4,7},{9,8},{10,9},{11,1... | collective-permute-start | bytes 221192 | tf_op jit(solution)/shard_map/ppermute | solution.py:24
  67.8 1.7 %collective-permute-start.16 = (f32[16,1152]{1,0:T(8,128)S(1)}, f32[16,1152]{1,0:T(8,128)S(1)}, u32[]{:S(2)}, u32[]{:S(2)}) collective-permute-start(f32[16,1152]{1,0:T(8,128)S(1)} %sums.3.a), channel_id=1, source_target_pairs={{2,0},{3,1},{0,2},{1,3},{6,4},{7,5},{4,6},{5,7},{10,8},{11,9},{8,1... | collective-permute-start | bytes 221192 | tf_op jit(solution)/shard_map/ppermute | solution.py:24
  69.5 3.5 %collective-permute-done.15.c = f32[16,1152]{1,0:T(8,128)S(1)} collective-permute-done((f32[16,1152]{1,0:T(8,128)S(1)}, f32[16,1152]{1,0:T(8,128)S(1)}, u32[]{:S(2)}, u32[]{:S(2)}) %collective-permute-start.15) | collective-permute-done | bytes 73760 | tf_op jit(solution)/shard_map/ppermute | solution.py:24
  73.1 2.7 %collective-permute-start.18 = (f32[16,1152]{1,0:T(8,128)S(1)}, f32[16,1152]{1,0:T(8,128)S(1)}, u32[]{:S(2)}, u32[]{:S(2)}) collective-permute-start(f32[16,1152]{1,0:T(8,128)S(1)} %sums.4.a), channel_id=1, source_target_pairs={{4,0},{16,4},{20,16},{0,20},{5,1},{17,5},{21,17},{1,21},{6,2},{18,... | collective-permute-start | bytes 221192 | tf_op jit(solution)/shard_map/ppermute | solution.py:24
  77.9 2.3 %collective-permute-done.19.c = f32[16,1152]{1,0:T(8,128)S(1)} collective-permute-done((f32[16,1152]{1,0:T(8,128)S(1)}, f32[16,1152]{1,0:T(8,128)S(1)}, u32[]{:S(2)}, u32[]{:S(2)}) %collective-permute-start.19) | collective-permute-done | bytes 73760 | tf_op jit(solution)/shard_map/ppermute | solution.py:24
  84.1 1.9 %collective-permute-done.22.c = f32[16,1152]{1,0:T(8,128)S(1)} collective-permute-done((f32[16,1152]{1,0:T(8,128)S(1)}, f32[16,1152]{1,0:T(8,128)S(1)}, u32[]{:S(2)}, u32[]{:S(2)}) %collective-permute-start.22) | collective-permute-done | bytes 73760 | tf_op jit(solution)/shard_map/ppermute | solution.py:24
  86.9 8.6 %collective-permute-start.25 = (f32[64,1152]{1,0:T(8,128)S(1)}, f32[64,1152]{1,0:T(8,128)S(1)}, u32[]{:S(2)}, u32[]{:S(2)}) collective-permute-start(f32[64,1152]{1,0:T(8,128)S(1)} %places.1.a), channel_id=1, source_target_pairs={{8,0},{0,8},{9,1},{1,9},{10,2},{2,10},{11,3},{3,11},{12,4},{4,12},... | collective-permute-start | bytes 884744 | tf_op jit(solution)/shard_map/ppermute | solution.py:24
  (69 shorter events, 25.7 us)
Async XLA Ops:
  0.6 8.5 %collective-permute-start = (bf16[384,1152]{1,0:T(8,128)(2,1)}, bf16[384,1152]{1,0:T(8,128)(2,1)S(1)}, u32[]{:S(2)}, u32[]{:S(2)}) collective-permute-start(bf16[384,1152]{1,0:T(8,128)(2,1)} %bitcast.9), channel_id=1, source_target_pairs={{8,0},{0,8},{9,1},{1,9},{10,2},{2,10},{11,3},{3,11},{12,4},{4,12},... | collective-permute-start | bytes 2654216 | tf_op jit(solution)/shard_map/ppermute | solution.py:24
  2.1 21.4 %collective-permute-start.1 = (bf16[384,1152]{1,0:T(8,128)(2,1)}, bf16[384,1152]{1,0:T(8,128)(2,1)S(1)}, u32[]{:S(2)}, u32[]{:S(2)}) collective-permute-start(bf16[384,1152]{1,0:T(8,128)(2,1)} %bitcast.10), channel_id=1, source_target_pairs={{16,0},{0,16},{17,1},{1,17},{18,2},{2,18},{19,3},{3,19},{20,4},{4,... | collective-permute-start | bytes 2654216 | tf_op jit(solution)/shard_map/ppermute | solution.py:24
  3.5 23.0 %collective-permute-start.2 = (bf16[384,1152]{1,0:T(8,128)(2,1)}, bf16[384,1152]{1,0:T(8,128)(2,1)S(1)}, u32[]{:S(2)}, u32[]{:S(2)}) collective-permute-start(bf16[384,1152]{1,0:T(8,128)(2,1)} %bitcast.5), channel_id=1, source_target_pairs={{32,0},{104,8},{64,32},{8,40},{96,64},{40,72},{0,96},{72,104},{33,... | collective-permute-start | bytes 2654216 | tf_op jit(solution)/shard_map/ppermute | solution.py:258
  5.2 21.4 %collective-permute-start.3 = (bf16[384,1152]{1,0:T(8,128)(2,1)}, bf16[384,1152]{1,0:T(8,128)(2,1)S(1)}, u32[]{:S(2)}, u32[]{:S(2)}) collective-permute-start(bf16[384,1152]{1,0:T(8,128)(2,1)} %bitcast.6), channel_id=1, source_target_pairs={{96,0},{40,8},{0,32},{72,40},{32,64},{104,72},{64,96},{8,104},{97,... | collective-permute-start | bytes 2654216 | tf_op jit(solution)/shard_map/ppermute | solution.py:258
  26.6 17.5 %collective-permute-start.5 = (bf16[384,1152]{1,0:T(8,128)(2,1)S(1)}, bf16[384,1152]{1,0:T(8,128)(2,1)S(1)}, u32[]{:S(2)}, u32[]{:S(2)}) collective-permute-start(bf16[384,1152]{1,0:T(8,128)(2,1)S(1)} %collective-permute-done.2.a), channel_id=1, source_target_pairs={{32,0},{104,8},{64,32},{8,40},{96,64},{40,72},{0,96},{72,104},{33,... | collective-permute-start | bytes 2654216 | tf_op jit(solution)/shard_map/ppermute | solution.py:258
  41.5 14.2 %collective-permute-start.9 = (f32[384,1152]{1,0:T(8,128)S(1)}, f32[384,1152]{1,0:T(8,128)S(1)}, u32[]{:S(2)}, u32[]{:S(2)}) collective-permute-start(f32[384,1152]{1,0:T(8,128)S(1)} %get-tuple-element.115), channel_id=1, source_target_pairs={{8,0},{0,8},{9,1},{1,9},{10,2},{2,10},{11,3},{3,11},{12,4},{4,12},... | collective-permute-start | bytes 5308424 | tf_op jit(solution)/shard_map/ppermute | solution.py:24
  45.9 4.6 %collective-permute-start.7 = (bf16[384,1280]{1,0:T(8,128)(2,1)S(1)}, bf16[384,1280]{1,0:T(8,128)(2,1)S(1)}, u32[]{:S(2)}, u32[]{:S(2)}) collective-permute-start(bf16[384,1280]{1,0:T(8,128)(2,1)S(1)} %embed_far.1.e0), channel_id=1, source_target_pairs={{8,0},{0,8},{9,1},{1,9},{10,2},{2,10},{11,3},{3,11},{12,4},{4,12},... | collective-permute-start | bytes 2949128 | tf_op jit(solution)/shard_map/ppermute | solution.py:24
  46.0 4.5 %collective-permute-start.6 = (bf16[384,1152]{1,0:T(8,128)(2,1)S(1)}, bf16[384,1152]{1,0:T(8,128)(2,1)S(1)}, u32[]{:S(2)}, u32[]{:S(2)}) collective-permute-start(bf16[384,1152]{1,0:T(8,128)(2,1)S(1)} %collective-permute-done.5.images.x0), channel_id=1, source_target_pairs={{8,0},{0,8},{9,1},{1,9},{10,2},{2,10},{11,3},{3,11},{12,4},{4,12},... | collective-permute-start | bytes 2654216 | tf_op jit(solution)/shard_map/ppermute | solution.py:24
  46.5 14.6 %collective-permute-start.13 = (f32[384,1152]{1,0:T(8,128)S(1)}, f32[384,1152]{1,0:T(8,128)S(1)}, u32[]{:S(2)}, u32[]{:S(2)}) collective-permute-start(f32[384,1152]{1,0:T(8,128)S(1)} %get-tuple-element.125), channel_id=1, source_target_pairs={{8,0},{0,8},{9,1},{1,9},{10,2},{2,10},{11,3},{3,11},{12,4},{4,12},... | collective-permute-start | bytes 5308424 | tf_op jit(solution)/shard_map/ppermute | solution.py:24
  57.3 15.8 %collective-permute-start.17 = (f16[272,1152]{1,0:T(8,128)(2,1)S(1)}, f16[272,1152]{1,0:T(8,128)(2,1)S(1)}, u32[]{:S(2)}, u32[]{:S(2)}) collective-permute-start(f16[272,1152]{1,0:T(8,128)(2,1)S(1)} %convert_element_type.12), channel_id=1, source_target_pairs={{16,0},{0,16},{17,1},{1,17},{18,2},{2,18},{19,3},{3,19},{20,4},{4,... | collective-permute-start | bytes 1880072 | tf_op jit(solution)/shard_map/ppermute | solution.py:24
  58.6 3.6 %collective-permute-start.10 = (f32[16,1152]{1,0:T(8,128)S(1)}, f32[16,1152]{1,0:T(8,128)S(1)}, u32[]{:S(2)}, u32[]{:S(2)}) collective-permute-start(f32[16,1152]{1,0:T(8,128)S(1)} %get-tuple-element.120), channel_id=1, source_target_pairs={{32,0},{64,32},{96,64},{0,96},{33,1},{65,33},{97,65},{1,97},{34,2}... | collective-permute-start | bytes 221192 | tf_op jit(solution)/shard_map/ppermute | solution.py:24
  59.2 4.4 %collective-permute-start.11 = (f32[16,1152]{1,0:T(8,128)S(1)}, f32[16,1152]{1,0:T(8,128)S(1)}, u32[]{:S(2)}, u32[]{:S(2)}) collective-permute-start(f32[16,1152]{1,0:T(8,128)S(1)} %get-tuple-element.121), channel_id=1, source_target_pairs={{96,0},{0,32},{32,64},{64,96},{97,1},{1,33},{33,65},{65,97},{98,2}... | collective-permute-start | bytes 221192 | tf_op jit(solution)/shard_map/ppermute | solution.py:24
  60.1 5.1 %collective-permute-start.12 = (f32[16,1152]{1,0:T(8,128)S(1)}, f32[16,1152]{1,0:T(8,128)S(1)}, u32[]{:S(2)}, u32[]{:S(2)}) collective-permute-start(f32[16,1152]{1,0:T(8,128)S(1)} %get-tuple-element.122), channel_id=1, source_target_pairs={{64,0},{96,32},{0,64},{32,96},{65,1},{97,33},{1,65},{33,97},{66,2}... | collective-permute-start | bytes 221192 | tf_op jit(solution)/shard_map/ppermute | solution.py:24
  65.2 4.3 %collective-permute-start.14 = (f32[16,1152]{1,0:T(8,128)S(1)}, f32[16,1152]{1,0:T(8,128)S(1)}, u32[]{:S(2)}, u32[]{:S(2)}) collective-permute-start(f32[16,1152]{1,0:T(8,128)S(1)} %sums.3.a), channel_id=1, source_target_pairs={{1,0},{2,1},{3,2},{0,3},{5,4},{6,5},{7,6},{4,7},{9,8},{10,9},{11,1... | collective-permute-start | bytes 221192 | tf_op jit(solution)/shard_map/ppermute | solution.py:24
  67.8 5.2 %collective-permute-start.15 = (f32[16,1152]{1,0:T(8,128)S(1)}, f32[16,1152]{1,0:T(8,128)S(1)}, u32[]{:S(2)}, u32[]{:S(2)}) collective-permute-start(f32[16,1152]{1,0:T(8,128)S(1)} %sums.3.a), channel_id=1, source_target_pairs={{3,0},{0,1},{1,2},{2,3},{7,4},{4,5},{5,6},{6,7},{11,8},{8,9},{9,10... | collective-permute-start | bytes 221192 | tf_op jit(solution)/shard_map/ppermute | solution.py:24
  67.8 5.2 %collective-permute-start.16 = (f32[16,1152]{1,0:T(8,128)S(1)}, f32[16,1152]{1,0:T(8,128)S(1)}, u32[]{:S(2)}, u32[]{:S(2)}) collective-permute-start(f32[16,1152]{1,0:T(8,128)S(1)} %sums.3.a), channel_id=1, source_target_pairs={{2,0},{3,1},{0,2},{1,3},{6,4},{7,5},{4,6},{5,7},{10,8},{11,9},{8,1... | collective-permute-start | bytes 221192 | tf_op jit(solution)/shard_map/ppermute | solution.py:24
  73.1 4.8 %collective-permute-start.18 = (f32[16,1152]{1,0:T(8,128)S(1)}, f32[16,1152]{1,0:T(8,128)S(1)}, u32[]{:S(2)}, u32[]{:S(2)}) collective-permute-start(f32[16,1152]{1,0:T(8,128)S(1)} %sums.4.a), channel_id=1, source_target_pairs={{4,0},{16,4},{20,16},{0,20},{5,1},{17,5},{21,17},{1,21},{6,2},{18,... | collective-permute-start | bytes 221192 | tf_op jit(solution)/shard_map/ppermute | solution.py:24
  75.8 4.4 %collective-permute-start.19 = (f32[16,1152]{1,0:T(8,128)S(1)}, f32[16,1152]{1,0:T(8,128)S(1)}, u32[]{:S(2)}, u32[]{:S(2)}) collective-permute-start(f32[16,1152]{1,0:T(8,128)S(1)} %sums.4.a), channel_id=1, source_target_pairs={{20,0},{0,4},{4,16},{16,20},{21,1},{1,5},{5,17},{17,21},{22,2},{2,... | collective-permute-start | bytes 221192 | tf_op jit(solution)/shard_map/ppermute | solution.py:24
  76.2 4.0 %collective-permute-start.20 = (f32[16,1152]{1,0:T(8,128)S(1)}, f32[16,1152]{1,0:T(8,128)S(1)}, u32[]{:S(2)}, u32[]{:S(2)}) collective-permute-start(f32[16,1152]{1,0:T(8,128)S(1)} %sums.4.a), channel_id=1, source_target_pairs={{16,0},{20,4},{0,16},{4,20},{17,1},{21,5},{1,17},{5,21},{18,2},{22... | collective-permute-start | bytes 221192 | tf_op jit(solution)/shard_map/ppermute | solution.py:24
  80.2 6.6 %collective-permute-start.24 = (f16[128,1152]{1,0:T(8,128)(2,1)S(1)}, f16[128,1152]{1,0:T(8,128)(2,1)S(1)}, u32[]{:S(2)}, u32[]{:S(2)}) collective-permute-start(f16[128,1152]{1,0:T(8,128)(2,1)S(1)} %convert_element_type.13), channel_id=1, source_target_pairs={{16,0},{0,16},{17,1},{1,17},{18,2},{2,18},{19,3},{3,19},{20,4},{4,... | collective-permute-start | bytes 884744 | tf_op jit(solution)/shard_map/ppermute | solution.py:24
  80.6 3.5 %collective-permute-start.21 = (f32[16,1152]{1,0:T(8,128)S(1)}, f32[16,1152]{1,0:T(8,128)S(1)}, u32[]{:S(2)}, u32[]{:S(2)}) collective-permute-start(f32[16,1152]{1,0:T(8,128)S(1)} %sums.5.a), channel_id=1, source_target_pairs={{32,0},{64,32},{96,64},{0,96},{33,1},{65,33},{97,65},{1,97},{34,2}... | collective-permute-start | bytes 221192 | tf_op jit(solution)/shard_map/ppermute | solution.py:24
  81.6 4.4 %collective-permute-start.22 = (f32[16,1152]{1,0:T(8,128)S(1)}, f32[16,1152]{1,0:T(8,128)S(1)}, u32[]{:S(2)}, u32[]{:S(2)}) collective-permute-start(f32[16,1152]{1,0:T(8,128)S(1)} %sums.5.a), channel_id=1, source_target_pairs={{96,0},{0,32},{32,64},{64,96},{97,1},{1,33},{33,65},{65,97},{98,2}... | collective-permute-start | bytes 221192 | tf_op jit(solution)/shard_map/ppermute | solution.py:24
  82.1 4.7 %collective-permute-start.23 = (f32[16,1152]{1,0:T(8,128)S(1)}, f32[16,1152]{1,0:T(8,128)S(1)}, u32[]{:S(2)}, u32[]{:S(2)}) collective-permute-start(f32[16,1152]{1,0:T(8,128)S(1)} %sums.5.a), channel_id=1, source_target_pairs={{64,0},{96,32},{0,64},{32,96},{65,1},{97,33},{1,65},{33,97},{66,2}... | collective-permute-start | bytes 221192 | tf_op jit(solution)/shard_map/ppermute | solution.py:24
  86.9 9.9 %collective-permute-start.25 = (f32[64,1152]{1,0:T(8,128)S(1)}, f32[64,1152]{1,0:T(8,128)S(1)}, u32[]{:S(2)}, u32[]{:S(2)}) collective-permute-start(f32[64,1152]{1,0:T(8,128)S(1)} %places.1.a), channel_id=1, source_target_pairs={{8,0},{0,8},{9,1},{1,9},{10,2},{2,10},{11,3},{3,11},{12,4},{4,12},... | collective-permute-start | bytes 884744 | tf_op jit(solution)/shard_map/ppermute | solution.py:24
  (11 other events, 22.7 us)

commit v6 on v5

--- a/solution.py
+++ b/solution.py
@@ -105,14 +105,13 @@
         inner[...] = inner[...] + part if k else part
 
 
-def side_kernel(consts, a, b, t0, t1, ups, packed, up, s0, s1, h0, h1, both, o0, o1, g0, g1, inner, w):
+def side_kernel(consts, a, b, t0, t1, ups, packed, up, h0, h1, both, g0, g1, inner, w0, w1):
     width, rows = up.shape[1], a.shape[0]
     embed(a, 0, both, packed, up)
     embed(b, rows, both, packed, up)
-    for k, (texts, s, h, o, g) in enumerate(((t0, s0, h0, o0, g0), (t1, s1, h1, o1, g1))):
+    for k, (texts, h, g, w) in enumerate(((t0, h0, g0, w0), (t1, h1, g1, w1))):
         w[...] = gate(mm_nt(texts[...], both[:, :width]), consts)
-        sums = mm(w[...], both[...])
-        o[...], g[...] = s[...] + sums[:, :width], h[...] + sums[:, width:]
+        g[...] = h[...] + mm(w[...], both[:, width:])
         part = mm(ups[:, k * rows : (k + 1) * rows], w[...])
         inner[...] = inner[...] + part if k else part
 
@@ -169,8 +168,13 @@
     sent[...] = jnp.where(first, up_sum, down_sum)
 
 
-def near_kernel(w, both, s, twin, out):
-    out[...] = s[...] + twin[...] + mm(w[...], both[:, : s.shape[1]])
+def twin_kernel(w, both, s, out):
+    out[...] = s[...] + mm(w[...], both[:, : s.shape[1]])
+
+
+def near_kernel(w0, both0, w1, both1, s, twin, out):
+    width = s.shape[1]
+    out[...] = s[...] + twin[...] + mm(w0[...], both0[:, :width]) + mm(w1[...], both1[:, :width])
 
 
 def away_kernel(w, both, s, twin, *outs):
@@ -248,6 +252,7 @@
         in_specs=[scalar, scalar],
         out_specs=scalar,
         out_shape=jax.ShapeDtypeStruct((3,), F32),
+        compiler_params=pltpu.CompilerParams(vmem_limit_bytes=MIB),
         name="consts",
     )(scale, offset)
     down = down.T
@@ -303,13 +308,13 @@
     ups2, s2, h2, inner0 = own_far(across, inner0)
     inner0, ahead, behind, across_twin = tied(inner0, ahead, behind, across_twin)
     far = turned(ahead, 1)
-    both1, s0, s1, h0, h1, inner1 = run(
+    both1, h0, h1, inner1, w_near, w_twin = run(
         side_kernel,
         "side_rows",
-        [consts, ahead, behind, texts, twin, ups0, packed, up, s0, s1, h0, h1],
-        [shape((2 * rows, wide), BF16), sums, sums, narrow, narrow, inner_sides],
-        [pltpu.VMEM((rows, 2 * rows), BF16)],
-        6.4 * unit + 4 * pair_flops,
+        [consts, ahead, behind, texts, twin, ups0, packed, up, h0, h1],
+        [shape((2 * rows, wide), BF16), narrow, narrow, inner_sides] + [shape((rows, 2 * rows), BF16)] * 2,
+        [],
+        6.4 * unit + 2 * pair_flops,
     )
     ups3, s3, h3, inner0 = own_far(across_twin, inner0)
     s3, h3, inner1 = side_far(across_twin, ups3, inner1, s3, h3)
@@ -317,7 +322,6 @@
     far_twin = from_ahead(far, "c", 1)
     (far_both,) = run(embed_kernel, "embed_far", [far, packed, up], [shape((rows, wide), BF16)], [], 3.2 * unit, False)
     far_both_twin = from_ahead(far_both, "c", 1)
-    s1 = from_ahead(s1, "c", 1)
     s3 = from_ahead(s3, "c", 1)
     inner1, far_both = tied(inner1, far_both)
     s2, h2, inner1 = side_far(across, ups2, inner1, s2, h2)
@@ -343,7 +347,7 @@
     def small(kernel, name, operands, outs, scratch=()):
         return run(kernel, name, operands, outs, scratch, 1, False)
 
-    sizes = (256, 128)
+    sizes = (304, 80)
     chunks = small(
         away_kernel, "away_sums", [w2, both2, s2, s3], [shape((n + (16 if k == 0 else 0), width), F32) for k, n in enumerate(sizes)]
     )
@@ -370,14 +374,16 @@
     sent, *chunks = tied(sent, *chunks)
     total = scattered(sent)
     moved = from_ahead(chunks[0], "y", 1).astype(F32)
-    (near,) = small(near_kernel, "near_sums", [w0, both2, s0, s1], [sums])
-    total, near = tied(total, near)
+    (s1,) = small(twin_kernel, "twin_sums", [w_twin, both1, s1], [sums])
     total = everyones("x")(total)
-    total, c0, chunk = tied(total, moved, chunks[1])
+    total, c0, s1, chunk = tied(total, moved, s1, chunks[1])
+    s1 = from_ahead(s1, "c", 1)
     total = everyones(("y", "h"))(total)
-    total, chunk = tied(total, chunk)
+    total, chunk, s1 = tied(total, chunk, s1)
     moved = from_ahead(chunk, "y", 1).astype(F32)
-    total, c1 = tied(gathered(total), moved)
+    total = gathered(total)
+    (near,) = small(near_kernel, "near_sums", [w_near, both1, w0, both2, s0, s1], [sums])
+    total, c1, near = tied(total, moved, near)
     other = from_ahead(total, "c", 1)
     (text_grad,) = small(finish_kernel, "finish", [near, c0, c1], [sums])
     grad_down, grad_up = small(join_kernel, "joined", [total, other], [grads, grads])

time: 98 us -> 97.2 us (level)
  starting transfers between devices: 36.9 us -> 34.6 us
  waiting for transfers between devices: 15.8 us -> 17.3 us
    ppermute x23, starting transfers between devices: 31.1 us -> 28.9 us  [from_ahead(): lax.ppermute(block, axis, [((i + distance) % n, i) for i in range(n)])]
    ppermute x23, waiting for transfers between devices: 15.7 us -> 17.3 us  [from_ahead(): lax.ppermute(block, axis, [((i + distance) % n, i) for i in range(n)])]
    unnamed x18 -> x16, local copies, waits for them, and re-layouts: 6.57 us -> 5.91 us
    pallas_call x18 -> x19, Pallas kernels: 35.6 us -> 36 us  [run(): pl.pallas_call(kernel, in_specs=ins, out_specs=[spec] * len(outs), out_sh...]
  transfers between devices with their start and end apart: 26 -> 26, of which waited for: 11 -> 10; matrix products, arithmetic and copies ran while one was open for 0% -> 0% of each run, Pallas kernels for 36% -> 37%
where the time goes in v6:
time: 97.2 us; the launch traced here: 96.9 us
  Pallas kernels  36.6 us (38%)
  starting transfers between devices  34.6 us (36%)
  waiting for transfers between devices  17.3 us (18%)
  local copies, waits for them, and re-layouts  5.91 us (6%)
  between operations  2.2 us (2%)
    pallas_call x19, Pallas kernels, run(): pl.pallas_call(kernel, in_specs=ins, out_specs=[spec] * len(outs), out_sh...  36 us
    ppermute x23, starting transfers between devices, from_ahead(): lax.ppermute(block, axis, [((i + distance) % n, i) for i in range(n)])  28.9 us
    ppermute x23, waiting for transfers between devices, from_ahead(): lax.ppermute(block, axis, [((i + distance) % n, i) for i in range(n)])  17.3 us
    unnamed x16, local copies, waits for them, and re-layouts  5.91 us
    ppermute x3, starting transfers between devices, turned(): lax.ppermute(block, ('z', 'c'), [(2 * step(z, c) + c, 2 * z + c) for z in...  5.73 us
  transfers between devices with their start and end apart: 26, of which 10 were waited for; matrix products, arithmetic and copies ran while one was open for 0% of the time, Pallas kernels for 37%

profile of v6, /device:TPU:1, one launch (start us, length us, event | category | flops | bytes accessed | tf_op | source)
XLA Modules:
  0.0 96.9 jit_solution(6933625851435017650)
XLA Ops:
  5.2 2.1 %collective-permute-start.3 = (bf16[384,1152]{1,0:T(8,128)(2,1)}, bf16[384,1152]{1,0:T(8,128)(2,1)S(1)}, u32[]{:S(2)}, u32[]{:S(2)}) collective-permute-start(bf16[384,1152]{1,0:T(8,128)(2,1)} %bitcast.6), channel_id=1, source_target_pairs={{96,0},{40,8},{0,32},{72,40},{32,64},{104,72},{64,96},{8,104},{97,... | collective-permute-start | bytes 2654216 | tf_op jit(solution)/shard_map/ppermute | solution.py:263
  12.4 1.7 %copy-done.6 = bf16[1152,1152]{1,0:T(8,128)(2,1)S(1)} copy-done((bf16[1152,1152]{1,0:T(8,128)(2,1)S(1)}, bf16[1152,1152]{1,0:T(8,128)(2,1)}, u32[]{:S(2)}) %copy-start.6) | copy-done | bytes 2654232
  15.1 5.5 %own_rows.1 = (bf16[384,1280]{1,0:T(8,128)(2,1)S(1)}, bf16[1152,1280]{1,0:T(8,128)(2,1)S(1)}, bf16[128,768]{1,0:T(8,128)(2,1)S(1)}, f32[384,1152]{1,0:T(8,128)S(...) custom-call(f32[3]{0:T(128)S(1)} %consts.1, ...), custom_call_target="tpu_custom_call" | custom-call | flops 2582013440 | bytes 13860876 | tf_op jit(solution)/shard_map/own_rows/pallas_call | solution.py:232
  20.6 3.0 %collective-permute-done.1.texts.t1 = bf16[384,1152]{1,0:T(8,128)(2,1)S(1)} collective-permute-done((bf16[384,1152]{1,0:T(8,128)(2,1)}, bf16[384,1152]{1,0:T(8,128)(2,1)S(1)}, u32[]{:S(2)}, u32[]{:S(2)}) %collective-permute-start.1) | collective-permute-done | bytes 884768 | tf_op jit(solution)/shard_map/ppermute | solution.py:24
  24.4 2.1 %own_far.2 = (bf16[128,384]{1,0:T(8,128)(2,1)S(1)}, f32[384,1152]{1,0:T(8,128)S(1)}, f32[384,128]{1,0:T(8,128)S(1)}, f32[128,384]{1,0:T(8,128)S(1)}) custom-call(f32[3]{0:T(128)S(1)} %consts.1, bf16[384,1280]{1,0:T(8,128)(2,1)S(1)} %get-tuple-element.72.both, bf16[384,1152]{1,0:T(8,128)(2,1)S(1)} %collective-permute-done.1.texts.t1, ...), custom_call_target="tpu_custom_call" | custom-call | flops 747424960 | bytes 4472844 | tf_op jit(solution)/shard_map/own_far/pallas_call | solution.py:232
  26.6 2.0 %collective-permute-start.5 = (bf16[384,1152]{1,0:T(8,128)(2,1)S(1)}, bf16[384,1152]{1,0:T(8,128)(2,1)S(1)}, u32[]{:S(2)}, u32[]{:S(2)}) collective-permute-start(bf16[384,1152]{1,0:T(8,128)(2,1)S(1)} %collective-permute-done.2.a), channel_id=1, source_target_pairs={{32,0},{104,8},{64,32},{8,40},{96,64},{40,72},{0,96},{72,104},{33,... | collective-permute-start | bytes 2654216 | tf_op jit(solution)/shard_map/ppermute | solution.py:263
  28.5 2.1 %own_far.3 = (bf16[128,384]{1,0:T(8,128)(2,1)S(1)}, f32[384,1152]{1,0:T(8,128)S(1)}, f32[384,128]{1,0:T(8,128)S(1)}, f32[128,384]{1,0:T(8,128)S(1)}) custom-call(f32[3]{0:T(128)S(1)} %consts.1, bf16[384,1280]{1,0:T(8,128)(2,1)S(1)} %get-tuple-element.72.both, bf16[384,1152]{1,0:T(8,128)(2,1)S(1)} %collective-permute-done.4.texts.t3, ...), custom_call_target="tpu_custom_call" | custom-call | flops 747424960 | bytes 4472844 | tf_op jit(solution)/shard_map/own_far/pallas_call | solution.py:232
  30.7 6.7 %side_rows.1 = (bf16[768,1280]{1,0:T(8,128)(2,1)S(1)}, f32[384,128]{1,0:T(8,128)S(1)}, f32[384,128]{1,0:T(8,128)S(1)}, f32[128,768]{1,0:T(8,128)S(1)}, bf16[384,...) custom-call(f32[3]{0:T(128)S(1)} %consts.1, bf16[384,1152]{1,0:T(8,128)(2,1)S(1)} %collective-permute-done.2.a, ...), custom_call_target="tpu_custom_call" | custom-call | flops 3669177088 | bytes 11157516 | tf_op jit(solution)/shard_map/side_rows/pallas_call | solution.py:232
  37.4 2.8 %side_far.2 = (f32[384,1152]{1,0:T(8,128)S(1)}, f32[384,128]{1,0:T(8,128)S(1)}, f32[128,768]{1,0:T(8,128)S(1)}) custom-call(f32[3]{0:T(128)S(1)} %consts.1, bf16[768,1280]{1,0:T(8,128)(2,1)S(1)} %get-tuple-element.83.both.both0, bf16[384,1152]{1,0:T(8,128)(2,1)S(1)} %collective-permute-done.4.texts.t3, bf16[128,384]{1,0:T(8,128)(2,1)S(1)} %get-tuple-element.86.ups, ...), custom_call_target="tpu_custom_call" | custom-call | flops 1494849920 | bytes 7667724 | tf_op jit(solution)/shard_map/side_far/pallas_call | solution.py:232
  40.2 2.6 %collective-permute-start.9 = (f32[384,1152]{1,0:T(8,128)S(1)}, f32[384,1152]{1,0:T(8,128)S(1)}, u32[]{:S(2)}, u32[]{:S(2)}) collective-permute-start(f32[384,1152]{1,0:T(8,128)S(1)} %get-tuple-element.114), channel_id=1, source_target_pairs={{8,0},{0,8},{9,1},{1,9},{10,2},{2,10},{11,3},{3,11},{12,4},{4,12},... | collective-permute-start | bytes 5308424 | tf_op jit(solution)/shard_map/ppermute | solution.py:24
  42.8 1.8 %embed_far.1.e0 = bf16[384,1280]{1,0:T(8,128)(2,1)S(1)} custom-call(bf16[384,1152]{1,0:T(8,128)(2,1)S(1)} %collective-permute-done.5.images.x0, bf16[1152,1280]{1,0:T(8,128)(2,1)S(1)} %get-tuple-element.80.packed, bf16[64,1152]{1,0:T(8,128)(2,1)S(1)} %copy-done.5), custom_call_target="tpu_custom_call" | custom-call | flops 1087163648 | bytes 4964352 | tf_op jit(solution)/shard_map/embed_far/pallas_call | solution.py:232
  45.2 2.8 %side_far.3 = (f32[384,1152]{1,0:T(8,128)S(1)}, f32[384,128]{1,0:T(8,128)S(1)}, f32[128,768]{1,0:T(8,128)S(1)}) custom-call(f32[3]{0:T(128)S(1)} %consts.1, bf16[768,1280]{1,0:T(8,128)(2,1)S(1)} %get-tuple-element.83.both.both0, bf16[384,1152]{1,0:T(8,128)(2,1)S(1)} %collective-permute-done.1.texts.t1, bf16[128,384]{1,0:T(8,128)(2,1)S(1)} %get-tuple-element.93.ups.ups1, ...), custom_call_target="tpu_custom_call" | custom-call | flops 1494849920 | bytes 7667724 | tf_op jit(solution)/shard_map/side_far/pallas_call | solution.py:232
  49.1 4.7 %far_rows.1 = (f32[64,1152]{1,0:T(8,128)S(1)}, f32[64,1152]{1,0:T(8,128)S(1)}, bf16[768,1280]{1,0:T(8,128)(2,1)S(1)}, bf16[384,768]{1,0:T(8,128)(2,1)S(1)}, bf16[384,768]{1,0:T(8,128)(2,1)S(1)}) custom-call(f32[3]{0:T(128)S(1)} %consts.1, bf16[384,1152]{1,0:T(8,128)(2,1)S(1)} %collective-permute-done.5.images.x0, ...), custom_call_target="tpu_custom_call" | custom-call | flops 1698693120 | bytes 10518540 | tf_op jit(solution)/shard_map/far_rows/pallas_call | solution.py:232
  57.1 2.0 %collective-permute-start.10 = (f32[16,1152]{1,0:T(8,128)S(1)}, f32[16,1152]{1,0:T(8,128)S(1)}, u32[]{:S(2)}, u32[]{:S(2)}) collective-permute-start(f32[16,1152]{1,0:T(8,128)S(1)} %get-tuple-element.119), channel_id=1, source_target_pairs={{32,0},{64,32},{96,64},{0,96},{33,1},{65,33},{97,65},{1,97},{34,2}... | collective-permute-start | bytes 221192 | tf_op jit(solution)/shard_map/ppermute | solution.py:24
  60.6 5.0 %collective-permute-done.11.c = f32[16,1152]{1,0:T(8,128)S(1)} collective-permute-done((f32[16,1152]{1,0:T(8,128)S(1)}, f32[16,1152]{1,0:T(8,128)S(1)}, u32[]{:S(2)}, u32[]{:S(2)}) %collective-permute-start.11) | collective-permute-done | bytes 73760 | tf_op jit(solution)/shard_map/ppermute | solution.py:24
  65.6 2.5 %collective-permute-start.13 = (f32[16,1152]{1,0:T(8,128)S(1)}, f32[16,1152]{1,0:T(8,128)S(1)}, u32[]{:S(2)}, u32[]{:S(2)}) collective-permute-start(f32[16,1152]{1,0:T(8,128)S(1)} %sums.3.a), channel_id=1, source_target_pairs={{1,0},{2,1},{3,2},{0,3},{5,4},{6,5},{7,6},{4,7},{9,8},{10,9},{11,1... | collective-permute-start | bytes 221192 | tf_op jit(solution)/shard_map/ppermute | solution.py:24
  70.9 2.5 %collective-permute-done.14.c = f32[16,1152]{1,0:T(8,128)S(1)} collective-permute-done((f32[16,1152]{1,0:T(8,128)S(1)}, f32[16,1152]{1,0:T(8,128)S(1)}, u32[]{:S(2)}, u32[]{:S(2)}) %collective-permute-start.14) | collective-permute-done | bytes 73760 | tf_op jit(solution)/shard_map/ppermute | solution.py:24
  73.9 2.1 %collective-permute-start.20 = (f32[384,1152]{1,0:T(8,128)S(1)}, f32[384,1152]{1,0:T(8,128)S(1)}, u32[]{:S(2)}, u32[]{:S(2)}) collective-permute-start(f32[384,1152]{1,0:T(8,128)S(1)} %twin_sums.1), channel_id=1, source_target_pairs={{8,0},{0,8},{9,1},{1,9},{10,2},{2,10},{11,3},{3,11},{12,4},{4,12},... | collective-permute-start | bytes 5308424 | tf_op jit(solution)/shard_map/ppermute | solution.py:24
  76.0 1.9 %collective-permute-start.17 = (f32[16,1152]{1,0:T(8,128)S(1)}, f32[16,1152]{1,0:T(8,128)S(1)}, u32[]{:S(2)}, u32[]{:S(2)}) collective-permute-start(f32[16,1152]{1,0:T(8,128)S(1)} %sums.4.a), channel_id=1, source_target_pairs={{4,0},{16,4},{20,16},{0,20},{5,1},{17,5},{21,17},{1,21},{6,2},{18,... | collective-permute-start | bytes 221192 | tf_op jit(solution)/shard_map/ppermute | solution.py:24
  79.3 2.0 %collective-permute-done.17.b = f32[16,1152]{1,0:T(8,128)S(1)} collective-permute-done((f32[16,1152]{1,0:T(8,128)S(1)}, f32[16,1152]{1,0:T(8,128)S(1)}, u32[]{:S(2)}, u32[]{:S(2)}) %collective-permute-start.17) | collective-permute-done | bytes 73760 | tf_op jit(solution)/shard_map/ppermute | solution.py:24
  84.2 2.2 %collective-permute-start.21 = (f32[16,1152]{1,0:T(8,128)S(1)}, f32[16,1152]{1,0:T(8,128)S(1)}, u32[]{:S(2)}, u32[]{:S(2)}) collective-permute-start(f32[16,1152]{1,0:T(8,128)S(1)} %sums.5.a), channel_id=1, source_target_pairs={{32,0},{64,32},{96,64},{0,96},{33,1},{65,33},{97,65},{1,97},{34,2}... | collective-permute-start | bytes 221192 | tf_op jit(solution)/shard_map/ppermute | solution.py:24
  87.6 1.7 %near_sums.1.near = f32[384,1152]{1,0:T(8,128)S(1)} custom-call(bf16[384,768]{1,0:T(8,128)(2,1)S(1)} %get-tuple-element.131.w0, bf16[768,1280]{1,0:T(8,128)(2,1)S(1)} %get-tuple-element.83.both.both0, bf16[384,768]{1,0:T(8,128)(2,1)S(1)} %get-tuple-element.132.w1, bf16[768,1280]{1,0:T(8,128)(2,1)S(1)} %get-tuple-element.112.both.both1, ...), custom_call_target="tpu_custom_call" | custom-call | flops 1 | bytes 10420224 | tf_op jit(solution)/shard_map/near_sums/pallas_call | solution.py:232
  89.3 2.1 %collective-permute-done.22.c = f32[16,1152]{1,0:T(8,128)S(1)} collective-permute-done((f32[16,1152]{1,0:T(8,128)S(1)}, f32[16,1152]{1,0:T(8,128)S(1)}, u32[]{:S(2)}, u32[]{:S(2)}) %collective-permute-start.22) | collective-permute-done | bytes 73760 | tf_op jit(solution)/shard_map/ppermute | solution.py:24
  91.8 2.8 %collective-permute-start.25 = (f32[64,1152]{1,0:T(8,128)S(1)}, f32[64,1152]{1,0:T(8,128)S(1)}, u32[]{:S(2)}, u32[]{:S(2)}) collective-permute-start(f32[64,1152]{1,0:T(8,128)S(1)} %places.1.a), channel_id=1, source_target_pairs={{8,0},{0,8},{9,1},{1,9},{10,2},{2,10},{11,3},{3,11},{12,4},{4,12},... | collective-permute-start | bytes 884744 | tf_op jit(solution)/shard_map/ppermute | solution.py:24
  (68 shorter events, 27.9 us)
Async XLA Ops:
  0.6 8.6 %collective-permute-start = (bf16[384,1152]{1,0:T(8,128)(2,1)}, bf16[384,1152]{1,0:T(8,128)(2,1)S(1)}, u32[]{:S(2)}, u32[]{:S(2)}) collective-permute-start(bf16[384,1152]{1,0:T(8,128)(2,1)} %bitcast.9), channel_id=1, source_target_pairs={{8,0},{0,8},{9,1},{1,9},{10,2},{2,10},{11,3},{3,11},{12,4},{4,12},... | collective-permute-start | bytes 2654216 | tf_op jit(solution)/shard_map/ppermute | solution.py:24
  2.1 21.4 %collective-permute-start.1 = (bf16[384,1152]{1,0:T(8,128)(2,1)}, bf16[384,1152]{1,0:T(8,128)(2,1)S(1)}, u32[]{:S(2)}, u32[]{:S(2)}) collective-permute-start(bf16[384,1152]{1,0:T(8,128)(2,1)} %bitcast.10), channel_id=1, source_target_pairs={{16,0},{0,16},{17,1},{1,17},{18,2},{2,18},{19,3},{3,19},{20,4},{4,... | collective-permute-start | bytes 2654216 | tf_op jit(solution)/shard_map/ppermute | solution.py:24
  3.5 23.0 %collective-permute-start.2 = (bf16[384,1152]{1,0:T(8,128)(2,1)}, bf16[384,1152]{1,0:T(8,128)(2,1)S(1)}, u32[]{:S(2)}, u32[]{:S(2)}) collective-permute-start(bf16[384,1152]{1,0:T(8,128)(2,1)} %bitcast.5), channel_id=1, source_target_pairs={{32,0},{104,8},{64,32},{8,40},{96,64},{40,72},{0,96},{72,104},{33,... | collective-permute-start | bytes 2654216 | tf_op jit(solution)/shard_map/ppermute | solution.py:263
  5.2 21.4 %collective-permute-start.3 = (bf16[384,1152]{1,0:T(8,128)(2,1)}, bf16[384,1152]{1,0:T(8,128)(2,1)S(1)}, u32[]{:S(2)}, u32[]{:S(2)}) collective-permute-start(bf16[384,1152]{1,0:T(8,128)(2,1)} %bitcast.6), channel_id=1, source_target_pairs={{96,0},{40,8},{0,32},{72,40},{32,64},{104,72},{64,96},{8,104},{97,... | collective-permute-start | bytes 2654216 | tf_op jit(solution)/shard_map/ppermute | solution.py:263
  26.6 16.2 %collective-permute-start.5 = (bf16[384,1152]{1,0:T(8,128)(2,1)S(1)}, bf16[384,1152]{1,0:T(8,128)(2,1)S(1)}, u32[]{:S(2)}, u32[]{:S(2)}) collective-permute-start(bf16[384,1152]{1,0:T(8,128)(2,1)S(1)} %collective-permute-done.2.a), channel_id=1, source_target_pairs={{32,0},{104,8},{64,32},{8,40},{96,64},{40,72},{0,96},{72,104},{33,... | collective-permute-start | bytes 2654216 | tf_op jit(solution)/shard_map/ppermute | solution.py:263
  40.2 14.0 %collective-permute-start.9 = (f32[384,1152]{1,0:T(8,128)S(1)}, f32[384,1152]{1,0:T(8,128)S(1)}, u32[]{:S(2)}, u32[]{:S(2)}) collective-permute-start(f32[384,1152]{1,0:T(8,128)S(1)} %get-tuple-element.114), channel_id=1, source_target_pairs={{8,0},{0,8},{9,1},{1,9},{10,2},{2,10},{11,3},{3,11},{12,4},{4,12},... | collective-permute-start | bytes 5308424 | tf_op jit(solution)/shard_map/ppermute | solution.py:24
  44.6 4.5 %collective-permute-start.7 = (bf16[384,1280]{1,0:T(8,128)(2,1)S(1)}, bf16[384,1280]{1,0:T(8,128)(2,1)S(1)}, u32[]{:S(2)}, u32[]{:S(2)}) collective-permute-start(bf16[384,1280]{1,0:T(8,128)(2,1)S(1)} %embed_far.1.e0), channel_id=1, source_target_pairs={{8,0},{0,8},{9,1},{1,9},{10,2},{2,10},{11,3},{3,11},{12,4},{4,12},... | collective-permute-start | bytes 2949128 | tf_op jit(solution)/shard_map/ppermute | solution.py:24
  44.7 4.4 %collective-permute-start.6 = (bf16[384,1152]{1,0:T(8,128)(2,1)S(1)}, bf16[384,1152]{1,0:T(8,128)(2,1)S(1)}, u32[]{:S(2)}, u32[]{:S(2)}) collective-permute-start(bf16[384,1152]{1,0:T(8,128)(2,1)S(1)} %collective-permute-done.5.images.x0), channel_id=1, source_target_pairs={{8,0},{0,8},{9,1},{1,9},{10,2},{2,10},{11,3},{3,11},{12,4},{4,12},... | collective-permute-start | bytes 2654216 | tf_op jit(solution)/shard_map/ppermute | solution.py:24
  55.8 18.0 %collective-permute-start.16 = (f16[320,1152]{1,0:T(8,128)(2,1)S(1)}, f16[320,1152]{1,0:T(8,128)(2,1)S(1)}, u32[]{:S(2)}, u32[]{:S(2)}) collective-permute-start(f16[320,1152]{1,0:T(8,128)(2,1)S(1)} %convert_element_type.12), channel_id=1, source_target_pairs={{16,0},{0,16},{17,1},{1,17},{18,2},{2,18},{19,3},{3,19},{20,4},{4,... | collective-permute-start | bytes 2211848 | tf_op jit(solution)/shard_map/ppermute | solution.py:24
  57.1 3.6 %collective-permute-start.10 = (f32[16,1152]{1,0:T(8,128)S(1)}, f32[16,1152]{1,0:T(8,128)S(1)}, u32[]{:S(2)}, u32[]{:S(2)}) collective-permute-start(f32[16,1152]{1,0:T(8,128)S(1)} %get-tuple-element.119), channel_id=1, source_target_pairs={{32,0},{64,32},{96,64},{0,96},{33,1},{65,33},{97,65},{1,97},{34,2}... | collective-permute-start | bytes 221192 | tf_op jit(solution)/shard_map/ppermute | solution.py:24
  59.1 6.5 %collective-permute-start.11 = (f32[16,1152]{1,0:T(8,128)S(1)}, f32[16,1152]{1,0:T(8,128)S(1)}, u32[]{:S(2)}, u32[]{:S(2)}) collective-permute-start(f32[16,1152]{1,0:T(8,128)S(1)} %get-tuple-element.120), channel_id=1, source_target_pairs={{96,0},{0,32},{32,64},{64,96},{97,1},{1,33},{33,65},{65,97},{98,2}... | collective-permute-start | bytes 221192 | tf_op jit(solution)/shard_map/ppermute | solution.py:24
  59.1 6.5 %collective-permute-start.12 = (f32[16,1152]{1,0:T(8,128)S(1)}, f32[16,1152]{1,0:T(8,128)S(1)}, u32[]{:S(2)}, u32[]{:S(2)}) collective-permute-start(f32[16,1152]{1,0:T(8,128)S(1)} %get-tuple-element.121), channel_id=1, source_target_pairs={{64,0},{96,32},{0,64},{32,96},{65,1},{97,33},{1,65},{33,97},{66,2}... | collective-permute-start | bytes 221192 | tf_op jit(solution)/shard_map/ppermute | solution.py:24
  65.6 5.2 %collective-permute-start.13 = (f32[16,1152]{1,0:T(8,128)S(1)}, f32[16,1152]{1,0:T(8,128)S(1)}, u32[]{:S(2)}, u32[]{:S(2)}) collective-permute-start(f32[16,1152]{1,0:T(8,128)S(1)} %sums.3.a), channel_id=1, source_target_pairs={{1,0},{2,1},{3,2},{0,3},{5,4},{6,5},{7,6},{4,7},{9,8},{10,9},{11,1... | collective-permute-start | bytes 221192 | tf_op jit(solution)/shard_map/ppermute | solution.py:24
  68.2 5.2 %collective-permute-start.14 = (f32[16,1152]{1,0:T(8,128)S(1)}, f32[16,1152]{1,0:T(8,128)S(1)}, u32[]{:S(2)}, u32[]{:S(2)}) collective-permute-start(f32[16,1152]{1,0:T(8,128)S(1)} %sums.3.a), channel_id=1, source_target_pairs={{3,0},{0,1},{1,2},{2,3},{7,4},{4,5},{5,6},{6,7},{11,8},{8,9},{9,10... | collective-permute-start | bytes 221192 | tf_op jit(solution)/shard_map/ppermute | solution.py:24
  68.2 5.2 %collective-permute-start.15 = (f32[16,1152]{1,0:T(8,128)S(1)}, f32[16,1152]{1,0:T(8,128)S(1)}, u32[]{:S(2)}, u32[]{:S(2)}) collective-permute-start(f32[16,1152]{1,0:T(8,128)S(1)} %sums.3.a), channel_id=1, source_target_pairs={{2,0},{3,1},{0,2},{1,3},{6,4},{7,5},{4,6},{5,7},{10,8},{11,9},{8,1... | collective-permute-start | bytes 221192 | tf_op jit(solution)/shard_map/ppermute | solution.py:24
  73.9 9.3 %collective-permute-start.20 = (f32[384,1152]{1,0:T(8,128)S(1)}, f32[384,1152]{1,0:T(8,128)S(1)}, u32[]{:S(2)}, u32[]{:S(2)}) collective-permute-start(f32[384,1152]{1,0:T(8,128)S(1)} %twin_sums.1), channel_id=1, source_target_pairs={{8,0},{0,8},{9,1},{1,9},{10,2},{2,10},{11,3},{3,11},{12,4},{4,12},... | collective-permute-start | bytes 5308424 | tf_op jit(solution)/shard_map/ppermute | solution.py:24
  76.0 5.3 %collective-permute-start.17 = (f32[16,1152]{1,0:T(8,128)S(1)}, f32[16,1152]{1,0:T(8,128)S(1)}, u32[]{:S(2)}, u32[]{:S(2)}) collective-permute-start(f32[16,1152]{1,0:T(8,128)S(1)} %sums.4.a), channel_id=1, source_target_pairs={{4,0},{16,4},{20,16},{0,20},{5,1},{17,5},{21,17},{1,21},{6,2},{18,... | collective-permute-start | bytes 221192 | tf_op jit(solution)/shard_map/ppermute | solution.py:24
  77.9 4.4 %collective-permute-start.18 = (f32[16,1152]{1,0:T(8,128)S(1)}, f32[16,1152]{1,0:T(8,128)S(1)}, u32[]{:S(2)}, u32[]{:S(2)}) collective-permute-start(f32[16,1152]{1,0:T(8,128)S(1)} %sums.4.a), channel_id=1, source_target_pairs={{20,0},{0,4},{4,16},{16,20},{21,1},{1,5},{5,17},{17,21},{22,2},{2,... | collective-permute-start | bytes 221192 | tf_op jit(solution)/shard_map/ppermute | solution.py:24
  79.0 4.1 %collective-permute-start.19 = (f32[16,1152]{1,0:T(8,128)S(1)}, f32[16,1152]{1,0:T(8,128)S(1)}, u32[]{:S(2)}, u32[]{:S(2)}) collective-permute-start(f32[16,1152]{1,0:T(8,128)S(1)} %sums.4.a), channel_id=1, source_target_pairs={{16,0},{20,4},{0,16},{4,20},{17,1},{21,5},{1,17},{5,21},{18,2},{22... | collective-permute-start | bytes 221192 | tf_op jit(solution)/shard_map/ppermute | solution.py:24
  83.2 8.6 %collective-permute-start.24 = (f16[80,1152]{1,0:T(8,128)(2,1)S(1)}, f16[80,1152]{1,0:T(8,128)(2,1)S(1)}, u32[]{:S(2)}, u32[]{:S(2)}) collective-permute-start(f16[80,1152]{1,0:T(8,128)(2,1)S(1)} %convert_element_type.13), channel_id=1, source_target_pairs={{16,0},{0,16},{17,1},{1,17},{18,2},{2,18},{19,3},{3,19},{20,4},{4,... | collective-permute-start | bytes 552968 | tf_op jit(solution)/shard_map/ppermute | solution.py:24
  84.2 5.1 %collective-permute-start.21 = (f32[16,1152]{1,0:T(8,128)S(1)}, f32[16,1152]{1,0:T(8,128)S(1)}, u32[]{:S(2)}, u32[]{:S(2)}) collective-permute-start(f32[16,1152]{1,0:T(8,128)S(1)} %sums.5.a), channel_id=1, source_target_pairs={{32,0},{64,32},{96,64},{0,96},{33,1},{65,33},{97,65},{1,97},{34,2}... | collective-permute-start | bytes 221192 | tf_op jit(solution)/shard_map/ppermute | solution.py:24
  86.4 5.0 %collective-permute-start.22 = (f32[16,1152]{1,0:T(8,128)S(1)}, f32[16,1152]{1,0:T(8,128)S(1)}, u32[]{:S(2)}, u32[]{:S(2)}) collective-permute-start(f32[16,1152]{1,0:T(8,128)S(1)} %sums.5.a), channel_id=1, source_target_pairs={{96,0},{0,32},{32,64},{64,96},{97,1},{1,33},{33,65},{65,97},{98,2}... | collective-permute-start | bytes 221192 | tf_op jit(solution)/shard_map/ppermute | solution.py:24
  86.4 5.4 %collective-permute-start.23 = (f32[16,1152]{1,0:T(8,128)S(1)}, f32[16,1152]{1,0:T(8,128)S(1)}, u32[]{:S(2)}, u32[]{:S(2)}) collective-permute-start(f32[16,1152]{1,0:T(8,128)S(1)} %sums.5.a), channel_id=1, source_target_pairs={{64,0},{96,32},{0,64},{32,96},{65,1},{97,33},{1,65},{33,97},{66,2}... | collective-permute-start | bytes 221192 | tf_op jit(solution)/shard_map/ppermute | solution.py:24
  91.8 4.2 %collective-permute-start.25 = (f32[64,1152]{1,0:T(8,128)S(1)}, f32[64,1152]{1,0:T(8,128)S(1)}, u32[]{:S(2)}, u32[]{:S(2)}) collective-permute-start(f32[64,1152]{1,0:T(8,128)S(1)} %places.1.a), channel_id=1, source_target_pairs={{8,0},{0,8},{9,1},{1,9},{10,2},{2,10},{11,3},{3,11},{12,4},{4,12},... | collective-permute-start | bytes 884744 | tf_op jit(solution)/shard_map/ppermute | solution.py:24
  (10 other events, 23.2 us)

commit v7 on v6

--- a/solution.py
+++ b/solution.py
@@ -13,6 +13,11 @@
 LOG2E = 1.4426950408889634
 REACH = 14.0
 MIB = 1 << 20
+
+
+def swapped(block, axis, flip):
+    n = lax.axis_size(axis)
+    return lax.ppermute(block, axis, [(i ^ flip, i) for i in range(n)])
 
 
 def tied(*values):
@@ -203,7 +208,7 @@
 def quarter_kernel(a, b, o0, o1, o2, o3, total):
     total[...] = a[...] + b[...]
     here, part = lax.axis_index("z"), o0.shape[0]
-    for out, d in ((o0, 0), (o1, 1), (o2, 3), (o3, 2)):
+    for out, d in ((o0, 0), (o1, 1), (o2, 2), (o3, 3)):
         out[...] = total[pl.ds(pl.multiple_of(((here + 4 - d) % 4) * part, part), part), :]
 
 
@@ -213,7 +218,7 @@
 
 def place_kernel(pairs, a, b, c, d, out):
     here, part = lax.axis_index("z"), a.shape[0]
-    for block, k in ((a, 0), (b, 1), (c, 3), (d, 2)):
+    for block, k in ((a, 0), (b, 1), (c, 2), (d, 3)):
         out[pl.ds(pl.multiple_of(((here + k) % 4) * part, part), part), :] = block[...] / pairs
 
 
@@ -347,26 +352,26 @@
     def small(kernel, name, operands, outs, scratch=()):
         return run(kernel, name, operands, outs, scratch, 1, False)
 
-    sizes = (304, 80)
+    sizes = (256, 128)
     chunks = small(
         away_kernel, "away_sums", [w2, both2, s2, s3], [shape((n + (16 if k == 0 else 0), width), F32) for k, n in enumerate(sizes)]
     )
     chunks = [chunk.astype(F16) for chunk in chunks]
 
-    def everyones(axis):
+    def everyones(axis, order, other):
         def summed(block):
-            others = [from_ahead(block, axis, d) for d in (1, 3, 2)]
+            others = [other(block, axis, d) for d in order]
             return small(sum_kernel, "sums", [block] + others, [quarter])[0]
 
         return summed
 
     def scattered(sent):
         pieces = small(quarter_kernel, "quarters", [kept, sent], [quarter] * 4, [pltpu.VMEM((rank, width), F32)])
-        pieces = [pieces[0]] + [from_ahead(p, "z", d) for p, d in zip(pieces[1:], (1, 3, 2))]
+        pieces = [pieces[0]] + [from_ahead(p, "z", d) for p, d in zip(pieces[1:], (1, 2, 3))]
         return small(sum_kernel, "sums", pieces, [quarter])[0]
 
     def gathered(block):
-        pieces = [block] + [from_ahead(block, "z", d) for d in (1, 3, 2)]
+        pieces = [block] + [from_ahead(block, "z", d) for d in (1, 2, 3)]
         return small(functools.partial(place_kernel, float(rows * 16)), "places", pieces, [grads])[0]
 
     quarter = shape((rank // 4, width), F32)
@@ -375,10 +380,10 @@
     total = scattered(sent)
     moved = from_ahead(chunks[0], "y", 1).astype(F32)
     (s1,) = small(twin_kernel, "twin_sums", [w_twin, both1, s1], [sums])
-    total = everyones("x")(total)
+    total = everyones("x", (1, 2, 3), from_ahead)(total)
     total, c0, s1, chunk = tied(total, moved, s1, chunks[1])
     s1 = from_ahead(s1, "c", 1)
-    total = everyones(("y", "h"))(total)
+    total = everyones(("y", "h"), (1, 2, 3), from_ahead)(total)
     total, chunk, s1 = tied(total, chunk, s1)
     moved = from_ahead(chunk, "y", 1).astype(F32)
     total = gathered(total)

time: 97.2 us -> 95.3 us (0.980)
  starting transfers between devices: 34.6 us -> 32.6 us
    ppermute x23, starting transfers between devices: 28.9 us -> 26.9 us  [from_ahead(): lax.ppermute(block, axis, [((i + distance) % n, i) for i in range(n)])]
  transfers between devices with their start and end apart: 26 -> 26, of which waited for: 10 -> 12; matrix products, arithmetic and copies ran while one was open for 0% -> 0% of each run, Pallas kernels for 37% -> 38%
where the time goes in v7:
time: 95.3 us; the launch traced here: 95 us
  Pallas kernels  36.7 us (39%)
  starting transfers between devices  32.6 us (34%)
  waiting for transfers between devices  17.4 us (18%)
  local copies, waits for them, and re-layouts  5.91 us (6%)
  between operations  2.2 us (2%)
    pallas_call x19, Pallas kernels, run(): pl.pallas_call(kernel, in_specs=ins, out_specs=[spec] * len(outs), out_sh...  36.1 us
    ppermute x23, starting transfers between devices, from_ahead(): lax.ppermute(block, axis, [((i + distance) % n, i) for i in range(n)])  26.9 us
    ppermute x23, waiting for transfers between devices, from_ahead(): lax.ppermute(block, axis, [((i + distance) % n, i) for i in range(n)])  17.4 us
    unnamed x16, local copies, waits for them, and re-layouts  5.91 us
    ppermute x3, starting transfers between devices, turned(): lax.ppermute(block, ('z', 'c'), [(2 * step(z, c) + c, 2 * z + c) for z in...  5.73 us
  transfers between devices with their start and end apart: 26, of which 12 were waited for; matrix products, arithmetic and copies ran while one was open for 0% of the time, Pallas kernels for 38%

profile of v7, /device:TPU:1, one launch (start us, length us, event | category | flops | bytes accessed | tf_op | source)
XLA Modules:
  0.0 95.0 jit_solution(9077208969064057506)
XLA Ops:
  3.5 1.6 %collective-permute-start.2 = (bf16[384,1152]{1,0:T(8,128)(2,1)}, bf16[384,1152]{1,0:T(8,128)(2,1)S(1)}, u32[]{:S(2)}, u32[]{:S(2)}) collective-permute-start(bf16[384,1152]{1,0:T(8,128)(2,1)} %bitcast.5), channel_id=1, source_target_pairs={{32,0},{104,8},{64,32},{8,40},{96,64},{40,72},{0,96},{72,104},{33,... | collective-permute-start | bytes 2654216 | tf_op jit(solution)/shard_map/ppermute | solution.py:268
  5.2 2.1 %collective-permute-start.3 = (bf16[384,1152]{1,0:T(8,128)(2,1)}, bf16[384,1152]{1,0:T(8,128)(2,1)S(1)}, u32[]{:S(2)}, u32[]{:S(2)}) collective-permute-start(bf16[384,1152]{1,0:T(8,128)(2,1)} %bitcast.6), channel_id=1, source_target_pairs={{96,0},{40,8},{0,32},{72,40},{32,64},{104,72},{64,96},{8,104},{97,... | collective-permute-start | bytes 2654216 | tf_op jit(solution)/shard_map/ppermute | solution.py:268
  12.4 1.7 %copy-done.6 = bf16[1152,1152]{1,0:T(8,128)(2,1)S(1)} copy-done((bf16[1152,1152]{1,0:T(8,128)(2,1)S(1)}, bf16[1152,1152]{1,0:T(8,128)(2,1)}, u32[]{:S(2)}) %copy-start.6) | copy-done | bytes 2654232
  15.1 5.5 %own_rows.1 = (bf16[384,1280]{1,0:T(8,128)(2,1)S(1)}, bf16[1152,1280]{1,0:T(8,128)(2,1)S(1)}, bf16[128,768]{1,0:T(8,128)(2,1)S(1)}, f32[384,1152]{1,0:T(8,128)S(...) custom-call(f32[3]{0:T(128)S(1)} %consts.1, ...), custom_call_target="tpu_custom_call" | custom-call | flops 2582013440 | bytes 13860876 | tf_op jit(solution)/shard_map/own_rows/pallas_call | solution.py:237
  20.6 3.0 %collective-permute-done.1.texts.t1 = bf16[384,1152]{1,0:T(8,128)(2,1)S(1)} collective-permute-done((bf16[384,1152]{1,0:T(8,128)(2,1)}, bf16[384,1152]{1,0:T(8,128)(2,1)S(1)}, u32[]{:S(2)}, u32[]{:S(2)}) %collective-permute-start.1) | collective-permute-done | bytes 884768 | tf_op jit(solution)/shard_map/ppermute | solution.py:29
  24.4 2.1 %own_far.2 = (bf16[128,384]{1,0:T(8,128)(2,1)S(1)}, f32[384,1152]{1,0:T(8,128)S(1)}, f32[384,128]{1,0:T(8,128)S(1)}, f32[128,384]{1,0:T(8,128)S(1)}) custom-call(f32[3]{0:T(128)S(1)} %consts.1, bf16[384,1280]{1,0:T(8,128)(2,1)S(1)} %get-tuple-element.72.both, bf16[384,1152]{1,0:T(8,128)(2,1)S(1)} %collective-permute-done.1.texts.t1, ...), custom_call_target="tpu_custom_call" | custom-call | flops 747424960 | bytes 4472844 | tf_op jit(solution)/shard_map/own_far/pallas_call | solution.py:237
  26.6 2.0 %collective-permute-start.5 = (bf16[384,1152]{1,0:T(8,128)(2,1)S(1)}, bf16[384,1152]{1,0:T(8,128)(2,1)S(1)}, u32[]{:S(2)}, u32[]{:S(2)}) collective-permute-start(bf16[384,1152]{1,0:T(8,128)(2,1)S(1)} %collective-permute-done.2.a), channel_id=1, source_target_pairs={{32,0},{104,8},{64,32},{8,40},{96,64},{40,72},{0,96},{72,104},{33,... | collective-permute-start | bytes 2654216 | tf_op jit(solution)/shard_map/ppermute | solution.py:268
  28.5 2.1 %own_far.3 = (bf16[128,384]{1,0:T(8,128)(2,1)S(1)}, f32[384,1152]{1,0:T(8,128)S(1)}, f32[384,128]{1,0:T(8,128)S(1)}, f32[128,384]{1,0:T(8,128)S(1)}) custom-call(f32[3]{0:T(128)S(1)} %consts.1, bf16[384,1280]{1,0:T(8,128)(2,1)S(1)} %get-tuple-element.72.both, bf16[384,1152]{1,0:T(8,128)(2,1)S(1)} %collective-permute-done.4.texts.t3, ...), custom_call_target="tpu_custom_call" | custom-call | flops 747424960 | bytes 4472844 | tf_op jit(solution)/shard_map/own_far/pallas_call | solution.py:237
  30.7 6.7 %side_rows.1 = (bf16[768,1280]{1,0:T(8,128)(2,1)S(1)}, f32[384,128]{1,0:T(8,128)S(1)}, f32[384,128]{1,0:T(8,128)S(1)}, f32[128,768]{1,0:T(8,128)S(1)}, bf16[384,...) custom-call(f32[3]{0:T(128)S(1)} %consts.1, bf16[384,1152]{1,0:T(8,128)(2,1)S(1)} %collective-permute-done.2.a, ...), custom_call_target="tpu_custom_call" | custom-call | flops 3669177088 | bytes 11157516 | tf_op jit(solution)/shard_map/side_rows/pallas_call | solution.py:237
  37.4 2.8 %side_far.2 = (f32[384,1152]{1,0:T(8,128)S(1)}, f32[384,128]{1,0:T(8,128)S(1)}, f32[128,768]{1,0:T(8,128)S(1)}) custom-call(f32[3]{0:T(128)S(1)} %consts.1, bf16[768,1280]{1,0:T(8,128)(2,1)S(1)} %get-tuple-element.83.both.both0, bf16[384,1152]{1,0:T(8,128)(2,1)S(1)} %collective-permute-done.4.texts.t3, bf16[128,384]{1,0:T(8,128)(2,1)S(1)} %get-tuple-element.86.ups, ...), custom_call_target="tpu_custom_call" | custom-call | flops 1494849920 | bytes 7667724 | tf_op jit(solution)/shard_map/side_far/pallas_call | solution.py:237
  40.1 2.7 %collective-permute-start.9 = (f32[384,1152]{1,0:T(8,128)S(1)}, f32[384,1152]{1,0:T(8,128)S(1)}, u32[]{:S(2)}, u32[]{:S(2)}) collective-permute-start(f32[384,1152]{1,0:T(8,128)S(1)} %get-tuple-element.114), channel_id=1, source_target_pairs={{8,0},{0,8},{9,1},{1,9},{10,2},{2,10},{11,3},{3,11},{12,4},{4,12},... | collective-permute-start | bytes 5308424 | tf_op jit(solution)/shard_map/ppermute | solution.py:29
  42.8 1.8 %embed_far.1.e0 = bf16[384,1280]{1,0:T(8,128)(2,1)S(1)} custom-call(bf16[384,1152]{1,0:T(8,128)(2,1)S(1)} %collective-permute-done.5.images.x0, bf16[1152,1280]{1,0:T(8,128)(2,1)S(1)} %get-tuple-element.80.packed, bf16[64,1152]{1,0:T(8,128)(2,1)S(1)} %copy-done.5), custom_call_target="tpu_custom_call" | custom-call | flops 1087163648 | bytes 4964352 | tf_op jit(solution)/shard_map/embed_far/pallas_call | solution.py:237
  45.2 2.8 %side_far.3 = (f32[384,1152]{1,0:T(8,128)S(1)}, f32[384,128]{1,0:T(8,128)S(1)}, f32[128,768]{1,0:T(8,128)S(1)}) custom-call(f32[3]{0:T(128)S(1)} %consts.1, bf16[768,1280]{1,0:T(8,128)(2,1)S(1)} %get-tuple-element.83.both.both0, bf16[384,1152]{1,0:T(8,128)(2,1)S(1)} %collective-permute-done.1.texts.t1, bf16[128,384]{1,0:T(8,128)(2,1)S(1)} %get-tuple-element.93.ups.ups1, ...), custom_call_target="tpu_custom_call" | custom-call | flops 1494849920 | bytes 7667724 | tf_op jit(solution)/shard_map/side_far/pallas_call | solution.py:237
  49.1 4.7 %far_rows.1 = (f32[64,1152]{1,0:T(8,128)S(1)}, f32[64,1152]{1,0:T(8,128)S(1)}, bf16[768,1280]{1,0:T(8,128)(2,1)S(1)}, bf16[384,768]{1,0:T(8,128)(2,1)S(1)}, bf16[384,768]{1,0:T(8,128)(2,1)S(1)}) custom-call(f32[3]{0:T(128)S(1)} %consts.1, bf16[384,1152]{1,0:T(8,128)(2,1)S(1)} %collective-permute-done.5.images.x0, ...), custom_call_target="tpu_custom_call" | custom-call | flops 1698693120 | bytes 10518540 | tf_op jit(solution)/shard_map/far_rows/pallas_call | solution.py:237
  57.1 2.0 %collective-permute-start.10 = (f32[16,1152]{1,0:T(8,128)S(1)}, f32[16,1152]{1,0:T(8,128)S(1)}, u32[]{:S(2)}, u32[]{:S(2)}) collective-permute-start(f32[16,1152]{1,0:T(8,128)S(1)} %get-tuple-element.119), channel_id=1, source_target_pairs={{32,0},{64,32},{96,64},{0,96},{33,1},{65,33},{97,65},{1,97},{34,2}... | collective-permute-start | bytes 221192 | tf_op jit(solution)/shard_map/ppermute | solution.py:29
  60.7 3.3 %collective-permute-done.11.c = f32[16,1152]{1,0:T(8,128)S(1)} collective-permute-done((f32[16,1152]{1,0:T(8,128)S(1)}, f32[16,1152]{1,0:T(8,128)S(1)}, u32[]{:S(2)}, u32[]{:S(2)}) %collective-permute-start.11) | collective-permute-done | bytes 73760 | tf_op jit(solution)/shard_map/ppermute | solution.py:29
  64.9 2.6 %collective-permute-start.13 = (f32[16,1152]{1,0:T(8,128)S(1)}, f32[16,1152]{1,0:T(8,128)S(1)}, u32[]{:S(2)}, u32[]{:S(2)}) collective-permute-start(f32[16,1152]{1,0:T(8,128)S(1)} %sums.3.a), channel_id=1, source_target_pairs={{1,0},{2,1},{3,2},{0,3},{5,4},{6,5},{7,6},{4,7},{9,8},{10,9},{11,1... | collective-permute-start | bytes 221192 | tf_op jit(solution)/shard_map/ppermute | solution.py:29
  69.5 2.7 %collective-permute-done.14.c = f32[16,1152]{1,0:T(8,128)S(1)} collective-permute-done((f32[16,1152]{1,0:T(8,128)S(1)}, f32[16,1152]{1,0:T(8,128)S(1)}, u32[]{:S(2)}, u32[]{:S(2)}) %collective-permute-start.14) | collective-permute-done | bytes 73760 | tf_op jit(solution)/shard_map/ppermute | solution.py:29
  73.1 3.1 %collective-permute-start.20 = (f32[384,1152]{1,0:T(8,128)S(1)}, f32[384,1152]{1,0:T(8,128)S(1)}, u32[]{:S(2)}, u32[]{:S(2)}) collective-permute-start(f32[384,1152]{1,0:T(8,128)S(1)} %twin_sums.1), channel_id=1, source_target_pairs={{8,0},{0,8},{9,1},{1,9},{10,2},{2,10},{11,3},{3,11},{12,4},{4,12},... | collective-permute-start | bytes 5308424 | tf_op jit(solution)/shard_map/ppermute | solution.py:29
  76.3 1.9 %collective-permute-start.17 = (f32[16,1152]{1,0:T(8,128)S(1)}, f32[16,1152]{1,0:T(8,128)S(1)}, u32[]{:S(2)}, u32[]{:S(2)}) collective-permute-start(f32[16,1152]{1,0:T(8,128)S(1)} %sums.4.a), channel_id=1, source_target_pairs={{4,0},{16,4},{20,16},{0,20},{5,1},{17,5},{21,17},{1,21},{6,2},{18,... | collective-permute-start | bytes 221192 | tf_op jit(solution)/shard_map/ppermute | solution.py:29
  78.6 1.6 %collective-permute-start.19 = (f32[16,1152]{1,0:T(8,128)S(1)}, f32[16,1152]{1,0:T(8,128)S(1)}, u32[]{:S(2)}, u32[]{:S(2)}) collective-permute-start(f32[16,1152]{1,0:T(8,128)S(1)} %sums.4.a), channel_id=1, source_target_pairs={{20,0},{0,4},{4,16},{16,20},{21,1},{1,5},{5,17},{17,21},{22,2},{2,... | collective-permute-start | bytes 221192 | tf_op jit(solution)/shard_map/ppermute | solution.py:29
  85.1 1.7 %near_sums.1.near = f32[384,1152]{1,0:T(8,128)S(1)} custom-call(bf16[384,768]{1,0:T(8,128)(2,1)S(1)} %get-tuple-element.131.w0, bf16[768,1280]{1,0:T(8,128)(2,1)S(1)} %get-tuple-element.83.both.both0, bf16[384,768]{1,0:T(8,128)(2,1)S(1)} %get-tuple-element.132.w1, bf16[768,1280]{1,0:T(8,128)(2,1)S(1)} %get-tuple-element.112.both.both1, ...), custom_call_target="tpu_custom_call" | custom-call | flops 1 | bytes 10420224 | tf_op jit(solution)/shard_map/near_sums/pallas_call | solution.py:237
  86.9 1.7 %collective-permute-done.22.c = f32[16,1152]{1,0:T(8,128)S(1)} collective-permute-done((f32[16,1152]{1,0:T(8,128)S(1)}, f32[16,1152]{1,0:T(8,128)S(1)}, u32[]{:S(2)}, u32[]{:S(2)}) %collective-permute-start.22) | collective-permute-done | bytes 73760 | tf_op jit(solution)/shard_map/ppermute | solution.py:29
  89.9 2.8 %collective-permute-start.25 = (f32[64,1152]{1,0:T(8,128)S(1)}, f32[64,1152]{1,0:T(8,128)S(1)}, u32[]{:S(2)}, u32[]{:S(2)}) collective-permute-start(f32[64,1152]{1,0:T(8,128)S(1)} %places.1.a), channel_id=1, source_target_pairs={{8,0},{0,8},{9,1},{1,9},{10,2},{2,10},{11,3},{3,11},{12,4},{4,12},... | collective-permute-start | bytes 884744 | tf_op jit(solution)/shard_map/ppermute | solution.py:29
  (68 shorter events, 27.8 us)
Async XLA Ops:
  0.6 8.6 %collective-permute-start = (bf16[384,1152]{1,0:T(8,128)(2,1)}, bf16[384,1152]{1,0:T(8,128)(2,1)S(1)}, u32[]{:S(2)}, u32[]{:S(2)}) collective-permute-start(bf16[384,1152]{1,0:T(8,128)(2,1)} %bitcast.9), channel_id=1, source_target_pairs={{8,0},{0,8},{9,1},{1,9},{10,2},{2,10},{11,3},{3,11},{12,4},{4,12},... | collective-permute-start | bytes 2654216 | tf_op jit(solution)/shard_map/ppermute | solution.py:29
  2.1 21.4 %collective-permute-start.1 = (bf16[384,1152]{1,0:T(8,128)(2,1)}, bf16[384,1152]{1,0:T(8,128)(2,1)S(1)}, u32[]{:S(2)}, u32[]{:S(2)}) collective-permute-start(bf16[384,1152]{1,0:T(8,128)(2,1)} %bitcast.10), channel_id=1, source_target_pairs={{16,0},{0,16},{17,1},{1,17},{18,2},{2,18},{19,3},{3,19},{20,4},{4,... | collective-permute-start | bytes 2654216 | tf_op jit(solution)/shard_map/ppermute | solution.py:29
  3.5 23.0 %collective-permute-start.2 = (bf16[384,1152]{1,0:T(8,128)(2,1)}, bf16[384,1152]{1,0:T(8,128)(2,1)S(1)}, u32[]{:S(2)}, u32[]{:S(2)}) collective-permute-start(bf16[384,1152]{1,0:T(8,128)(2,1)} %bitcast.5), channel_id=1, source_target_pairs={{32,0},{104,8},{64,32},{8,40},{96,64},{40,72},{0,96},{72,104},{33,... | collective-permute-start | bytes 2654216 | tf_op jit(solution)/shard_map/ppermute | solution.py:268
  5.2 21.4 %collective-permute-start.3 = (bf16[384,1152]{1,0:T(8,128)(2,1)}, bf16[384,1152]{1,0:T(8,128)(2,1)S(1)}, u32[]{:S(2)}, u32[]{:S(2)}) collective-permute-start(bf16[384,1152]{1,0:T(8,128)(2,1)} %bitcast.6), channel_id=1, source_target_pairs={{96,0},{40,8},{0,32},{72,40},{32,64},{104,72},{64,96},{8,104},{97,... | collective-permute-start | bytes 2654216 | tf_op jit(solution)/shard_map/ppermute | solution.py:268
  26.6 16.2 %collective-permute-start.5 = (bf16[384,1152]{1,0:T(8,128)(2,1)S(1)}, bf16[384,1152]{1,0:T(8,128)(2,1)S(1)}, u32[]{:S(2)}, u32[]{:S(2)}) collective-permute-start(bf16[384,1152]{1,0:T(8,128)(2,1)S(1)} %collective-permute-done.2.a), channel_id=1, source_target_pairs={{32,0},{104,8},{64,32},{8,40},{96,64},{40,72},{0,96},{72,104},{33,... | collective-permute-start | bytes 2654216 | tf_op jit(solution)/shard_map/ppermute | solution.py:268
  40.1 14.1 %collective-permute-start.9 = (f32[384,1152]{1,0:T(8,128)S(1)}, f32[384,1152]{1,0:T(8,128)S(1)}, u32[]{:S(2)}, u32[]{:S(2)}) collective-permute-start(f32[384,1152]{1,0:T(8,128)S(1)} %get-tuple-element.114), channel_id=1, source_target_pairs={{8,0},{0,8},{9,1},{1,9},{10,2},{2,10},{11,3},{3,11},{12,4},{4,12},... | collective-permute-start | bytes 5308424 | tf_op jit(solution)/shard_map/ppermute | solution.py:29
  44.6 4.5 %collective-permute-start.7 = (bf16[384,1280]{1,0:T(8,128)(2,1)S(1)}, bf16[384,1280]{1,0:T(8,128)(2,1)S(1)}, u32[]{:S(2)}, u32[]{:S(2)}) collective-permute-start(bf16[384,1280]{1,0:T(8,128)(2,1)S(1)} %embed_far.1.e0), channel_id=1, source_target_pairs={{8,0},{0,8},{9,1},{1,9},{10,2},{2,10},{11,3},{3,11},{12,4},{4,12},... | collective-permute-start | bytes 2949128 | tf_op jit(solution)/shard_map/ppermute | solution.py:29
  44.7 4.4 %collective-permute-start.6 = (bf16[384,1152]{1,0:T(8,128)(2,1)S(1)}, bf16[384,1152]{1,0:T(8,128)(2,1)S(1)}, u32[]{:S(2)}, u32[]{:S(2)}) collective-permute-start(bf16[384,1152]{1,0:T(8,128)(2,1)S(1)} %collective-permute-done.5.images.x0), channel_id=1, source_target_pairs={{8,0},{0,8},{9,1},{1,9},{10,2},{2,10},{11,3},{3,11},{12,4},{4,12},... | collective-permute-start | bytes 2654216 | tf_op jit(solution)/shard_map/ppermute | solution.py:29
  55.8 17.3 %collective-permute-start.16 = (f16[272,1152]{1,0:T(8,128)(2,1)S(1)}, f16[272,1152]{1,0:T(8,128)(2,1)S(1)}, u32[]{:S(2)}, u32[]{:S(2)}) collective-permute-start(f16[272,1152]{1,0:T(8,128)(2,1)S(1)} %convert_element_type.12), channel_id=1, source_target_pairs={{16,0},{0,16},{17,1},{1,17},{18,2},{2,18},{19,3},{3,19},{20,4},{4,... | collective-permute-start | bytes 1880072 | tf_op jit(solution)/shard_map/ppermute | solution.py:29
  57.1 3.6 %collective-permute-start.10 = (f32[16,1152]{1,0:T(8,128)S(1)}, f32[16,1152]{1,0:T(8,128)S(1)}, u32[]{:S(2)}, u32[]{:S(2)}) collective-permute-start(f32[16,1152]{1,0:T(8,128)S(1)} %get-tuple-element.119), channel_id=1, source_target_pairs={{32,0},{64,32},{96,64},{0,96},{33,1},{65,33},{97,65},{1,97},{34,2}... | collective-permute-start | bytes 221192 | tf_op jit(solution)/shard_map/ppermute | solution.py:29
  59.1 4.8 %collective-permute-start.11 = (f32[16,1152]{1,0:T(8,128)S(1)}, f32[16,1152]{1,0:T(8,128)S(1)}, u32[]{:S(2)}, u32[]{:S(2)}) collective-permute-start(f32[16,1152]{1,0:T(8,128)S(1)} %get-tuple-element.120), channel_id=1, source_target_pairs={{64,0},{96,32},{0,64},{32,96},{65,1},{97,33},{1,65},{33,97},{66,2}... | collective-permute-start | bytes 221192 | tf_op jit(solution)/shard_map/ppermute | solution.py:29
  59.1 5.8 %collective-permute-start.12 = (f32[16,1152]{1,0:T(8,128)S(1)}, f32[16,1152]{1,0:T(8,128)S(1)}, u32[]{:S(2)}, u32[]{:S(2)}) collective-permute-start(f32[16,1152]{1,0:T(8,128)S(1)} %get-tuple-element.121), channel_id=1, source_target_pairs={{96,0},{0,32},{32,64},{64,96},{97,1},{1,33},{33,65},{65,97},{98,2}... | collective-permute-start | bytes 221192 | tf_op jit(solution)/shard_map/ppermute | solution.py:29
  64.9 4.6 %collective-permute-start.13 = (f32[16,1152]{1,0:T(8,128)S(1)}, f32[16,1152]{1,0:T(8,128)S(1)}, u32[]{:S(2)}, u32[]{:S(2)}) collective-permute-start(f32[16,1152]{1,0:T(8,128)S(1)} %sums.3.a), channel_id=1, source_target_pairs={{1,0},{2,1},{3,2},{0,3},{5,4},{6,5},{7,6},{4,7},{9,8},{10,9},{11,1... | collective-permute-start | bytes 221192 | tf_op jit(solution)/shard_map/ppermute | solution.py:29
  67.5 4.8 %collective-permute-start.14 = (f32[16,1152]{1,0:T(8,128)S(1)}, f32[16,1152]{1,0:T(8,128)S(1)}, u32[]{:S(2)}, u32[]{:S(2)}) collective-permute-start(f32[16,1152]{1,0:T(8,128)S(1)} %sums.3.a), channel_id=1, source_target_pairs={{2,0},{3,1},{0,2},{1,3},{6,4},{7,5},{4,6},{5,7},{10,8},{11,9},{8,1... | collective-permute-start | bytes 221192 | tf_op jit(solution)/shard_map/ppermute | solution.py:29
  68.0 5.0 %collective-permute-start.15 = (f32[16,1152]{1,0:T(8,128)S(1)}, f32[16,1152]{1,0:T(8,128)S(1)}, u32[]{:S(2)}, u32[]{:S(2)}) collective-permute-start(f32[16,1152]{1,0:T(8,128)S(1)} %sums.3.a), channel_id=1, source_target_pairs={{3,0},{0,1},{1,2},{2,3},{7,4},{4,5},{5,6},{6,7},{11,8},{8,9},{9,10... | collective-permute-start | bytes 221192 | tf_op jit(solution)/shard_map/ppermute | solution.py:29
  73.1 9.9 %collective-permute-start.20 = (f32[384,1152]{1,0:T(8,128)S(1)}, f32[384,1152]{1,0:T(8,128)S(1)}, u32[]{:S(2)}, u32[]{:S(2)}) collective-permute-start(f32[384,1152]{1,0:T(8,128)S(1)} %twin_sums.1), channel_id=1, source_target_pairs={{8,0},{0,8},{9,1},{1,9},{10,2},{2,10},{11,3},{3,11},{12,4},{4,12},... | collective-permute-start | bytes 5308424 | tf_op jit(solution)/shard_map/ppermute | solution.py:29
  76.3 5.3 %collective-permute-start.17 = (f32[16,1152]{1,0:T(8,128)S(1)}, f32[16,1152]{1,0:T(8,128)S(1)}, u32[]{:S(2)}, u32[]{:S(2)}) collective-permute-start(f32[16,1152]{1,0:T(8,128)S(1)} %sums.4.a), channel_id=1, source_target_pairs={{4,0},{16,4},{20,16},{0,20},{5,1},{17,5},{21,17},{1,21},{6,2},{18,... | collective-permute-start | bytes 221192 | tf_op jit(solution)/shard_map/ppermute | solution.py:29
  78.2 3.5 %collective-permute-start.18 = (f32[16,1152]{1,0:T(8,128)S(1)}, f32[16,1152]{1,0:T(8,128)S(1)}, u32[]{:S(2)}, u32[]{:S(2)}) collective-permute-start(f32[16,1152]{1,0:T(8,128)S(1)} %sums.4.a), channel_id=1, source_target_pairs={{16,0},{20,4},{0,16},{4,20},{17,1},{21,5},{1,17},{5,21},{18,2},{22... | collective-permute-start | bytes 221192 | tf_op jit(solution)/shard_map/ppermute | solution.py:29
  78.6 4.4 %collective-permute-start.19 = (f32[16,1152]{1,0:T(8,128)S(1)}, f32[16,1152]{1,0:T(8,128)S(1)}, u32[]{:S(2)}, u32[]{:S(2)}) collective-permute-start(f32[16,1152]{1,0:T(8,128)S(1)} %sums.4.a), channel_id=1, source_target_pairs={{20,0},{0,4},{4,16},{16,20},{21,1},{1,5},{5,17},{17,21},{22,2},{2,... | collective-permute-start | bytes 221192 | tf_op jit(solution)/shard_map/ppermute | solution.py:29
  83.1 6.8 %collective-permute-start.24 = (f16[128,1152]{1,0:T(8,128)(2,1)S(1)}, f16[128,1152]{1,0:T(8,128)(2,1)S(1)}, u32[]{:S(2)}, u32[]{:S(2)}) collective-permute-start(f16[128,1152]{1,0:T(8,128)(2,1)S(1)} %convert_element_type.13), channel_id=1, source_target_pairs={{16,0},{0,16},{17,1},{1,17},{18,2},{2,18},{19,3},{3,19},{20,4},{4,... | collective-permute-start | bytes 884744 | tf_op jit(solution)/shard_map/ppermute | solution.py:29
  83.2 3.6 %collective-permute-start.21 = (f32[16,1152]{1,0:T(8,128)S(1)}, f32[16,1152]{1,0:T(8,128)S(1)}, u32[]{:S(2)}, u32[]{:S(2)}) collective-permute-start(f32[16,1152]{1,0:T(8,128)S(1)} %sums.5.a), channel_id=1, source_target_pairs={{32,0},{64,32},{96,64},{0,96},{33,1},{65,33},{97,65},{1,97},{34,2}... | collective-permute-start | bytes 221192 | tf_op jit(solution)/shard_map/ppermute | solution.py:29
  83.8 4.8 %collective-permute-start.22 = (f32[16,1152]{1,0:T(8,128)S(1)}, f32[16,1152]{1,0:T(8,128)S(1)}, u32[]{:S(2)}, u32[]{:S(2)}) collective-permute-start(f32[16,1152]{1,0:T(8,128)S(1)} %sums.5.a), channel_id=1, source_target_pairs={{64,0},{96,32},{0,64},{32,96},{65,1},{97,33},{1,65},{33,97},{66,2}... | collective-permute-start | bytes 221192 | tf_op jit(solution)/shard_map/ppermute | solution.py:29
  84.3 5.0 %collective-permute-start.23 = (f32[16,1152]{1,0:T(8,128)S(1)}, f32[16,1152]{1,0:T(8,128)S(1)}, u32[]{:S(2)}, u32[]{:S(2)}) collective-permute-start(f32[16,1152]{1,0:T(8,128)S(1)} %sums.5.a), channel_id=1, source_target_pairs={{96,0},{0,32},{32,64},{64,96},{97,1},{1,33},{33,65},{65,97},{98,2}... | collective-permute-start | bytes 221192 | tf_op jit(solution)/shard_map/ppermute | solution.py:29
  89.9 4.2 %collective-permute-start.25 = (f32[64,1152]{1,0:T(8,128)S(1)}, f32[64,1152]{1,0:T(8,128)S(1)}, u32[]{:S(2)}, u32[]{:S(2)}) collective-permute-start(f32[64,1152]{1,0:T(8,128)S(1)} %places.1.a), channel_id=1, source_target_pairs={{8,0},{0,8},{9,1},{1,9},{10,2},{2,10},{11,3},{3,11},{12,4},{4,12},... | collective-permute-start | bytes 884744 | tf_op jit(solution)/shard_map/ppermute | solution.py:29
  (10 other events, 23.2 us)

commit v8 on v7

--- a/solution.py
+++ b/solution.py
@@ -13,11 +13,6 @@
 LOG2E = 1.4426950408889634
 REACH = 14.0
 MIB = 1 << 20
-
-
-def swapped(block, axis, flip):
-    n = lax.axis_size(axis)
-    return lax.ppermute(block, axis, [(i ^ flip, i) for i in range(n)])
 
 
 def tied(*values):
@@ -218,7 +213,7 @@
 
 def place_kernel(pairs, a, b, c, d, out):
     here, part = lax.axis_index("z"), a.shape[0]
-    for block, k in ((a, 0), (b, 1), (c, 2), (d, 3)):
+    for block, k in ((a, 0), (b, 2), (c, 3), (d, 1)):
         out[pl.ds(pl.multiple_of(((here + k) % 4) * part, part), part), :] = block[...] / pairs
 
 
@@ -352,7 +347,7 @@
     def small(kernel, name, operands, outs, scratch=()):
         return run(kernel, name, operands, outs, scratch, 1, False)
 
-    sizes = (256, 128)
+    sizes = (272, 112)
     chunks = small(
         away_kernel, "away_sums", [w2, both2, s2, s3], [shape((n + (16 if k == 0 else 0), width), F32) for k, n in enumerate(sizes)]
     )
@@ -371,26 +366,26 @@
         return small(sum_kernel, "sums", pieces, [quarter])[0]
 
     def gathered(block):
-        pieces = [block] + [from_ahead(block, "z", d) for d in (1, 2, 3)]
+        pieces = [block] + [from_ahead(block, "z", d) for d in (2, 3, 1)]
         return small(functools.partial(place_kernel, float(rows * 16)), "places", pieces, [grads])[0]
 
     quarter = shape((rank // 4, width), F32)
     sent = from_ahead(sent, "c", 1)
     sent, *chunks = tied(sent, *chunks)
     total = scattered(sent)
-    moved = from_ahead(chunks[0], "y", 1).astype(F32)
+    moved = from_ahead(chunks[0], "y", 1)
     (s1,) = small(twin_kernel, "twin_sums", [w_twin, both1, s1], [sums])
-    total = everyones("x", (1, 2, 3), from_ahead)(total)
+    total = everyones("x", (2, 3, 1), from_ahead)(total)
     total, c0, s1, chunk = tied(total, moved, s1, chunks[1])
     s1 = from_ahead(s1, "c", 1)
     total = everyones(("y", "h"), (1, 2, 3), from_ahead)(total)
     total, chunk, s1 = tied(total, chunk, s1)
-    moved = from_ahead(chunk, "y", 1).astype(F32)
+    moved = from_ahead(chunk, "y", 1)
     total = gathered(total)
     (near,) = small(near_kernel, "near_sums", [w_near, both1, w0, both2, s0, s1], [sums])
     total, c1, near = tied(total, moved, near)
     other = from_ahead(total, "c", 1)
-    (text_grad,) = small(finish_kernel, "finish", [near, c0, c1], [sums])
+    (text_grad,) = small(finish_kernel, "finish", [near, c0.astype(F32), c1.astype(F32)], [sums])
     grad_down, grad_up = small(join_kernel, "joined", [total, other], [grads, grads])
     grad_down = grad_down.T
     return text_grad[None], grad_down, grad_up

time: 95.3 us -> 93.9 us (0.985)
  waiting for transfers between devices: 17.4 us -> 12.8 us
  starting transfers between devices: 32.6 us -> 35.8 us
    ppermute x23, waiting for transfers between devices: 17.4 us -> 12.8 us  [from_ahead(): lax.ppermute(block, axis, [((i + distance) % n, i) for i in range(n)])]
    ppermute x23, starting transfers between devices: 26.9 us -> 30 us  [from_ahead(): lax.ppermute(block, axis, [((i + distance) % n, i) for i in range(n)])]
  transfers between devices with their start and end apart: 26 -> 26, of which waited for: 12 -> 10; matrix products, arithmetic and copies ran while one was open for 0% -> 0% of each run, Pallas kernels for 38% -> 38%
where the time goes in v8:
time: 93.9 us; the launch traced here: 93.5 us
  Pallas kernels  36.6 us (39%)
  starting transfers between devices  35.8 us (38%)
  waiting for transfers between devices  12.8 us (14%)
  local copies, waits for them, and re-layouts  5.91 us (6%)
  between operations  2.2 us (2%)
    pallas_call x19, Pallas kernels, run(): pl.pallas_call(kernel, in_specs=ins, out_specs=[spec] * len(outs), out_sh...  36 us
    ppermute x23, starting transfers between devices, from_ahead(): lax.ppermute(block, axis, [((i + distance) % n, i) for i in range(n)])  30 us
    ppermute x23, waiting for transfers between devices, from_ahead(): lax.ppermute(block, axis, [((i + distance) % n, i) for i in range(n)])  12.8 us
    unnamed x16, local copies, waits for them, and re-layouts  5.91 us
    ppermute x3, starting transfers between devices, turned(): lax.ppermute(block, ('z', 'c'), [(2 * step(z, c) + c, 2 * z + c) for z in...  5.73 us
  transfers between devices with their start and end apart: 26, of which 10 were waited for; matrix products, arithmetic and copies ran while one was open for 0% of the time, Pallas kernels for 38%

profile of v8, /device:TPU:1, one launch (start us, length us, event | category | flops | bytes accessed | tf_op | source)
XLA Modules:
  0.0 93.5 jit_solution(11358217619898823205)
XLA Ops:
  3.5 1.6 %collective-permute-start.2 = (bf16[384,1152]{1,0:T(8,128)(2,1)}, bf16[384,1152]{1,0:T(8,128)(2,1)S(1)}, u32[]{:S(2)}, u32[]{:S(2)}) collective-permute-start(bf16[384,1152]{1,0:T(8,128)(2,1)} %bitcast.5), channel_id=1, source_target_pairs={{32,0},{104,8},{64,32},{8,40},{96,64},{40,72},{0,96},{72,104},{33,... | collective-permute-start | bytes 2654216 | tf_op jit(solution)/shard_map/ppermute | solution.py:263
  5.2 2.1 %collective-permute-start.3 = (bf16[384,1152]{1,0:T(8,128)(2,1)}, bf16[384,1152]{1,0:T(8,128)(2,1)S(1)}, u32[]{:S(2)}, u32[]{:S(2)}) collective-permute-start(bf16[384,1152]{1,0:T(8,128)(2,1)} %bitcast.6), channel_id=1, source_target_pairs={{96,0},{40,8},{0,32},{72,40},{32,64},{104,72},{64,96},{8,104},{97,... | collective-permute-start | bytes 2654216 | tf_op jit(solution)/shard_map/ppermute | solution.py:263
  12.4 1.7 %copy-done.6 = bf16[1152,1152]{1,0:T(8,128)(2,1)S(1)} copy-done((bf16[1152,1152]{1,0:T(8,128)(2,1)S(1)}, bf16[1152,1152]{1,0:T(8,128)(2,1)}, u32[]{:S(2)}) %copy-start.6) | copy-done | bytes 2654232
  15.1 5.5 %own_rows.1 = (bf16[384,1280]{1,0:T(8,128)(2,1)S(1)}, bf16[1152,1280]{1,0:T(8,128)(2,1)S(1)}, bf16[128,768]{1,0:T(8,128)(2,1)S(1)}, f32[384,1152]{1,0:T(8,128)S(...) custom-call(f32[3]{0:T(128)S(1)} %consts.1, ...), custom_call_target="tpu_custom_call" | custom-call | flops 2582013440 | bytes 13860876 | tf_op jit(solution)/shard_map/own_rows/pallas_call | solution.py:232
  20.6 3.0 %collective-permute-done.1.texts.t1 = bf16[384,1152]{1,0:T(8,128)(2,1)S(1)} collective-permute-done((bf16[384,1152]{1,0:T(8,128)(2,1)}, bf16[384,1152]{1,0:T(8,128)(2,1)S(1)}, u32[]{:S(2)}, u32[]{:S(2)}) %collective-permute-start.1) | collective-permute-done | bytes 884768 | tf_op jit(solution)/shard_map/ppermute | solution.py:24
  24.4 2.1 %own_far.2 = (bf16[128,384]{1,0:T(8,128)(2,1)S(1)}, f32[384,1152]{1,0:T(8,128)S(1)}, f32[384,128]{1,0:T(8,128)S(1)}, f32[128,384]{1,0:T(8,128)S(1)}) custom-call(f32[3]{0:T(128)S(1)} %consts.1, bf16[384,1280]{1,0:T(8,128)(2,1)S(1)} %get-tuple-element.72.both, bf16[384,1152]{1,0:T(8,128)(2,1)S(1)} %collective-permute-done.1.texts.t1, ...), custom_call_target="tpu_custom_call" | custom-call | flops 747424960 | bytes 4472844 | tf_op jit(solution)/shard_map/own_far/pallas_call | solution.py:232
  26.6 2.0 %collective-permute-start.5 = (bf16[384,1152]{1,0:T(8,128)(2,1)S(1)}, bf16[384,1152]{1,0:T(8,128)(2,1)S(1)}, u32[]{:S(2)}, u32[]{:S(2)}) collective-permute-start(bf16[384,1152]{1,0:T(8,128)(2,1)S(1)} %collective-permute-done.2.a), channel_id=1, source_target_pairs={{32,0},{104,8},{64,32},{8,40},{96,64},{40,72},{0,96},{72,104},{33,... | collective-permute-start | bytes 2654216 | tf_op jit(solution)/shard_map/ppermute | solution.py:263
  28.5 2.1 %own_far.3 = (bf16[128,384]{1,0:T(8,128)(2,1)S(1)}, f32[384,1152]{1,0:T(8,128)S(1)}, f32[384,128]{1,0:T(8,128)S(1)}, f32[128,384]{1,0:T(8,128)S(1)}) custom-call(f32[3]{0:T(128)S(1)} %consts.1, bf16[384,1280]{1,0:T(8,128)(2,1)S(1)} %get-tuple-element.72.both, bf16[384,1152]{1,0:T(8,128)(2,1)S(1)} %collective-permute-done.4.texts.t3, ...), custom_call_target="tpu_custom_call" | custom-call | flops 747424960 | bytes 4472844 | tf_op jit(solution)/shard_map/own_far/pallas_call | solution.py:232
  30.7 6.7 %side_rows.1 = (bf16[768,1280]{1,0:T(8,128)(2,1)S(1)}, f32[384,128]{1,0:T(8,128)S(1)}, f32[384,128]{1,0:T(8,128)S(1)}, f32[128,768]{1,0:T(8,128)S(1)}, bf16[384,...) custom-call(f32[3]{0:T(128)S(1)} %consts.1, bf16[384,1152]{1,0:T(8,128)(2,1)S(1)} %collective-permute-done.2.a, ...), custom_call_target="tpu_custom_call" | custom-call | flops 3669177088 | bytes 11157516 | tf_op jit(solution)/shard_map/side_rows/pallas_call | solution.py:232
  37.4 2.8 %side_far.2 = (f32[384,1152]{1,0:T(8,128)S(1)}, f32[384,128]{1,0:T(8,128)S(1)}, f32[128,768]{1,0:T(8,128)S(1)}) custom-call(f32[3]{0:T(128)S(1)} %consts.1, bf16[768,1280]{1,0:T(8,128)(2,1)S(1)} %get-tuple-element.83.both.both0, bf16[384,1152]{1,0:T(8,128)(2,1)S(1)} %collective-permute-done.4.texts.t3, bf16[128,384]{1,0:T(8,128)(2,1)S(1)} %get-tuple-element.86.ups, ...), custom_call_target="tpu_custom_call" | custom-call | flops 1494849920 | bytes 7667724 | tf_op jit(solution)/shard_map/side_far/pallas_call | solution.py:232
  40.1 2.7 %collective-permute-start.9 = (f32[384,1152]{1,0:T(8,128)S(1)}, f32[384,1152]{1,0:T(8,128)S(1)}, u32[]{:S(2)}, u32[]{:S(2)}) collective-permute-start(f32[384,1152]{1,0:T(8,128)S(1)} %get-tuple-element.114), channel_id=1, source_target_pairs={{8,0},{0,8},{9,1},{1,9},{10,2},{2,10},{11,3},{3,11},{12,4},{4,12},... | collective-permute-start | bytes 5308424 | tf_op jit(solution)/shard_map/ppermute | solution.py:24
  42.8 1.8 %embed_far.1.e0 = bf16[384,1280]{1,0:T(8,128)(2,1)S(1)} custom-call(bf16[384,1152]{1,0:T(8,128)(2,1)S(1)} %collective-permute-done.5.images.x0, bf16[1152,1280]{1,0:T(8,128)(2,1)S(1)} %get-tuple-element.80.packed, bf16[64,1152]{1,0:T(8,128)(2,1)S(1)} %copy-done.5), custom_call_target="tpu_custom_call" | custom-call | flops 1087163648 | bytes 4964352 | tf_op jit(solution)/shard_map/embed_far/pallas_call | solution.py:232
  45.2 2.8 %side_far.3 = (f32[384,1152]{1,0:T(8,128)S(1)}, f32[384,128]{1,0:T(8,128)S(1)}, f32[128,768]{1,0:T(8,128)S(1)}) custom-call(f32[3]{0:T(128)S(1)} %consts.1, bf16[768,1280]{1,0:T(8,128)(2,1)S(1)} %get-tuple-element.83.both.both0, bf16[384,1152]{1,0:T(8,128)(2,1)S(1)} %collective-permute-done.1.texts.t1, bf16[128,384]{1,0:T(8,128)(2,1)S(1)} %get-tuple-element.93.ups.ups1, ...), custom_call_target="tpu_custom_call" | custom-call | flops 1494849920 | bytes 7667724 | tf_op jit(solution)/shard_map/side_far/pallas_call | solution.py:232
  49.1 4.7 %far_rows.1 = (f32[64,1152]{1,0:T(8,128)S(1)}, f32[64,1152]{1,0:T(8,128)S(1)}, bf16[768,1280]{1,0:T(8,128)(2,1)S(1)}, bf16[384,768]{1,0:T(8,128)(2,1)S(1)}, bf16[384,768]{1,0:T(8,128)(2,1)S(1)}) custom-call(f32[3]{0:T(128)S(1)} %consts.1, bf16[384,1152]{1,0:T(8,128)(2,1)S(1)} %collective-permute-done.5.images.x0, ...), custom_call_target="tpu_custom_call" | custom-call | flops 1698693120 | bytes 10518540 | tf_op jit(solution)/shard_map/far_rows/pallas_call | solution.py:232
  57.1 2.0 %collective-permute-start.10 = (f32[16,1152]{1,0:T(8,128)S(1)}, f32[16,1152]{1,0:T(8,128)S(1)}, u32[]{:S(2)}, u32[]{:S(2)}) collective-permute-start(f32[16,1152]{1,0:T(8,128)S(1)} %get-tuple-element.119), channel_id=1, source_target_pairs={{32,0},{64,32},{96,64},{0,96},{33,1},{65,33},{97,65},{1,97},{34,2}... | collective-permute-start | bytes 221192 | tf_op jit(solution)/shard_map/ppermute | solution.py:24
  60.6 3.3 %collective-permute-done.11.c = f32[16,1152]{1,0:T(8,128)S(1)} collective-permute-done((f32[16,1152]{1,0:T(8,128)S(1)}, f32[16,1152]{1,0:T(8,128)S(1)}, u32[]{:S(2)}, u32[]{:S(2)}) %collective-permute-start.11) | collective-permute-done | bytes 73760 | tf_op jit(solution)/shard_map/ppermute | solution.py:24
  65.0 2.8 %collective-permute-start.13 = (f32[16,1152]{1,0:T(8,128)S(1)}, f32[16,1152]{1,0:T(8,128)S(1)}, u32[]{:S(2)}, u32[]{:S(2)}) collective-permute-start(f32[16,1152]{1,0:T(8,128)S(1)} %sums.3.a), channel_id=1, source_target_pairs={{2,0},{3,1},{0,2},{1,3},{6,4},{7,5},{4,6},{5,7},{10,8},{11,9},{8,1... | collective-permute-start | bytes 221192 | tf_op jit(solution)/shard_map/ppermute | solution.py:24
  68.1 2.3 %collective-permute-start.15 = (f32[16,1152]{1,0:T(8,128)S(1)}, f32[16,1152]{1,0:T(8,128)S(1)}, u32[]{:S(2)}, u32[]{:S(2)}) collective-permute-start(f32[16,1152]{1,0:T(8,128)S(1)} %sums.3.a), channel_id=1, source_target_pairs={{1,0},{2,1},{3,2},{0,3},{5,4},{6,5},{7,6},{4,7},{9,8},{10,9},{11,1... | collective-permute-start | bytes 221192 | tf_op jit(solution)/shard_map/ppermute | solution.py:24
  72.8 2.6 %collective-permute-start.20 = (f32[384,1152]{1,0:T(8,128)S(1)}, f32[384,1152]{1,0:T(8,128)S(1)}, u32[]{:S(2)}, u32[]{:S(2)}) collective-permute-start(f32[384,1152]{1,0:T(8,128)S(1)} %twin_sums.1), channel_id=1, source_target_pairs={{8,0},{0,8},{9,1},{1,9},{10,2},{2,10},{11,3},{3,11},{12,4},{4,12},... | collective-permute-start | bytes 5308424 | tf_op jit(solution)/shard_map/ppermute | solution.py:24
  75.4 1.9 %collective-permute-start.17 = (f32[16,1152]{1,0:T(8,128)S(1)}, f32[16,1152]{1,0:T(8,128)S(1)}, u32[]{:S(2)}, u32[]{:S(2)}) collective-permute-start(f32[16,1152]{1,0:T(8,128)S(1)} %sums.4.a), channel_id=1, source_target_pairs={{4,0},{16,4},{20,16},{0,20},{5,1},{17,5},{21,17},{1,21},{6,2},{18,... | collective-permute-start | bytes 221192 | tf_op jit(solution)/shard_map/ppermute | solution.py:24
  77.7 1.6 %collective-permute-start.19 = (f32[16,1152]{1,0:T(8,128)S(1)}, f32[16,1152]{1,0:T(8,128)S(1)}, u32[]{:S(2)}, u32[]{:S(2)}) collective-permute-start(f32[16,1152]{1,0:T(8,128)S(1)} %sums.4.a), channel_id=1, source_target_pairs={{20,0},{0,4},{4,16},{16,20},{21,1},{1,5},{5,17},{17,21},{22,2},{2,... | collective-permute-start | bytes 221192 | tf_op jit(solution)/shard_map/ppermute | solution.py:24
  83.5 2.5 %collective-permute-start.23 = (f32[16,1152]{1,0:T(8,128)S(1)}, f32[16,1152]{1,0:T(8,128)S(1)}, u32[]{:S(2)}, u32[]{:S(2)}) collective-permute-start(f32[16,1152]{1,0:T(8,128)S(1)} %sums.5.a), channel_id=1, source_target_pairs={{32,0},{64,32},{96,64},{0,96},{33,1},{65,33},{97,65},{1,97},{34,2}... | collective-permute-start | bytes 221192 | tf_op jit(solution)/shard_map/ppermute | solution.py:24
  86.0 1.7 %near_sums.1.near = f32[384,1152]{1,0:T(8,128)S(1)} custom-call(bf16[384,768]{1,0:T(8,128)(2,1)S(1)} %get-tuple-element.131.w0, bf16[768,1280]{1,0:T(8,128)(2,1)S(1)} %get-tuple-element.83.both.both0, bf16[384,768]{1,0:T(8,128)(2,1)S(1)} %get-tuple-element.132.w1, bf16[768,1280]{1,0:T(8,128)(2,1)S(1)} %get-tuple-element.112.both.both1, ...), custom_call_target="tpu_custom_call" | custom-call | flops 1 | bytes 10420224 | tf_op jit(solution)/shard_map/near_sums/pallas_call | solution.py:232
  88.2 2.9 %collective-permute-start.25 = (f32[64,1152]{1,0:T(8,128)S(1)}, f32[64,1152]{1,0:T(8,128)S(1)}, u32[]{:S(2)}, u32[]{:S(2)}) collective-permute-start(f32[64,1152]{1,0:T(8,128)S(1)} %places.1.a), channel_id=1, source_target_pairs={{8,0},{0,8},{9,1},{1,9},{10,2},{2,10},{11,3},{3,11},{12,4},{4,12},... | collective-permute-start | bytes 884744 | tf_op jit(solution)/shard_map/ppermute | solution.py:24
  (68 shorter events, 26.2 us)
Async XLA Ops:
  0.6 8.6 %collective-permute-start = (bf16[384,1152]{1,0:T(8,128)(2,1)}, bf16[384,1152]{1,0:T(8,128)(2,1)S(1)}, u32[]{:S(2)}, u32[]{:S(2)}) collective-permute-start(bf16[384,1152]{1,0:T(8,128)(2,1)} %bitcast.9), channel_id=1, source_target_pairs={{8,0},{0,8},{9,1},{1,9},{10,2},{2,10},{11,3},{3,11},{12,4},{4,12},... | collective-permute-start | bytes 2654216 | tf_op jit(solution)/shard_map/ppermute | solution.py:24
  2.1 21.4 %collective-permute-start.1 = (bf16[384,1152]{1,0:T(8,128)(2,1)}, bf16[384,1152]{1,0:T(8,128)(2,1)S(1)}, u32[]{:S(2)}, u32[]{:S(2)}) collective-permute-start(bf16[384,1152]{1,0:T(8,128)(2,1)} %bitcast.10), channel_id=1, source_target_pairs={{16,0},{0,16},{17,1},{1,17},{18,2},{2,18},{19,3},{3,19},{20,4},{4,... | collective-permute-start | bytes 2654216 | tf_op jit(solution)/shard_map/ppermute | solution.py:24
  3.5 23.0 %collective-permute-start.2 = (bf16[384,1152]{1,0:T(8,128)(2,1)}, bf16[384,1152]{1,0:T(8,128)(2,1)S(1)}, u32[]{:S(2)}, u32[]{:S(2)}) collective-permute-start(bf16[384,1152]{1,0:T(8,128)(2,1)} %bitcast.5), channel_id=1, source_target_pairs={{32,0},{104,8},{64,32},{8,40},{96,64},{40,72},{0,96},{72,104},{33,... | collective-permute-start | bytes 2654216 | tf_op jit(solution)/shard_map/ppermute | solution.py:263
  5.2 21.4 %collective-permute-start.3 = (bf16[384,1152]{1,0:T(8,128)(2,1)}, bf16[384,1152]{1,0:T(8,128)(2,1)S(1)}, u32[]{:S(2)}, u32[]{:S(2)}) collective-permute-start(bf16[384,1152]{1,0:T(8,128)(2,1)} %bitcast.6), channel_id=1, source_target_pairs={{96,0},{40,8},{0,32},{72,40},{32,64},{104,72},{64,96},{8,104},{97,... | collective-permute-start | bytes 2654216 | tf_op jit(solution)/shard_map/ppermute | solution.py:263
  26.6 16.2 %collective-permute-start.5 = (bf16[384,1152]{1,0:T(8,128)(2,1)S(1)}, bf16[384,1152]{1,0:T(8,128)(2,1)S(1)}, u32[]{:S(2)}, u32[]{:S(2)}) collective-permute-start(bf16[384,1152]{1,0:T(8,128)(2,1)S(1)} %collective-permute-done.2.a), channel_id=1, source_target_pairs={{32,0},{104,8},{64,32},{8,40},{96,64},{40,72},{0,96},{72,104},{33,... | collective-permute-start | bytes 2654216 | tf_op jit(solution)/shard_map/ppermute | solution.py:263
  40.1 14.1 %collective-permute-start.9 = (f32[384,1152]{1,0:T(8,128)S(1)}, f32[384,1152]{1,0:T(8,128)S(1)}, u32[]{:S(2)}, u32[]{:S(2)}) collective-permute-start(f32[384,1152]{1,0:T(8,128)S(1)} %get-tuple-element.114), channel_id=1, source_target_pairs={{8,0},{0,8},{9,1},{1,9},{10,2},{2,10},{11,3},{3,11},{12,4},{4,12},... | collective-permute-start | bytes 5308424 | tf_op jit(solution)/shard_map/ppermute | solution.py:24
  44.6 4.5 %collective-permute-start.7 = (bf16[384,1280]{1,0:T(8,128)(2,1)S(1)}, bf16[384,1280]{1,0:T(8,128)(2,1)S(1)}, u32[]{:S(2)}, u32[]{:S(2)}) collective-permute-start(bf16[384,1280]{1,0:T(8,128)(2,1)S(1)} %embed_far.1.e0), channel_id=1, source_target_pairs={{8,0},{0,8},{9,1},{1,9},{10,2},{2,10},{11,3},{3,11},{12,4},{4,12},... | collective-permute-start | bytes 2949128 | tf_op jit(solution)/shard_map/ppermute | solution.py:24
  44.7 4.4 %collective-permute-start.6 = (bf16[384,1152]{1,0:T(8,128)(2,1)S(1)}, bf16[384,1152]{1,0:T(8,128)(2,1)S(1)}, u32[]{:S(2)}, u32[]{:S(2)}) collective-permute-start(bf16[384,1152]{1,0:T(8,128)(2,1)S(1)} %collective-permute-done.5.images.x0), channel_id=1, source_target_pairs={{8,0},{0,8},{9,1},{1,9},{10,2},{2,10},{11,3},{3,11},{12,4},{4,12},... | collective-permute-start | bytes 2654216 | tf_op jit(solution)/shard_map/ppermute | solution.py:24
  55.8 17.1 %collective-permute-start.16 = (f16[288,1152]{1,0:T(8,128)(2,1)S(1)}, f16[288,1152]{1,0:T(8,128)(2,1)S(1)}, u32[]{:S(2)}, u32[]{:S(2)}) collective-permute-start(f16[288,1152]{1,0:T(8,128)(2,1)S(1)} %convert_element_type.12), channel_id=1, source_target_pairs={{16,0},{0,16},{17,1},{1,17},{18,2},{2,18},{19,3},{3,19},{20,4},{4,... | collective-permute-start | bytes 1990664 | tf_op jit(solution)/shard_map/ppermute | solution.py:24
  57.1 3.6 %collective-permute-start.10 = (f32[16,1152]{1,0:T(8,128)S(1)}, f32[16,1152]{1,0:T(8,128)S(1)}, u32[]{:S(2)}, u32[]{:S(2)}) collective-permute-start(f32[16,1152]{1,0:T(8,128)S(1)} %get-tuple-element.119), channel_id=1, source_target_pairs={{32,0},{64,32},{96,64},{0,96},{33,1},{65,33},{97,65},{1,97},{34,2}... | collective-permute-start | bytes 221192 | tf_op jit(solution)/shard_map/ppermute | solution.py:24
  59.1 4.8 %collective-permute-start.11 = (f32[16,1152]{1,0:T(8,128)S(1)}, f32[16,1152]{1,0:T(8,128)S(1)}, u32[]{:S(2)}, u32[]{:S(2)}) collective-permute-start(f32[16,1152]{1,0:T(8,128)S(1)} %get-tuple-element.120), channel_id=1, source_target_pairs={{64,0},{96,32},{0,64},{32,96},{65,1},{97,33},{1,65},{33,97},{66,2}... | collective-permute-start | bytes 221192 | tf_op jit(solution)/shard_map/ppermute | solution.py:24
  59.1 5.8 %collective-permute-start.12 = (f32[16,1152]{1,0:T(8,128)S(1)}, f32[16,1152]{1,0:T(8,128)S(1)}, u32[]{:S(2)}, u32[]{:S(2)}) collective-permute-start(f32[16,1152]{1,0:T(8,128)S(1)} %get-tuple-element.121), channel_id=1, source_target_pairs={{96,0},{0,32},{32,64},{64,96},{97,1},{1,33},{33,65},{65,97},{98,2}... | collective-permute-start | bytes 221192 | tf_op jit(solution)/shard_map/ppermute | solution.py:24
  65.0 6.4 %collective-permute-start.13 = (f32[16,1152]{1,0:T(8,128)S(1)}, f32[16,1152]{1,0:T(8,128)S(1)}, u32[]{:S(2)}, u32[]{:S(2)}) collective-permute-start(f32[16,1152]{1,0:T(8,128)S(1)} %sums.3.a), channel_id=1, source_target_pairs={{2,0},{3,1},{0,2},{1,3},{6,4},{7,5},{4,6},{5,7},{10,8},{11,9},{8,1... | collective-permute-start | bytes 221192 | tf_op jit(solution)/shard_map/ppermute | solution.py:24
  67.7 5.0 %collective-permute-start.14 = (f32[16,1152]{1,0:T(8,128)S(1)}, f32[16,1152]{1,0:T(8,128)S(1)}, u32[]{:S(2)}, u32[]{:S(2)}) collective-permute-start(f32[16,1152]{1,0:T(8,128)S(1)} %sums.3.a), channel_id=1, source_target_pairs={{3,0},{0,1},{1,2},{2,3},{7,4},{4,5},{5,6},{6,7},{11,8},{8,9},{9,10... | collective-permute-start | bytes 221192 | tf_op jit(solution)/shard_map/ppermute | solution.py:24
  68.1 4.7 %collective-permute-start.15 = (f32[16,1152]{1,0:T(8,128)S(1)}, f32[16,1152]{1,0:T(8,128)S(1)}, u32[]{:S(2)}, u32[]{:S(2)}) collective-permute-start(f32[16,1152]{1,0:T(8,128)S(1)} %sums.3.a), channel_id=1, source_target_pairs={{1,0},{2,1},{3,2},{0,3},{5,4},{6,5},{7,6},{4,7},{9,8},{10,9},{11,1... | collective-permute-start | bytes 221192 | tf_op jit(solution)/shard_map/ppermute | solution.py:24
  72.8 9.3 %collective-permute-start.20 = (f32[384,1152]{1,0:T(8,128)S(1)}, f32[384,1152]{1,0:T(8,128)S(1)}, u32[]{:S(2)}, u32[]{:S(2)}) collective-permute-start(f32[384,1152]{1,0:T(8,128)S(1)} %twin_sums.1), channel_id=1, source_target_pairs={{8,0},{0,8},{9,1},{1,9},{10,2},{2,10},{11,3},{3,11},{12,4},{4,12},... | collective-permute-start | bytes 5308424 | tf_op jit(solution)/shard_map/ppermute | solution.py:24
  75.4 5.3 %collective-permute-start.17 = (f32[16,1152]{1,0:T(8,128)S(1)}, f32[16,1152]{1,0:T(8,128)S(1)}, u32[]{:S(2)}, u32[]{:S(2)}) collective-permute-start(f32[16,1152]{1,0:T(8,128)S(1)} %sums.4.a), channel_id=1, source_target_pairs={{4,0},{16,4},{20,16},{0,20},{5,1},{17,5},{21,17},{1,21},{6,2},{18,... | collective-permute-start | bytes 221192 | tf_op jit(solution)/shard_map/ppermute | solution.py:24
  77.3 3.5 %collective-permute-start.18 = (f32[16,1152]{1,0:T(8,128)S(1)}, f32[16,1152]{1,0:T(8,128)S(1)}, u32[]{:S(2)}, u32[]{:S(2)}) collective-permute-start(f32[16,1152]{1,0:T(8,128)S(1)} %sums.4.a), channel_id=1, source_target_pairs={{16,0},{20,4},{0,16},{4,20},{17,1},{21,5},{1,17},{5,21},{18,2},{22... | collective-permute-start | bytes 221192 | tf_op jit(solution)/shard_map/ppermute | solution.py:24
  77.7 4.4 %collective-permute-start.19 = (f32[16,1152]{1,0:T(8,128)S(1)}, f32[16,1152]{1,0:T(8,128)S(1)}, u32[]{:S(2)}, u32[]{:S(2)}) collective-permute-start(f32[16,1152]{1,0:T(8,128)S(1)} %sums.4.a), channel_id=1, source_target_pairs={{20,0},{0,4},{4,16},{16,20},{21,1},{1,5},{5,17},{17,21},{22,2},{2,... | collective-permute-start | bytes 221192 | tf_op jit(solution)/shard_map/ppermute | solution.py:24
  82.2 6.0 %collective-permute-start.24 = (f16[112,1152]{1,0:T(8,128)(2,1)S(1)}, f16[112,1152]{1,0:T(8,128)(2,1)S(1)}, u32[]{:S(2)}, u32[]{:S(2)}) collective-permute-start(f16[112,1152]{1,0:T(8,128)(2,1)S(1)} %convert_element_type.13), channel_id=1, source_target_pairs={{16,0},{0,16},{17,1},{1,17},{18,2},{2,18},{19,3},{3,19},{20,4},{4,... | collective-permute-start | bytes 774152 | tf_op jit(solution)/shard_map/ppermute | solution.py:24
  82.3 5.4 %collective-permute-start.21 = (f32[16,1152]{1,0:T(8,128)S(1)}, f32[16,1152]{1,0:T(8,128)S(1)}, u32[]{:S(2)}, u32[]{:S(2)}) collective-permute-start(f32[16,1152]{1,0:T(8,128)S(1)} %sums.5.a), channel_id=1, source_target_pairs={{64,0},{96,32},{0,64},{32,96},{65,1},{97,33},{1,65},{33,97},{66,2}... | collective-permute-start | bytes 221192 | tf_op jit(solution)/shard_map/ppermute | solution.py:24
  83.3 4.5 %collective-permute-start.22 = (f32[16,1152]{1,0:T(8,128)S(1)}, f32[16,1152]{1,0:T(8,128)S(1)}, u32[]{:S(2)}, u32[]{:S(2)}) collective-permute-start(f32[16,1152]{1,0:T(8,128)S(1)} %sums.5.a), channel_id=1, source_target_pairs={{96,0},{0,32},{32,64},{64,96},{97,1},{1,33},{33,65},{65,97},{98,2}... | collective-permute-start | bytes 221192 | tf_op jit(solution)/shard_map/ppermute | solution.py:24
  83.5 4.3 %collective-permute-start.23 = (f32[16,1152]{1,0:T(8,128)S(1)}, f32[16,1152]{1,0:T(8,128)S(1)}, u32[]{:S(2)}, u32[]{:S(2)}) collective-permute-start(f32[16,1152]{1,0:T(8,128)S(1)} %sums.5.a), channel_id=1, source_target_pairs={{32,0},{64,32},{96,64},{0,96},{33,1},{65,33},{97,65},{1,97},{34,2}... | collective-permute-start | bytes 221192 | tf_op jit(solution)/shard_map/ppermute | solution.py:24
  88.2 4.5 %collective-permute-start.25 = (f32[64,1152]{1,0:T(8,128)S(1)}, f32[64,1152]{1,0:T(8,128)S(1)}, u32[]{:S(2)}, u32[]{:S(2)}) collective-permute-start(f32[64,1152]{1,0:T(8,128)S(1)} %places.1.a), channel_id=1, source_target_pairs={{8,0},{0,8},{9,1},{1,9},{10,2},{2,10},{11,3},{3,11},{12,4},{4,12},... | collective-permute-start | bytes 884744 | tf_op jit(solution)/shard_map/ppermute | solution.py:24
  (10 other events, 23.2 us)

commit v9 on v8

--- a/solution.py
+++ b/solution.py
@@ -119,6 +119,14 @@
 def own_far_kernel(consts, both, texts, up, inner0, ups, s, h, inner, w):
     width = texts.shape[1]
     text_ups(texts, up, ups, 0)
+    w[...] = gate(mm_nt(texts[...], both[:, :width]), consts)
+    sums = mm(w[...], both[...])
+    s[...], h[...] = sums[:, :width], sums[:, width:]
+    inner[...] = inner0[...] + mm(ups[...], w[...])
+
+
+def own_far_given_kernel(consts, both, texts, ups, inner0, s, h, inner, w):
+    width = texts.shape[1]
     w[...] = gate(mm_nt(texts[...], both[:, :width]), consts)
     sums = mm(w[...], both[...])
     s[...], h[...] = sums[:, :width], sums[:, width:]
@@ -306,6 +314,7 @@
         )
 
     ups2, s2, h2, inner0 = own_far(across, inner0)
+    ups3 = from_ahead(ups2, "c", 1)
     inner0, ahead, behind, across_twin = tied(inner0, ahead, behind, across_twin)
     far = turned(ahead, 1)
     both1, h0, h1, inner1, w_near, w_twin = run(
@@ -316,7 +325,14 @@
         [],
         6.4 * unit + 2 * pair_flops,
     )
-    ups3, s3, h3, inner0 = own_far(across_twin, inner0)
+    s3, h3, inner0 = run(
+        own_far_given_kernel,
+        "own_far",
+        [consts, both0, across_twin, ups3, inner0],
+        [sums, narrow, inner_own],
+        [square],
+        pair_flops,
+    )
     s3, h3, inner1 = side_far(across_twin, ups3, inner1, s3, h3)
     inner1, far = tied(inner1, far)
     far_twin = from_ahead(far, "c", 1)

time: 93.9 us -> 94 us (level)
  waiting for transfers between devices: 12.8 us -> 14.2 us
  starting transfers between devices: 35.8 us -> 34.6 us
    ppermute x23 -> x24, waiting for transfers between devices: 12.8 us -> 14.2 us  [from_ahead(): lax.ppermute(block, axis, [((i + distance) % n, i) for i in range(n)])]
    ppermute x23 -> x24, starting transfers between devices: 30 us -> 29.1 us  [from_ahead(): lax.ppermute(block, axis, [((i + distance) % n, i) for i in range(n)])]
  transfers between devices with their start and end apart: 26 -> 27, of which waited for: 10 -> 12; matrix products, arithmetic and copies ran while one was open for 0% -> 0% of each run, Pallas kernels for 38% -> 38%
where the time goes in v9:
time: 94 us; the launch traced here: 93.6 us
  Pallas kernels  36.4 us (39%)
  starting transfers between devices  34.6 us (37%)
  waiting for transfers between devices  14.2 us (15%)
  local copies, waits for them, and re-layouts  5.91 us (6%)
  between operations  2.2 us (2%)
    pallas_call x19, Pallas kernels, run(): pl.pallas_call(kernel, in_specs=ins, out_specs=[spec] * len(outs), out_sh...  35.8 us
    ppermute x24, starting transfers between devices, from_ahead(): lax.ppermute(block, axis, [((i + distance) % n, i) for i in range(n)])  29.1 us
    ppermute x24, waiting for transfers between devices, from_ahead(): lax.ppermute(block, axis, [((i + distance) % n, i) for i in range(n)])  14.2 us
    unnamed x16, local copies, waits for them, and re-layouts  5.91 us
    ppermute x3, starting transfers between devices, turned(): lax.ppermute(block, ('z', 'c'), [(2 * step(z, c) + c, 2 * z + c) for z in...  5.55 us
  transfers between devices with their start and end apart: 27, of which 12 were waited for; matrix products, arithmetic and copies ran while one was open for 0% of the time, Pallas kernels for 38%

profile of v9, /device:TPU:1, one launch (start us, length us, event | category | flops | bytes accessed | tf_op | source)
XLA Modules:
  0.0 93.6 jit_solution(17973739504406354298)
XLA Ops:
  3.5 1.6 %collective-permute-start.2 = (bf16[384,1152]{1,0:T(8,128)(2,1)}, bf16[384,1152]{1,0:T(8,128)(2,1)S(1)}, u32[]{:S(2)}, u32[]{:S(2)}) collective-permute-start(bf16[384,1152]{1,0:T(8,128)(2,1)} %bitcast.5), channel_id=1, source_target_pairs={{32,0},{104,8},{64,32},{8,40},{96,64},{40,72},{0,96},{72,104},{33,... | collective-permute-start | bytes 2654216 | tf_op jit(solution)/shard_map/ppermute | solution.py:271
  5.2 2.1 %collective-permute-start.3 = (bf16[384,1152]{1,0:T(8,128)(2,1)}, bf16[384,1152]{1,0:T(8,128)(2,1)S(1)}, u32[]{:S(2)}, u32[]{:S(2)}) collective-permute-start(bf16[384,1152]{1,0:T(8,128)(2,1)} %bitcast.6), channel_id=1, source_target_pairs={{96,0},{40,8},{0,32},{72,40},{32,64},{104,72},{64,96},{8,104},{97,... | collective-permute-start | bytes 2654216 | tf_op jit(solution)/shard_map/ppermute | solution.py:271
  12.4 1.7 %copy-done.6 = bf16[1152,1152]{1,0:T(8,128)(2,1)S(1)} copy-done((bf16[1152,1152]{1,0:T(8,128)(2,1)S(1)}, bf16[1152,1152]{1,0:T(8,128)(2,1)}, u32[]{:S(2)}) %copy-start.6) | copy-done | bytes 2654232
  15.1 5.5 %own_rows.1 = (bf16[384,1280]{1,0:T(8,128)(2,1)S(1)}, bf16[1152,1280]{1,0:T(8,128)(2,1)S(1)}, bf16[128,768]{1,0:T(8,128)(2,1)S(1)}, f32[384,1152]{1,0:T(8,128)S(...) custom-call(f32[3]{0:T(128)S(1)} %consts.1, ...), custom_call_target="tpu_custom_call" | custom-call | flops 2582013440 | bytes 13860876 | tf_op jit(solution)/shard_map/own_rows/pallas_call | solution.py:240
  20.6 3.0 %collective-permute-done.1.texts.t1 = bf16[384,1152]{1,0:T(8,128)(2,1)S(1)} collective-permute-done((bf16[384,1152]{1,0:T(8,128)(2,1)}, bf16[384,1152]{1,0:T(8,128)(2,1)S(1)}, u32[]{:S(2)}, u32[]{:S(2)}) %collective-permute-start.1) | collective-permute-done | bytes 884768 | tf_op jit(solution)/shard_map/ppermute | solution.py:24
  24.4 2.1 %own_far.2 = (bf16[128,384]{1,0:T(8,128)(2,1)S(1)}, f32[384,1152]{1,0:T(8,128)S(1)}, f32[384,128]{1,0:T(8,128)S(1)}, f32[128,384]{1,0:T(8,128)S(1)}) custom-call(f32[3]{0:T(128)S(1)} %consts.1, bf16[384,1280]{1,0:T(8,128)(2,1)S(1)} %get-tuple-element.71.both, bf16[384,1152]{1,0:T(8,128)(2,1)S(1)} %collective-permute-done.1.texts.t1, ...), custom_call_target="tpu_custom_call" | custom-call | flops 747424960 | bytes 4472844 | tf_op jit(solution)/shard_map/own_far/pallas_call | solution.py:240
  26.6 1.8 %collective-permute-start.6 = (bf16[384,1152]{1,0:T(8,128)(2,1)S(1)}, bf16[384,1152]{1,0:T(8,128)(2,1)S(1)}, u32[]{:S(2)}, u32[]{:S(2)}) collective-permute-start(bf16[384,1152]{1,0:T(8,128)(2,1)S(1)} %collective-permute-done.2.a), channel_id=1, source_target_pairs={{32,0},{104,8},{64,32},{8,40},{96,64},{40,72},{0,96},{72,104},{33,... | collective-permute-start | bytes 2654216 | tf_op jit(solution)/shard_map/ppermute | solution.py:271
  28.4 2.7 %collective-permute-start.5 = (bf16[128,384]{1,0:T(8,128)(2,1)S(1)}, bf16[128,384]{1,0:T(8,128)(2,1)S(1)}, u32[]{:S(2)}, u32[]{:S(2)}) collective-permute-start(bf16[128,384]{1,0:T(8,128)(2,1)S(1)} %get-tuple-element.84.ups.ups1), channel_id=1, source_target_pairs={{8,0},{0,8},{9,1},{1,9},{10,2},{2,10},{11,3},{3,11},{12,4},{4,12},... | collective-permute-start | bytes 294920 | tf_op jit(solution)/shard_map/ppermute | solution.py:24
  32.0 1.9 %own_far.3 = (f32[384,1152]{1,0:T(8,128)S(1)}, f32[384,128]{1,0:T(8,128)S(1)}, f32[128,384]{1,0:T(8,128)S(1)}) custom-call(f32[3]{0:T(128)S(1)} %consts.1, bf16[384,1280]{1,0:T(8,128)(2,1)S(1)} %get-tuple-element.71.both, bf16[384,1152]{1,0:T(8,128)(2,1)S(1)} %collective-permute-done.4.texts.t3, bf16[128,384]{1,0:T(8,128)(2,1)S(1)} %collective-permute-done.5.ups, ...), custom_call_target="tpu_custom_call" | custom-call | flops 747424960 | bytes 4325388 | tf_op jit(solution)/shard_map/own_far/pallas_call | solution.py:240
  34.0 6.7 %side_rows.1 = (bf16[768,1280]{1,0:T(8,128)(2,1)S(1)}, f32[384,128]{1,0:T(8,128)S(1)}, f32[384,128]{1,0:T(8,128)S(1)}, f32[128,768]{1,0:T(8,128)S(1)}, bf16[384,...) custom-call(f32[3]{0:T(128)S(1)} %consts.1, bf16[384,1152]{1,0:T(8,128)(2,1)S(1)} %collective-permute-done.2.a, ...), custom_call_target="tpu_custom_call" | custom-call | flops 3669177088 | bytes 11157516 | tf_op jit(solution)/shard_map/side_rows/pallas_call | solution.py:240
  40.7 2.8 %side_far.2 = (f32[384,1152]{1,0:T(8,128)S(1)}, f32[384,128]{1,0:T(8,128)S(1)}, f32[128,768]{1,0:T(8,128)S(1)}) custom-call(f32[3]{0:T(128)S(1)} %consts.1, bf16[768,1280]{1,0:T(8,128)(2,1)S(1)} %get-tuple-element.82.both.both0, bf16[384,1152]{1,0:T(8,128)(2,1)S(1)} %collective-permute-done.4.texts.t3, bf16[128,384]{1,0:T(8,128)(2,1)S(1)} %collective-permute-done.5.ups, ...), custom_call_target="tpu_custom_call" | custom-call | flops 1494849920 | bytes 7667724 | tf_op jit(solution)/shard_map/side_far/pallas_call | solution.py:240
  43.9 1.8 %embed_far.1.e0 = bf16[384,1280]{1,0:T(8,128)(2,1)S(1)} custom-call(bf16[384,1152]{1,0:T(8,128)(2,1)S(1)} %collective-permute-done.6.images.x0, bf16[1152,1280]{1,0:T(8,128)(2,1)S(1)} %get-tuple-element.79.packed, bf16[64,1152]{1,0:T(8,128)(2,1)S(1)} %copy-done.5), custom_call_target="tpu_custom_call" | custom-call | flops 1087163648 | bytes 4964352 | tf_op jit(solution)/shard_map/embed_far/pallas_call | solution.py:240
  46.2 2.8 %side_far.3 = (f32[384,1152]{1,0:T(8,128)S(1)}, f32[384,128]{1,0:T(8,128)S(1)}, f32[128,768]{1,0:T(8,128)S(1)}) custom-call(f32[3]{0:T(128)S(1)} %consts.1, bf16[768,1280]{1,0:T(8,128)(2,1)S(1)} %get-tuple-element.82.both.both0, bf16[384,1152]{1,0:T(8,128)(2,1)S(1)} %collective-permute-done.1.texts.t1, bf16[128,384]{1,0:T(8,128)(2,1)S(1)} %get-tuple-element.84.ups.ups1, ...), custom_call_target="tpu_custom_call" | custom-call | flops 1494849920 | bytes 7667724 | tf_op jit(solution)/shard_map/side_far/pallas_call | solution.py:240
  50.2 4.7 %far_rows.1 = (f32[64,1152]{1,0:T(8,128)S(1)}, f32[64,1152]{1,0:T(8,128)S(1)}, bf16[768,1280]{1,0:T(8,128)(2,1)S(1)}, bf16[384,768]{1,0:T(8,128)(2,1)S(1)}, bf16[384,768]{1,0:T(8,128)(2,1)S(1)}) custom-call(f32[3]{0:T(128)S(1)} %consts.1, bf16[384,1152]{1,0:T(8,128)(2,1)S(1)} %collective-permute-done.6.images.x0, ...), custom_call_target="tpu_custom_call" | custom-call | flops 1698693120 | bytes 10518540 | tf_op jit(solution)/shard_map/far_rows/pallas_call | solution.py:240
  60.0 1.8 %collective-permute-done.11.b = f32[16,1152]{1,0:T(8,128)S(1)} collective-permute-done((f32[16,1152]{1,0:T(8,128)S(1)}, f32[16,1152]{1,0:T(8,128)S(1)}, u32[]{:S(2)}, u32[]{:S(2)}) %collective-permute-start.11) | collective-permute-done | bytes 73760 | tf_op jit(solution)/shard_map/ppermute | solution.py:24
  61.8 2.1 %collective-permute-done.12.c = f32[16,1152]{1,0:T(8,128)S(1)} collective-permute-done((f32[16,1152]{1,0:T(8,128)S(1)}, f32[16,1152]{1,0:T(8,128)S(1)}, u32[]{:S(2)}, u32[]{:S(2)}) %collective-permute-start.12) | collective-permute-done | bytes 73760 | tf_op jit(solution)/shard_map/ppermute | solution.py:24
  65.4 2.8 %collective-permute-start.14 = (f32[16,1152]{1,0:T(8,128)S(1)}, f32[16,1152]{1,0:T(8,128)S(1)}, u32[]{:S(2)}, u32[]{:S(2)}) collective-permute-start(f32[16,1152]{1,0:T(8,128)S(1)} %sums.3.a), channel_id=1, source_target_pairs={{2,0},{3,1},{0,2},{1,3},{6,4},{7,5},{4,6},{5,7},{10,8},{11,9},{8,1... | collective-permute-start | bytes 221192 | tf_op jit(solution)/shard_map/ppermute | solution.py:24
  68.5 2.4 %collective-permute-start.16 = (f32[16,1152]{1,0:T(8,128)S(1)}, f32[16,1152]{1,0:T(8,128)S(1)}, u32[]{:S(2)}, u32[]{:S(2)}) collective-permute-start(f32[16,1152]{1,0:T(8,128)S(1)} %sums.3.a), channel_id=1, source_target_pairs={{1,0},{2,1},{3,2},{0,3},{5,4},{6,5},{7,6},{4,7},{9,8},{10,9},{11,1... | collective-permute-start | bytes 221192 | tf_op jit(solution)/shard_map/ppermute | solution.py:24
  73.2 2.4 %collective-permute-start.21 = (f32[384,1152]{1,0:T(8,128)S(1)}, f32[384,1152]{1,0:T(8,128)S(1)}, u32[]{:S(2)}, u32[]{:S(2)}) collective-permute-start(f32[384,1152]{1,0:T(8,128)S(1)} %twin_sums.1), channel_id=1, source_target_pairs={{8,0},{0,8},{9,1},{1,9},{10,2},{2,10},{11,3},{3,11},{12,4},{4,12},... | collective-permute-start | bytes 5308424 | tf_op jit(solution)/shard_map/ppermute | solution.py:24
  75.7 1.9 %collective-permute-start.18 = (f32[16,1152]{1,0:T(8,128)S(1)}, f32[16,1152]{1,0:T(8,128)S(1)}, u32[]{:S(2)}, u32[]{:S(2)}) collective-permute-start(f32[16,1152]{1,0:T(8,128)S(1)} %sums.4.a), channel_id=1, source_target_pairs={{4,0},{16,4},{20,16},{0,20},{5,1},{17,5},{21,17},{1,21},{6,2},{18,... | collective-permute-start | bytes 221192 | tf_op jit(solution)/shard_map/ppermute | solution.py:24
  78.0 1.5 %collective-permute-start.20 = (f32[16,1152]{1,0:T(8,128)S(1)}, f32[16,1152]{1,0:T(8,128)S(1)}, u32[]{:S(2)}, u32[]{:S(2)}) collective-permute-start(f32[16,1152]{1,0:T(8,128)S(1)} %sums.4.a), channel_id=1, source_target_pairs={{20,0},{0,4},{4,16},{16,20},{21,1},{1,5},{5,17},{17,21},{22,2},{2,... | collective-permute-start | bytes 221192 | tf_op jit(solution)/shard_map/ppermute | solution.py:24
  83.9 2.1 %collective-permute-start.24 = (f32[16,1152]{1,0:T(8,128)S(1)}, f32[16,1152]{1,0:T(8,128)S(1)}, u32[]{:S(2)}, u32[]{:S(2)}) collective-permute-start(f32[16,1152]{1,0:T(8,128)S(1)} %sums.5.a), channel_id=1, source_target_pairs={{32,0},{64,32},{96,64},{0,96},{33,1},{65,33},{97,65},{1,97},{34,2}... | collective-permute-start | bytes 221192 | tf_op jit(solution)/shard_map/ppermute | solution.py:24
  86.0 1.7 %near_sums.1.near = f32[384,1152]{1,0:T(8,128)S(1)} custom-call(bf16[384,768]{1,0:T(8,128)(2,1)S(1)} %get-tuple-element.129.w0, bf16[768,1280]{1,0:T(8,128)(2,1)S(1)} %get-tuple-element.82.both.both0, bf16[384,768]{1,0:T(8,128)(2,1)S(1)} %get-tuple-element.130.w1, bf16[768,1280]{1,0:T(8,128)(2,1)S(1)} %get-tuple-element.110.both.both1, ...), custom_call_target="tpu_custom_call" | custom-call | flops 1 | bytes 10420224 | tf_op jit(solution)/shard_map/near_sums/pallas_call | solution.py:240
  88.5 2.7 %collective-permute-start.26 = (f32[64,1152]{1,0:T(8,128)S(1)}, f32[64,1152]{1,0:T(8,128)S(1)}, u32[]{:S(2)}, u32[]{:S(2)}) collective-permute-start(f32[64,1152]{1,0:T(8,128)S(1)} %places.1.a), channel_id=1, source_target_pairs={{8,0},{0,8},{9,1},{1,9},{10,2},{2,10},{11,3},{3,11},{12,4},{4,12},... | collective-permute-start | bytes 884744 | tf_op jit(solution)/shard_map/ppermute | solution.py:24
  (70 shorter events, 28.7 us)
Async XLA Ops:
  0.6 8.6 %collective-permute-start = (bf16[384,1152]{1,0:T(8,128)(2,1)}, bf16[384,1152]{1,0:T(8,128)(2,1)S(1)}, u32[]{:S(2)}, u32[]{:S(2)}) collective-permute-start(bf16[384,1152]{1,0:T(8,128)(2,1)} %bitcast.9), channel_id=1, source_target_pairs={{8,0},{0,8},{9,1},{1,9},{10,2},{2,10},{11,3},{3,11},{12,4},{4,12},... | collective-permute-start | bytes 2654216 | tf_op jit(solution)/shard_map/ppermute | solution.py:24
  2.1 21.4 %collective-permute-start.1 = (bf16[384,1152]{1,0:T(8,128)(2,1)}, bf16[384,1152]{1,0:T(8,128)(2,1)S(1)}, u32[]{:S(2)}, u32[]{:S(2)}) collective-permute-start(bf16[384,1152]{1,0:T(8,128)(2,1)} %bitcast.10), channel_id=1, source_target_pairs={{16,0},{0,16},{17,1},{1,17},{18,2},{2,18},{19,3},{3,19},{20,4},{4,... | collective-permute-start | bytes 2654216 | tf_op jit(solution)/shard_map/ppermute | solution.py:24
  3.5 23.0 %collective-permute-start.2 = (bf16[384,1152]{1,0:T(8,128)(2,1)}, bf16[384,1152]{1,0:T(8,128)(2,1)S(1)}, u32[]{:S(2)}, u32[]{:S(2)}) collective-permute-start(bf16[384,1152]{1,0:T(8,128)(2,1)} %bitcast.5), channel_id=1, source_target_pairs={{32,0},{104,8},{64,32},{8,40},{96,64},{40,72},{0,96},{72,104},{33,... | collective-permute-start | bytes 2654216 | tf_op jit(solution)/shard_map/ppermute | solution.py:271
  5.2 21.4 %collective-permute-start.3 = (bf16[384,1152]{1,0:T(8,128)(2,1)}, bf16[384,1152]{1,0:T(8,128)(2,1)S(1)}, u32[]{:S(2)}, u32[]{:S(2)}) collective-permute-start(bf16[384,1152]{1,0:T(8,128)(2,1)} %bitcast.6), channel_id=1, source_target_pairs={{96,0},{40,8},{0,32},{72,40},{32,64},{104,72},{64,96},{8,104},{97,... | collective-permute-start | bytes 2654216 | tf_op jit(solution)/shard_map/ppermute | solution.py:271
  26.6 17.3 %collective-permute-start.6 = (bf16[384,1152]{1,0:T(8,128)(2,1)S(1)}, bf16[384,1152]{1,0:T(8,128)(2,1)S(1)}, u32[]{:S(2)}, u32[]{:S(2)}) collective-permute-start(bf16[384,1152]{1,0:T(8,128)(2,1)S(1)} %collective-permute-done.2.a), channel_id=1, source_target_pairs={{32,0},{104,8},{64,32},{8,40},{96,64},{40,72},{0,96},{72,104},{33,... | collective-permute-start | bytes 2654216 | tf_op jit(solution)/shard_map/ppermute | solution.py:271
  28.4 3.6 %collective-permute-start.5 = (bf16[128,384]{1,0:T(8,128)(2,1)S(1)}, bf16[128,384]{1,0:T(8,128)(2,1)S(1)}, u32[]{:S(2)}, u32[]{:S(2)}) collective-permute-start(bf16[128,384]{1,0:T(8,128)(2,1)S(1)} %get-tuple-element.84.ups.ups1), channel_id=1, source_target_pairs={{8,0},{0,8},{9,1},{1,9},{10,2},{2,10},{11,3},{3,11},{12,4},{4,12},... | collective-permute-start | bytes 294920 | tf_op jit(solution)/shard_map/ppermute | solution.py:24
  43.4 11.8 %collective-permute-start.10 = (f32[384,1152]{1,0:T(8,128)S(1)}, f32[384,1152]{1,0:T(8,128)S(1)}, u32[]{:S(2)}, u32[]{:S(2)}) collective-permute-start(f32[384,1152]{1,0:T(8,128)S(1)} %get-tuple-element.112), channel_id=1, source_target_pairs={{8,0},{0,8},{9,1},{1,9},{10,2},{2,10},{11,3},{3,11},{12,4},{4,12},... | collective-permute-start | bytes 5308424 | tf_op jit(solution)/shard_map/ppermute | solution.py:24
  45.6 4.5 %collective-permute-start.8 = (bf16[384,1280]{1,0:T(8,128)(2,1)S(1)}, bf16[384,1280]{1,0:T(8,128)(2,1)S(1)}, u32[]{:S(2)}, u32[]{:S(2)}) collective-permute-start(bf16[384,1280]{1,0:T(8,128)(2,1)S(1)} %embed_far.1.e0), channel_id=1, source_target_pairs={{8,0},{0,8},{9,1},{1,9},{10,2},{2,10},{11,3},{3,11},{12,4},{4,12},... | collective-permute-start | bytes 2949128 | tf_op jit(solution)/shard_map/ppermute | solution.py:24
  45.9 4.3 %collective-permute-start.7 = (bf16[384,1152]{1,0:T(8,128)(2,1)S(1)}, bf16[384,1152]{1,0:T(8,128)(2,1)S(1)}, u32[]{:S(2)}, u32[]{:S(2)}) collective-permute-start(bf16[384,1152]{1,0:T(8,128)(2,1)S(1)} %collective-permute-done.6.images.x0), channel_id=1, source_target_pairs={{8,0},{0,8},{9,1},{1,9},{10,2},{2,10},{11,3},{3,11},{12,4},{4,12},... | collective-permute-start | bytes 2654216 | tf_op jit(solution)/shard_map/ppermute | solution.py:24
  56.8 16.4 %collective-permute-start.17 = (f16[288,1152]{1,0:T(8,128)(2,1)S(1)}, f16[288,1152]{1,0:T(8,128)(2,1)S(1)}, u32[]{:S(2)}, u32[]{:S(2)}) collective-permute-start(f16[288,1152]{1,0:T(8,128)(2,1)S(1)} %convert_element_type.12), channel_id=1, source_target_pairs={{16,0},{0,16},{17,1},{1,17},{18,2},{2,18},{19,3},{3,19},{20,4},{4,... | collective-permute-start | bytes 1990664 | tf_op jit(solution)/shard_map/ppermute | solution.py:24
  58.2 3.6 %collective-permute-start.11 = (f32[16,1152]{1,0:T(8,128)S(1)}, f32[16,1152]{1,0:T(8,128)S(1)}, u32[]{:S(2)}, u32[]{:S(2)}) collective-permute-start(f32[16,1152]{1,0:T(8,128)S(1)} %get-tuple-element.117), channel_id=1, source_target_pairs={{32,0},{64,32},{96,64},{0,96},{33,1},{65,33},{97,65},{1,97},{34,2}... | collective-permute-start | bytes 221192 | tf_op jit(solution)/shard_map/ppermute | solution.py:24
  59.1 4.8 %collective-permute-start.12 = (f32[16,1152]{1,0:T(8,128)S(1)}, f32[16,1152]{1,0:T(8,128)S(1)}, u32[]{:S(2)}, u32[]{:S(2)}) collective-permute-start(f32[16,1152]{1,0:T(8,128)S(1)} %get-tuple-element.118), channel_id=1, source_target_pairs={{64,0},{96,32},{0,64},{32,96},{65,1},{97,33},{1,65},{33,97},{66,2}... | collective-permute-start | bytes 221192 | tf_op jit(solution)/shard_map/ppermute | solution.py:24
  59.3 6.1 %collective-permute-start.13 = (f32[16,1152]{1,0:T(8,128)S(1)}, f32[16,1152]{1,0:T(8,128)S(1)}, u32[]{:S(2)}, u32[]{:S(2)}) collective-permute-start(f32[16,1152]{1,0:T(8,128)S(1)} %get-tuple-element.119), channel_id=1, source_target_pairs={{96,0},{0,32},{32,64},{64,96},{97,1},{1,33},{33,65},{65,97},{98,2}... | collective-permute-start | bytes 221192 | tf_op jit(solution)/shard_map/ppermute | solution.py:24
  65.4 6.5 %collective-permute-start.14 = (f32[16,1152]{1,0:T(8,128)S(1)}, f32[16,1152]{1,0:T(8,128)S(1)}, u32[]{:S(2)}, u32[]{:S(2)}) collective-permute-start(f32[16,1152]{1,0:T(8,128)S(1)} %sums.3.a), channel_id=1, source_target_pairs={{2,0},{3,1},{0,2},{1,3},{6,4},{7,5},{4,6},{5,7},{10,8},{11,9},{8,1... | collective-permute-start | bytes 221192 | tf_op jit(solution)/shard_map/ppermute | solution.py:24
  68.2 5.0 %collective-permute-start.15 = (f32[16,1152]{1,0:T(8,128)S(1)}, f32[16,1152]{1,0:T(8,128)S(1)}, u32[]{:S(2)}, u32[]{:S(2)}) collective-permute-start(f32[16,1152]{1,0:T(8,128)S(1)} %sums.3.a), channel_id=1, source_target_pairs={{3,0},{0,1},{1,2},{2,3},{7,4},{4,5},{5,6},{6,7},{11,8},{8,9},{9,10... | collective-permute-start | bytes 221192 | tf_op jit(solution)/shard_map/ppermute | solution.py:24
  68.5 4.7 %collective-permute-start.16 = (f32[16,1152]{1,0:T(8,128)S(1)}, f32[16,1152]{1,0:T(8,128)S(1)}, u32[]{:S(2)}, u32[]{:S(2)}) collective-permute-start(f32[16,1152]{1,0:T(8,128)S(1)} %sums.3.a), channel_id=1, source_target_pairs={{1,0},{2,1},{3,2},{0,3},{5,4},{6,5},{7,6},{4,7},{9,8},{10,9},{11,1... | collective-permute-start | bytes 221192 | tf_op jit(solution)/shard_map/ppermute | solution.py:24
  73.2 9.2 %collective-permute-start.21 = (f32[384,1152]{1,0:T(8,128)S(1)}, f32[384,1152]{1,0:T(8,128)S(1)}, u32[]{:S(2)}, u32[]{:S(2)}) collective-permute-start(f32[384,1152]{1,0:T(8,128)S(1)} %twin_sums.1), channel_id=1, source_target_pairs={{8,0},{0,8},{9,1},{1,9},{10,2},{2,10},{11,3},{3,11},{12,4},{4,12},... | collective-permute-start | bytes 5308424 | tf_op jit(solution)/shard_map/ppermute | solution.py:24
  75.7 5.3 %collective-permute-start.18 = (f32[16,1152]{1,0:T(8,128)S(1)}, f32[16,1152]{1,0:T(8,128)S(1)}, u32[]{:S(2)}, u32[]{:S(2)}) collective-permute-start(f32[16,1152]{1,0:T(8,128)S(1)} %sums.4.a), channel_id=1, source_target_pairs={{4,0},{16,4},{20,16},{0,20},{5,1},{17,5},{21,17},{1,21},{6,2},{18,... | collective-permute-start | bytes 221192 | tf_op jit(solution)/shard_map/ppermute | solution.py:24
  78.0 4.4 %collective-permute-start.20 = (f32[16,1152]{1,0:T(8,128)S(1)}, f32[16,1152]{1,0:T(8,128)S(1)}, u32[]{:S(2)}, u32[]{:S(2)}) collective-permute-start(f32[16,1152]{1,0:T(8,128)S(1)} %sums.4.a), channel_id=1, source_target_pairs={{20,0},{0,4},{4,16},{16,20},{21,1},{1,5},{5,17},{17,21},{22,2},{2,... | collective-permute-start | bytes 221192 | tf_op jit(solution)/shard_map/ppermute | solution.py:24
  82.5 6.0 %collective-permute-start.25 = (f16[112,1152]{1,0:T(8,128)(2,1)S(1)}, f16[112,1152]{1,0:T(8,128)(2,1)S(1)}, u32[]{:S(2)}, u32[]{:S(2)}) collective-permute-start(f16[112,1152]{1,0:T(8,128)(2,1)S(1)} %convert_element_type.13), channel_id=1, source_target_pairs={{16,0},{0,16},{17,1},{1,17},{18,2},{2,18},{19,3},{3,19},{20,4},{4,... | collective-permute-start | bytes 774152 | tf_op jit(solution)/shard_map/ppermute | solution.py:24
  82.6 5.2 %collective-permute-start.22 = (f32[16,1152]{1,0:T(8,128)S(1)}, f32[16,1152]{1,0:T(8,128)S(1)}, u32[]{:S(2)}, u32[]{:S(2)}) collective-permute-start(f32[16,1152]{1,0:T(8,128)S(1)} %sums.5.a), channel_id=1, source_target_pairs={{64,0},{96,32},{0,64},{32,96},{65,1},{97,33},{1,65},{33,97},{66,2}... | collective-permute-start | bytes 221192 | tf_op jit(solution)/shard_map/ppermute | solution.py:24
  83.3 4.8 %collective-permute-start.23 = (f32[16,1152]{1,0:T(8,128)S(1)}, f32[16,1152]{1,0:T(8,128)S(1)}, u32[]{:S(2)}, u32[]{:S(2)}) collective-permute-start(f32[16,1152]{1,0:T(8,128)S(1)} %sums.5.a), channel_id=1, source_target_pairs={{96,0},{0,32},{32,64},{64,96},{97,1},{1,33},{33,65},{65,97},{98,2}... | collective-permute-start | bytes 221192 | tf_op jit(solution)/shard_map/ppermute | solution.py:24
  83.9 4.2 %collective-permute-start.24 = (f32[16,1152]{1,0:T(8,128)S(1)}, f32[16,1152]{1,0:T(8,128)S(1)}, u32[]{:S(2)}, u32[]{:S(2)}) collective-permute-start(f32[16,1152]{1,0:T(8,128)S(1)} %sums.5.a), channel_id=1, source_target_pairs={{32,0},{64,32},{96,64},{0,96},{33,1},{65,33},{97,65},{1,97},{34,2}... | collective-permute-start | bytes 221192 | tf_op jit(solution)/shard_map/ppermute | solution.py:24
  88.5 4.3 %collective-permute-start.26 = (f32[64,1152]{1,0:T(8,128)S(1)}, f32[64,1152]{1,0:T(8,128)S(1)}, u32[]{:S(2)}, u32[]{:S(2)}) collective-permute-start(f32[64,1152]{1,0:T(8,128)S(1)} %places.1.a), channel_id=1, source_target_pairs={{8,0},{0,8},{9,1},{1,9},{10,2},{2,10},{11,3},{3,11},{12,4},{4,12},... | collective-permute-start | bytes 884744 | tf_op jit(solution)/shard_map/ppermute | solution.py:24
  (11 other events, 27.8 us)
